TPU v7x, 128 devices: a whole 4x4x4 slice. The times are simulated.
128 devices in a mesh: decode: 16 (over x, y), pool: 8 (over z, core).
Axes of the slice: x: 4, y: 4, z: 4, core: 2. Of those that a mesh axis runs over, the one named last changes fastest.
Arguments:
- q_nope: bfloat16 [8192, 8192], P('decode', 'pool'), may hold values from -6 to 6
- q_rope: bfloat16 [8192, 4096], P('decode', 'pool'), may hold values from -8 to 8
- up_keys: bfloat16 [64, 128, 512], P('pool'), may hold values from -0.5 to 0.5
- up_values: bfloat16 [64, 512, 128], P('pool'), may hold values from -1 to 1
- page_pool: bfloat16 [4096, 64, 576], P(('decode', 'pool')), may hold values from -6 to 6
- page_table: int32 [128, 16], P('decode'), may hold values from 0 to 4095, as said below
- lengths: int32 [128], P('decode'), may hold values from 1 to 1024, 81920 in all
- prefix_latent: bfloat16 [384, 576], P('decode'), may hold values from -8 to 8
- tree_latent: bfloat16 [8192, 576], P('decode'), may hold values from -6 to 6
- parents: int32 [128, 64], P('decode'), may hold values from 0 to 62, as said below
Outputs:
- attended: bfloat16 [8192, 8192], P('decode', 'pool')
Inputs may be any that keep to these rules, and one draw needn't show every extreme that they name: `page_table`: entry (q, j) is the global number of page j of request q, which holds context positions j * 64 to (j + 1) * 64 - 1. Page n lies on device n // 32 of decode+pool (decode index slowest) as its local page n % 32. No two entries name the same page. The pages of one decode group's 8 requests lie at most 2 on any one device, and exactly 2 on some. parents[q, 0] = 0 for the root; every other node names an earlier node.
All inputs are finite; a program needn't handle non-finite values. No bound on the sum of `lengths` on one device may be relied on, other than what follows from the above.
Results may differ from a plain program's by a relative error of at most 0.0075.
Values may be sent and summed in bfloat16 or wider, within the bound.
No kernel may reach another device: no remote copies, remote signals or barrier semaphores. Data moves between devices by JAX's collectives and lax.ppermute only.
A program may use at most 128 MiB of HBM per device.

v0:
```python
import jax
import jax.numpy as jnp
from jax import lax
from jax.sharding import PartitionSpec as P


def ancestry(parent_row):
    size = parent_row.shape[0]
    nodes = jnp.arange(size, dtype=jnp.int32)
    links = (parent_row[:, None] == nodes[None, :]).astype(jnp.int32)
    reach = jnp.maximum(links, (nodes[:, None] == nodes[None, :]).astype(jnp.int32))
    for sweep in range(max(1, (size - 1).bit_length())):
        reach = jnp.minimum(jnp.dot(reach, reach), 1)
    return reach > 0


def against(queries, keys):
    return lax.dot_general(
        queries, keys, (((1,), (1,)), ((), ())), preferred_element_type=jnp.float32
    )


def local(
    q_nope,
    q_rope,
    up_keys,
    up_values,
    page_pool,
    page_table,
    lengths,
    prefix_latent,
    tree_latent,
    parents,
):
    heads = up_keys.shape[0]
    nope_dim = up_keys.shape[1]
    latent_dim = up_keys.shape[2]
    rope_dim = q_rope.shape[1] // heads
    value_dim = up_values.shape[2]
    requests = parents.shape[0]
    tree_size = parents.shape[1]
    pages_per = page_table.shape[1]
    page_size = page_pool.shape[1]
    pool_local = page_pool.shape[0]
    scale = (nope_dim + rope_dim) ** (-0.5)
    decode_count = lax.axis_size("decode")
    pool_count = lax.axis_size("pool")
    owners = decode_count * pool_count
    flat_pages = page_table.reshape(-1)
    owner_of = flat_pages // pool_local
    local_of = flat_pages % pool_local
    entries = flat_pages.shape[0]
    capacity = 2 * entries // owners
    order = jnp.arange(entries, dtype=jnp.int32)
    earlier = (order[None, :] < order[:, None]) & (owner_of[None, :] == owner_of[:, None])
    rank_of = jnp.sum(earlier.astype(jnp.int32), axis=1)
    asks = jnp.zeros((owners, capacity), jnp.int32).at[owner_of, rank_of].set(local_of)
    received = lax.all_to_all(asks, ("decode", "pool"), split_axis=0, concat_axis=0, tiled=True)
    taken = jnp.take(page_pool, received.reshape(-1), axis=0)
    pages = lax.all_to_all(
        taken.reshape(received.shape + page_pool.shape[1:]),
        ("decode", "pool"),
        split_axis=0,
        concat_axis=0,
        tiled=True,
    )
    slot_of = owner_of * capacity + rank_of
    fetched = pages.reshape(owners * capacity, page_size, -1)
    prefix_all = lax.all_gather(prefix_latent, "decode", axis=0, tiled=True)
    query_nope = q_nope.reshape(-1, heads, nope_dim)
    absorbed = jnp.einsum(
        "rhn,hnl->rhl", query_nope, up_keys, preferred_element_type=jnp.float32
    ).astype(jnp.bfloat16)
    combined = jnp.concatenate([absorbed, q_rope.reshape(-1, heads, rope_dim)], axis=2)
    slots = slot_of.reshape(requests, pages_per)
    position = jnp.arange(pages_per * page_size, dtype=jnp.int32)

    def one_request(index):
        start = index * tree_size
        queries = lax.dynamic_slice_in_dim(combined, start, tree_size, 0).reshape(
            tree_size * heads, -1
        )
        context = jnp.take(fetched, slots[index], axis=0).reshape(pages_per * page_size, -1)
        tree_keys = lax.dynamic_slice_in_dim(tree_latent, start, tree_size, 0)
        prefix_scores = against(queries, prefix_all) * scale
        context_scores = against(queries, context) * scale
        tree_scores = against(queries, tree_keys) * scale
        context_seen = (position < lengths[index])[None, :]
        tree_seen = jnp.repeat(ancestry(parents[index]), heads, axis=0)
        lowest = jnp.float32(-jnp.inf)
        top = jnp.maximum(
            jnp.max(prefix_scores, axis=1),
            jnp.max(jnp.where(context_seen, context_scores, lowest), axis=1),
        )
        top = jnp.maximum(top, jnp.max(jnp.where(tree_seen, tree_scores, lowest), axis=1))[:, None]
        weights_prefix = jnp.exp(prefix_scores - top).astype(jnp.bfloat16)
        weights_context = jnp.where(context_seen, jnp.exp(context_scores - top), 0.0).astype(
            jnp.bfloat16
        )
        weights_tree = jnp.where(tree_seen, jnp.exp(tree_scores - top), 0.0).astype(jnp.bfloat16)
        total = jnp.sum(weights_prefix.astype(jnp.float32), axis=1)
        total = total + jnp.sum(weights_context.astype(jnp.float32), axis=1)
        total = total + jnp.sum(weights_tree.astype(jnp.float32), axis=1)
        mixed = jnp.dot(
            weights_prefix, prefix_all[:, :latent_dim], preferred_element_type=jnp.float32
        )
        mixed = mixed + jnp.dot(
            weights_context, context[:, :latent_dim], preferred_element_type=jnp.float32
        )
        mixed = mixed + jnp.dot(
            weights_tree, tree_keys[:, :latent_dim], preferred_element_type=jnp.float32
        )
        latent_out = (
            (mixed / total[:, None]).astype(jnp.bfloat16).reshape(tree_size, heads, latent_dim)
        )
        result = jnp.einsum(
            "thl,hlv->thv", latent_out, up_values, preferred_element_type=jnp.float32
        )
        return result.astype(jnp.bfloat16).reshape(tree_size, heads * value_dim)

    outputs = lax.map(one_request, jnp.arange(requests, dtype=jnp.int32))
    return outputs.reshape(-1, heads * value_dim)


def solution(mesh):
    in_specs = (
        P("decode", "pool"),
        P("decode", "pool"),
        P("pool", None, None),
        P("pool", None, None),
        P(("decode", "pool"), None, None),
        P("decode", None),
        P("decode"),
        P("decode", None),
        P("decode", None),
        P("decode", None),
    )
    out_specs = P("decode", "pool")
    return jax.shard_map(local, mesh=mesh, in_specs=in_specs, out_specs=out_specs, check_vma=False)
```

profile of v0, /device:TPU:1, one launch (start us, length us, event | category | flops | bytes accessed | tf_op | source)
XLA Modules:
  0.0 621.9 jit_solution(12041349895895737963)
XLA Ops:
  1.9 6.4 %scatter_fusion = s32[128,2]{0,1:T(2,128)S(1)} fusion(s32[128,2]{0,1:T(2,128)S(1)} %broadcast_in_dim.84, s32[128]{0:T(128)S(1)} %fusion.50, s32[128]{0:T(128)S(1)} %get-tuple-element.164), kind=kCustom, calls=%fused_computation.2 | custom fusion | bytes 2560 | tf_op jit(solution)/shard_map/scatter | solution.py:57
  8.4 20.7 %all_to_all.14 = s32[128,1,2]{2,1,0:T(1,128)S(1)} all-to-all(s32[128,1,2]{2,1,0:T(1,128)S(1)} %copy.46), channel_id=1, replica_groups=mesh['decode'=16,'pool'=8] {'decode','pool'}, dimensions={0} | all-to-all | bytes 2048 | tf_op jit(solution)/shard_map/all_to_all | solution.py:58
  30.8 11.4 %gather_fusion.1 = bf16[256,64,576]{2,1,0:T(8,128)(2,1)} fusion(bf16[32,64,576]{2,1,0:T(8,128)(2,1)S(1)} %copy-done, s32[1024]{0:T(1024)S(1)} %pad_clamp_fusion.1), kind=kCustom, calls=%fused_computation.1 | custom fusion | bytes 37749760 | tf_op jit(solution)/shard_map/jit(_take)/gather | solution.py:59
  42.2 17.8 %broadcast_select_fusion.1 = bf16[128,2,64,576]{3,2,1,0:T(8,128)(2,1)} fusion(bf16[128,2,64,576]{3,2,1,0:T(8,128)(2,1)} %bitcast.106, pred[128,2]{1,0:T(8,128)(4,1)S(1)} %copy.48), kind=kLoop, calls=%fused_computation.74 | loop fusion | flops 9437184 | bytes 37748992 | tf_op jit(solution)/shard_map/jit(_take)/select_n | solution.py:59
  60.0 5.8 all-to-all-start.1
  70.0 9.2 %copy.49 = bf16[512,8,576]{2,1,0:T(8,128)(2,1)} copy(bf16[512,8,576]{0,2,1:T(8,128)(2,1)} %pad_maximum_fusion) | data formatting | bytes 9437184
  79.2 307.1 %all_gather.3 = bf16[384,576]{1,0:T(8,128)(2,1)S(1)} all-gather(bf16[24,576]{1,0:T(8,128)(2,1)S(1)} %copy-done.8), channel_id=1, replica_groups=mesh['decode'=16,'pool'=8] {'decode'}, dimensions={0}, use_global_device_ids=true | all-gather | bytes 470016 | tf_op jit(solution)/shard_map/all_gather | solution.py:69
  386.4 233.7 %while.11 = (s32[]{:T(128)}, bf16[8,64,1024]{2,1,0:T(8,128)(2,1)}, s32[8]{0:T(128)S(1)}, bf16[512,8,576]{2,1,0:T(8,128)(2,1)}, bf16[384,576]{1,0:T(8,128)(2,1)S(...) while((s32[]{:T(128)}, bf16[8,64,1024]{2,1,0:T(8,128)(2,1)}, ...), condition=%wide.region_9.10_spmd.clone, body=%wide.region_2.9_spmd.clone.sunk | while | flops 1721255040 | bytes 39191488 | solution.py:121
  389.0 7.7 %gather_fusion = bf16[16,64,576]{2,1,0:T(8,128)(2,1)S(1)} fusion(bf16[256,64,576]{2,1,0:T(8,128)(2,1)} %get-tuple-element.284, s32[1024]{0:T(1024)S(1)} %pad_clamp_fusion.3), kind=kCustom, calls=%fused_computation.clone.clone.1 | custom fusion | bytes 2359360 | tf_op jit(solution)/shard_map/while/body/eval_jaxpr/jit(_take)/gather | solution.py:83
  398.9 3.4 select_reduce_fusion.5
  418.2 7.7 %gather_fusion = bf16[16,64,576]{2,1,0:T(8,128)(2,1)S(1)} fusion(bf16[256,64,576]{2,1,0:T(8,128)(2,1)} %get-tuple-element.284, s32[1024]{0:T(1024)S(1)} %pad_clamp_fusion.3), kind=kCustom, calls=%fused_computation.clone.clone.1 | custom fusion | bytes 2359360 | tf_op jit(solution)/shard_map/while/body/eval_jaxpr/jit(_take)/gather | solution.py:83
  428.1 3.4 select_reduce_fusion.5
  447.4 7.7 %gather_fusion = bf16[16,64,576]{2,1,0:T(8,128)(2,1)S(1)} fusion(bf16[256,64,576]{2,1,0:T(8,128)(2,1)} %get-tuple-element.284, s32[1024]{0:T(1024)S(1)} %pad_clamp_fusion.3), kind=kCustom, calls=%fused_computation.clone.clone.1 | custom fusion | bytes 2359360 | tf_op jit(solution)/shard_map/while/body/eval_jaxpr/jit(_take)/gather | solution.py:83
  457.3 3.4 select_reduce_fusion.5
  476.6 7.7 %gather_fusion = bf16[16,64,576]{2,1,0:T(8,128)(2,1)S(1)} fusion(bf16[256,64,576]{2,1,0:T(8,128)(2,1)} %get-tuple-element.284, s32[1024]{0:T(1024)S(1)} %pad_clamp_fusion.3), kind=kCustom, calls=%fused_computation.clone.clone.1 | custom fusion | bytes 2359360 | tf_op jit(solution)/shard_map/while/body/eval_jaxpr/jit(_take)/gather | solution.py:83
  486.5 3.4 select_reduce_fusion.5
  505.8 7.7 %gather_fusion = bf16[16,64,576]{2,1,0:T(8,128)(2,1)S(1)} fusion(bf16[256,64,576]{2,1,0:T(8,128)(2,1)} %get-tuple-element.284, s32[1024]{0:T(1024)S(1)} %pad_clamp_fusion.3), kind=kCustom, calls=%fused_computation.clone.clone.1 | custom fusion | bytes 2359360 | tf_op jit(solution)/shard_map/while/body/eval_jaxpr/jit(_take)/gather | solution.py:83
  515.7 3.4 select_reduce_fusion.5
  535.1 7.7 %gather_fusion = bf16[16,64,576]{2,1,0:T(8,128)(2,1)S(1)} fusion(bf16[256,64,576]{2,1,0:T(8,128)(2,1)} %get-tuple-element.284, s32[1024]{0:T(1024)S(1)} %pad_clamp_fusion.3), kind=kCustom, calls=%fused_computation.clone.clone.1 | custom fusion | bytes 2359360 | tf_op jit(solution)/shard_map/while/body/eval_jaxpr/jit(_take)/gather | solution.py:83
  545.0 3.4 select_reduce_fusion.5
  564.3 7.7 %gather_fusion = bf16[16,64,576]{2,1,0:T(8,128)(2,1)S(1)} fusion(bf16[256,64,576]{2,1,0:T(8,128)(2,1)} %get-tuple-element.284, s32[1024]{0:T(1024)S(1)} %pad_clamp_fusion.3), kind=kCustom, calls=%fused_computation.clone.clone.1 | custom fusion | bytes 2359360 | tf_op jit(solution)/shard_map/while/body/eval_jaxpr/jit(_take)/gather | solution.py:83
  574.2 3.4 select_reduce_fusion.5
  593.5 7.7 %gather_fusion = bf16[16,64,576]{2,1,0:T(8,128)(2,1)S(1)} fusion(bf16[256,64,576]{2,1,0:T(8,128)(2,1)} %get-tuple-element.284, s32[1024]{0:T(1024)S(1)} %pad_clamp_fusion.3), kind=kCustom, calls=%fused_computation.clone.clone.1 | custom fusion | bytes 2359360 | tf_op jit(solution)/shard_map/while/body/eval_jaxpr/jit(_take)/gather | solution.py:83
  603.4 3.4 select_reduce_fusion.5
  (303 shorter events, 132.5 us)
Async XLA Ops:
  0.0 30.8 %copy-start = (bf16[32,64,576]{2,1,0:T(8,128)(2,1)S(1)}, bf16[32,64,576]{2,1,0:T(8,128)(2,1)}, u32[]{:S(2)}) copy-start(bf16[32,64,576]{2,1,0:T(8,128)(2,1)} %param.16) | copy-start | bytes 7077892
  60.0 5.9 copy-start.6
  60.0 6.1 copy-start.4
  60.0 6.1 copy-start.5
  60.0 326.4 %all-to-all-start.1 = ((bf16[128,2,64,576]{3,2,1,0:T(8,128)(2,1)}), bf16[128,2,64,576]{3,2,1,0:T(8,128)(2,1)}, u32[]{:S(2)}, u32[]{:S(2)}) async-start(bf16[128,2,64,576]{3,2,1,0:T(8,128)(2,1)} %broadcast_select_fusion.1), calls=%async_computation.1 | async-start | bytes 41943040 | tf_op jit(solution)/shard_map/all_to_all | solution.py:60
  70.0 9.2 %copy-start.8 = (bf16[24,576]{1,0:T(8,128)(2,1)S(1)}, bf16[24,576]{1,0:T(8,128)(2,1)}, u32[]{:S(2)}) copy-start(bf16[24,576]{1,0:T(8,128)(2,1)} %param.19) | copy-start | bytes 82948
  70.0 316.4 %copy-start.7 = (s32[8,16]{1,0:T(8,128)S(1)}, s32[8,16]{1,0:T(8,128)}, u32[]{:S(2)}) copy-start(s32[8,16]{1,0:T(8,128)} %param.17) | copy-start | bytes 1540
  70.0 316.4 %copy-start.9 = (s32[8]{0:T(128)S(1)}, s32[8]{0:T(128)}, u32[]{:S(2)}) copy-start(s32[8]{0:T(128)} %param.18) | copy-start | bytes 100
  404.4 3.4 copy-start.2
  413.0 1.4 copy-start.3
  433.6 3.4 copy-start.2
  442.2 1.4 copy-start.3
  462.9 3.4 copy-start.2
  471.5 1.4 copy-start.3
  492.1 3.4 copy-start.2
  500.7 1.4 copy-start.3
  521.3 3.4 copy-start.2
  529.9 1.4 copy-start.3
  550.5 3.4 copy-start.2
  559.1 1.4 copy-start.3
  579.7 3.4 copy-start.2
  608.9 3.4 copy-start.2
  617.5 1.4 copy-start.3
  620.1 1.7 copy-start.1
  (1 other events, 1.4 us)
where the time goes:
time: 630 us; the launch traced here: 622 us
  blocking collectives  328 us (52%)
  local copies, waits for them, and re-layouts  119 us (19%)
  matrix products  113 us (18%)
  other arithmetic  34.9 us (6%)
  loops' own time  21.3 us (3%)
    all_gather x1, blocking collectives, local(): prefix_all = lax.all_gather(prefix_latent, 'decode', axis=0, tiled=True)  307 us
    gather x8, local copies, waits for them, and re-layouts, one_request(): jnp.take(fetched, slots[index], axis=0).reshape(pages_per * page_size, -1)  62 us
    dot_general x24, matrix products, against(): lax.dot_general(queries, keys, (((1,), (1,)), ((), ())), preferred_elemen...  53.4 us
    another operation x1, loops' own time, local(): outputs = lax.map(one_request, jnp.arange(requests, dtype=jnp.int32))  21.3 us
    dot_general x8, matrix products, one_request(): jnp.dot(weights_context, context[:, :latent_dim], preferred_element_type=...  21.3 us
    all_to_all x1, blocking collectives, local(): lax.all_to_all(asks, ('decode', 'pool'), split_axis=0, concat_axis=0, til...  20.7 us
    select_n x2, other arithmetic, local(): taken = jnp.take(page_pool, received.reshape(-1), axis=0)  17.8 us
  transfers between devices with their start and end apart: 1, of which 0 were waited for; matrix products, arithmetic and copies ran while one was open for 2% of the time, Pallas kernels for 0%

commit v1 on v0

v1 whole, which is shorter than its diff:
```python
import functools
import math

import jax
import jax.numpy as jnp
from jax import lax
from jax.experimental import pallas as pl
from jax.experimental.pallas import tpu as pltpu
from jax.sharding import PartitionSpec as P

F32 = jnp.float32
BF16 = jnp.bfloat16
VMEM_LIMIT = 48 * 1024 * 1024


def nt_dot(a, b):
    return lax.dot_general(a, b, (((1,), (1,)), ((), ())), preferred_element_type=F32)


def prepare_kernel(rows_ref, rope_ref, keys_ref, parents_ref, q_ref, seen_ref):
    head = pl.program_id(0)
    latent = keys_ref.shape[2]
    absorbed = jnp.dot(rows_ref[...], keys_ref[0], preferred_element_type=F32)
    q_ref[0, :, :latent] = absorbed.astype(BF16)
    pair = rope_ref[...].astype(F32)
    lane = lax.broadcasted_iota(jnp.int32, pair.shape, 1)
    half = pair.shape[1] // 2
    turned = pltpu.roll(pair, half, 1)
    even = lax.rem(head, 2) == 0
    source = jnp.where(even, pair, turned)
    other = jnp.where(even, turned, pair)
    q_ref[0, :, latent : latent + 2 * half] = jnp.where(lane < half, source, 0.0).astype(BF16)
    q_ref[0, :, latent + 2 * half :] = jnp.where(lane >= half, other, 0.0).astype(BF16)
    size = parents_ref.shape[1]
    columns = lax.broadcasted_iota(jnp.int32, (size, size), 1)
    rows = lax.broadcasted_iota(jnp.int32, (size, size), 0)
    links = (parents_ref[0] == columns) | (rows == columns)
    reach = links.astype(F32)
    for sweep in range(max(1, (size - 1).bit_length())):
        reach = jnp.minimum(
            jnp.dot(reach.astype(BF16), reach.astype(BF16), preferred_element_type=F32), 1.0
        )
    lowest = jnp.full((size, size), -jnp.inf, F32)
    seen_ref[0] = jnp.concatenate([jnp.where(reach > 0.5, 0.0, lowest), lowest], axis=1)


def prepare(q_nope, q_rope, up_keys, parents):
    heads, nope, latent = up_keys.shape
    rows = q_nope.shape[0]
    requests, size = parents.shape
    rope = q_rope.shape[1] // heads
    return pl.pallas_call(
        prepare_kernel,
        grid=(heads,),
        in_specs=[
            pl.BlockSpec((rows, nope), lambda h: (0, h)),
            pl.BlockSpec((rows, 2 * rope), lambda h: (0, h // 2)),
            pl.BlockSpec((1, nope, latent), lambda h: (h, 0, 0)),
            pl.BlockSpec((1, size, 1), lambda h: (h, 0, 0)),
        ],
        out_specs=[
            pl.BlockSpec((1, rows, latent + 4 * rope), lambda h: (h, 0, 0)),
            pl.BlockSpec((1, size, 2 * size), lambda h: (h, 0, 0)),
        ],
        out_shape=[
            jax.ShapeDtypeStruct((heads, rows, latent + 4 * rope), BF16),
            jax.ShapeDtypeStruct((requests, size, 2 * size), F32),
        ],
        cost_estimate=pl.CostEstimate(
            flops=2 * rows * heads * nope * latent, bytes_accessed=10_000_000, transcendentals=0
        ),
        compiler_params=pltpu.CompilerParams(vmem_limit_bytes=VMEM_LIMIT),
        name="prepare",
    )(q_nope, q_rope, up_keys, parents[:, :, None])


def pack_kernel(wanted_ref, pool_ref, out_ref):
    groups = wanted_ref.shape[0]
    shares = out_ref.shape[0] // groups
    latent = 512
    rope = pool_ref.shape[2] - latent

    def body(group, carry):
        first = pool_ref.at[pl.ds(wanted_ref[group, 0] * shares, shares)]
        second = pool_ref.at[pl.ds(wanted_ref[group, 1] * shares, shares)]
        out = out_ref.at[pl.ds(group * shares, shares)]
        out[:, :, :latent] = first[:, :, :latent]
        out[:, :, latent : 2 * latent] = second[:, :, :latent]
        out[:, :, 2 * latent :] = jnp.concatenate(
            [first[:, :, latent:], second[:, :, latent:]], axis=2
        )
        return carry

    lax.fori_loop(0, groups, body, 0)


def pack(wanted, pool, shares):
    groups = wanted.shape[0]
    eighth = pool.shape[1] // shares
    width = pool.shape[2]
    return pl.pallas_call(
        pack_kernel,
        in_specs=[
            pl.BlockSpec(memory_space=pltpu.SMEM),
            pl.BlockSpec(memory_space=pltpu.VMEM),
        ],
        out_specs=pl.BlockSpec(memory_space=pltpu.VMEM),
        out_shape=jax.ShapeDtypeStruct((groups * shares, eighth, 2 * width), BF16),
        cost_estimate=pl.CostEstimate(flops=0, bytes_accessed=5_000_000, transcendentals=0),
        compiler_params=pltpu.CompilerParams(vmem_limit_bytes=VMEM_LIMIT),
        name="pack",
    )(wanted, pool.reshape(pool.shape[0] * shares, eighth, width))


def compact_kernel(source_ref, slot_ref, got_ref, after_ref, out_ref):
    pairs = out_ref.shape[0]
    per = 8
    latent = 512
    half = (out_ref.shape[2] - 2 * latent) // 2

    def body(k, carry):
        request = k // per
        first = request * (2 * per) + lax.rem(k, per)
        ropes = []
        for side, entry in enumerate((first, first + per)):
            source = source_ref[entry]
            slot = slot_ref[entry]
            start = pl.multiple_of(slot * latent, latent)
            out_ref[k, :, side * latent : (side + 1) * latent] = got_ref[
                source, :, pl.ds(start, latent)
            ]
            both = got_ref[source, :, 2 * latent :].astype(F32)
            ropes.append(jnp.where(slot == side, both, pltpu.roll(both, half, 1)))
        lane = lax.broadcasted_iota(jnp.int32, ropes[0].shape, 1)
        out_ref[k, :, 2 * latent :] = jnp.where(lane < half, ropes[0], ropes[1]).astype(BF16)
        return carry

    lax.fori_loop(0, pairs, body, 0, unroll=4)


def compact(source, slot, got, after):
    entries = source.shape[0]
    return pl.pallas_call(
        compact_kernel,
        in_specs=[
            pl.BlockSpec(memory_space=pltpu.SMEM),
            pl.BlockSpec(memory_space=pltpu.SMEM),
            pl.BlockSpec(memory_space=pltpu.VMEM),
            pl.BlockSpec(memory_space=pl.ANY),
        ],
        out_specs=pl.BlockSpec(memory_space=pltpu.VMEM),
        out_shape=jax.ShapeDtypeStruct((entries // 2,) + got.shape[1:], BF16),
        cost_estimate=pl.CostEstimate(flops=0, bytes_accessed=4_000_000, transcendentals=0),
        compiler_params=pltpu.CompilerParams(vmem_limit_bytes=VMEM_LIMIT),
        name="compact",
    )(source, slot, got, after)


def base_kernel(scale, q_ref, prefix_ref, tree_ref, seen_ref, stats_ref, sum_ref, lat_ref, rope_ref):
    heads, size, wide = q_ref.shape
    latent = prefix_ref.shape[1] - 128
    twice = (wide - latent) // 2
    shared = prefix_ref.shape[0]
    count = lat_ref.shape[0]
    factor = scale * math.log2(math.e)
    some = 4
    block = some * size

    @pl.when(pl.program_id(0) == 0)
    def _():
        lat_ref[:shared, :] = prefix_ref[:, :latent]
        rope_ref[:shared, :] = prefix_ref[:, latent:]
        lat_ref[shared + size :, :] = jnp.zeros((count - shared - size, latent), BF16)
        rope_ref[shared + size :, :] = jnp.zeros((count - shared - size, twice), BF16)

    lat_ref[shared : shared + size, :] = tree_ref[:, :latent]
    rope_ref[shared : shared + size, :] = tree_ref[:, latent:]
    hidden = jnp.concatenate([seen_ref[0]] * some, axis=0)
    lane = lax.broadcasted_iota(jnp.int32, (block, 128), 1)
    for step in range(heads // some):
        which = slice(step * some, (step + 1) * some)
        rows = slice(step * block, (step + 1) * block)
        q = q_ref[which, :, :latent].reshape(block, latent)
        q_rope = q_ref[which, :, latent : latent + twice].reshape(block, twice)
        scores = nt_dot(q, lat_ref[...]) + nt_dot(q_rope, rope_ref[...])
        scores = jnp.concatenate([scores[:, :shared], scores[:, shared:] + hidden], axis=1)
        top = jnp.max(scores, axis=1, keepdims=True)
        weights = jnp.exp2((scores - top) * factor)
        total = jnp.sum(weights, axis=1, keepdims=True)
        sum_ref[0, rows, :] = jnp.dot(
            weights.astype(BF16), lat_ref[...], preferred_element_type=F32
        )
        stats_ref[0, rows, :] = jnp.where(lane < 64, top, total)


def base(scale, q, prefix, tree, seen):
    heads, total_rows, wide = q.shape
    requests, size = seen.shape[:2]
    latent = prefix.shape[1] - 128
    rows = heads * size
    count = prefix.shape[0] + 2 * size
    return pl.pallas_call(
        functools.partial(base_kernel, scale),
        grid=(requests,),
        in_specs=[
            pl.BlockSpec((heads, size, wide), lambda i: (0, i, 0)),
            pl.BlockSpec(prefix.shape, lambda i: (0, 0)),
            pl.BlockSpec((size, tree.shape[1]), lambda i: (i, 0)),
            pl.BlockSpec((1, size, 2 * size), lambda i: (i, 0, 0)),
        ],
        out_specs=[
            pl.BlockSpec((1, rows, 128), lambda i: (i, 0, 0)),
            pl.BlockSpec((1, rows, latent), lambda i: (i, 0, 0)),
        ],
        out_shape=[
            jax.ShapeDtypeStruct((requests, rows, 128), F32),
            jax.ShapeDtypeStruct((requests, rows, latent), F32),
        ],
        scratch_shapes=[pltpu.VMEM((count, latent), BF16), pltpu.VMEM((count, 128), BF16)],
        cost_estimate=pl.CostEstimate(
            flops=2 * requests * rows * count * (2 * latent + 64),
            bytes_accessed=requests * rows * (latent * 6 + 1024),
            transcendentals=requests * rows * count,
        ),
        compiler_params=pltpu.CompilerParams(vmem_limit_bytes=VMEM_LIMIT),
        name="base",
    )(q, prefix, tree, seen)


def context_kernel(
    scale, lengths_ref, q_ref, pages_ref, stats_ref, sum_ref, values_ref, out_ref, mixed_ref
):
    heads, size, wide = q_ref.shape
    latent = values_ref.shape[1]
    twice = (wide - latent) // 2
    shares, per, _ = pages_ref.shape
    request = pl.program_id(0)
    length = lengths_ref[request]
    factor = scale * math.log2(math.e)
    lowest = F32(-jnp.inf)
    some = 4
    block = some * size
    part = per // 2
    section = shares * part

    column = lax.broadcasted_iota(jnp.int32, (1, section), 1)
    position = (column % part) // 8 * 64 + column // part * 8 + column % 8

    def keys(index, start, stop):
        half = index % 2
        return pages_ref[:, half * part : (half + 1) * part, start:stop].reshape(
            section, stop - start
        )

    def work(sections):
        for step in range(heads // some):
            which = slice(step * some, (step + 1) * some)
            rows = slice(step * block, (step + 1) * block)
            q = q_ref[which, :, :latent].reshape(block, latent)
            scores = []
            for index in range(sections):
                side = index // 2
                q_rope = q_ref[
                    which, :, latent + side * twice : latent + (side + 1) * twice
                ].reshape(block, twice)
                score = nt_dot(q, keys(index, side * latent, (side + 1) * latent))
                score = score + nt_dot(q_rope, keys(index, 2 * latent, 2 * latent + twice))
                if index == sections - 1:
                    score = jnp.where(position + index * section < length, score, lowest)
                scores.append(score)
            before = stats_ref[0, rows, :1]
            peak = functools.reduce(jnp.maximum, scores)
            top = jnp.maximum(before, jnp.max(peak, axis=1, keepdims=True))
            fade = jnp.exp2((before - top) * factor)
            total = stats_ref[0, rows, 64:65] * fade
            mixed = sum_ref[0, rows, :] * fade
            gained = None
            for index in range(sections):
                side = index // 2
                weights = jnp.exp2((scores[index] - top) * factor)
                gained = weights if gained is None else gained + weights
                mixed = mixed + jnp.dot(
                    weights.astype(BF16),
                    keys(index, side * latent, (side + 1) * latent),
                    preferred_element_type=F32,
                )
            total = total + jnp.sum(gained, axis=1, keepdims=True)
            final = (mixed / total).astype(BF16).reshape(some, size, latent)
            mixed_ref[which, pl.ds(pl.multiple_of(request * size, size), size), :] = final

    count = pl.cdiv(length, section)
    for sections in range(1, 5):

        @pl.when(count == sections)
        def _():
            work(sections)

    value = values_ref.shape[2]

    @pl.when(request == pl.num_programs(0) - 1)
    def _():
        for head in range(heads):
            out_ref[:, head * value : (head + 1) * value] = jnp.dot(
                mixed_ref[head], values_ref[head], preferred_element_type=F32
            ).astype(BF16)


def context(scale, lengths, q, pages, stats, sums, up_values):
    heads, total_rows, wide = q.shape
    requests, rows, latent = sums.shape
    size = rows // heads
    value = up_values.shape[2]
    shares, all_rows, width = pages.shape
    per = all_rows // requests
    grid_spec = pltpu.PrefetchScalarGridSpec(
        num_scalar_prefetch=1,
        grid=(requests,),
        in_specs=[
            pl.BlockSpec((heads, size, wide), lambda i, *_: (0, i, 0)),
            pl.BlockSpec((shares, per, width), lambda i, *_: (0, i, 0)),
            pl.BlockSpec((1, rows, 128), lambda i, *_: (i, 0, 0)),
            pl.BlockSpec((1, rows, latent), lambda i, *_: (i, 0, 0)),
            pl.BlockSpec(up_values.shape, lambda i, *_: (0, 0, 0)),
        ],
        out_specs=pl.BlockSpec((total_rows, heads * value), lambda i, *_: (0, 0)),
        scratch_shapes=[pltpu.VMEM((heads, total_rows, latent), BF16)],
    )
    count = 2 * shares * per
    return pl.pallas_call(
        functools.partial(context_kernel, scale),
        grid_spec=grid_spec,
        out_shape=jax.ShapeDtypeStruct((total_rows, heads * value), BF16),
        cost_estimate=pl.CostEstimate(
            flops=2 * requests * rows * count * (2 * latent + 64),
            bytes_accessed=requests * rows * latent * 8,
            transcendentals=requests * rows * count,
        ),
        compiler_params=pltpu.CompilerParams(vmem_limit_bytes=VMEM_LIMIT),
        name="context",
    )(lengths, q, pages, stats, sums, up_values)


def local(
    q_nope,
    q_rope,
    up_keys,
    up_values,
    page_pool,
    page_table,
    lengths,
    prefix_latent,
    tree_latent,
    parents,
):
    heads, nope_dim, latent_dim = up_keys.shape
    rope_dim = q_rope.shape[1] // heads
    scale = (nope_dim + rope_dim) ** (-0.5)
    groups = lax.axis_size("decode")
    shares = lax.axis_size("pool")
    pool_local = page_pool.shape[0]
    width = page_pool.shape[2]
    me = lax.axis_index("pool")

    flat = page_table.reshape(-1)
    entries = flat.shape[0]
    owner_of = flat // pool_local
    order = jnp.arange(entries, dtype=jnp.int32)
    owners = jnp.arange(groups, dtype=jnp.int32) * shares + me
    match = owner_of[None, :] == owners[:, None]
    code = order * pool_local + flat % pool_local
    first = jnp.min(jnp.where(match, code[None, :], entries * pool_local), axis=1)
    last = jnp.max(jnp.where(match, code[None, :], 0), axis=1)
    asks = jnp.stack([first, last], axis=1) % pool_local
    wanted = lax.all_to_all(asks, "decode", split_axis=0, concat_axis=0, tiled=True)
    earlier = (order[None, :] < order[:, None]) & (owner_of[None, :] == owner_of[:, None])
    slot_of = jnp.any(earlier, axis=1).astype(jnp.int32)

    wide = latent_dim + 2 * rope_dim
    prefix = prefix_latent
    step = 1
    while step < groups:
        pairs = [(i, i ^ step) for i in range(groups)]
        prefix = jnp.concatenate([prefix, lax.ppermute(prefix, "decode", pairs)], axis=0)
        step *= 2
    prefix = jnp.pad(prefix, ((0, 0), (0, wide - width)))
    tree = jnp.pad(tree_latent, ((0, 0), (0, wide - width)))

    packed = pack(wanted, page_pool, shares)
    got = lax.all_to_all(packed, ("decode", "pool"), split_axis=0, concat_axis=0, tiled=True)
    q, seen = prepare(q_nope, q_rope, up_keys, parents)
    mine = compact(owner_of, slot_of, got, seen)
    pages = lax.all_gather(mine.reshape(-1, 2 * width), "pool", axis=0, tiled=False)
    stats, sums = base(scale, q, prefix, tree, seen)
    return context(scale, lengths, q, pages, stats, sums, up_values)


def solution(mesh):
    in_specs = (
        P("decode", "pool"),
        P("decode", "pool"),
        P("pool", None, None),
        P("pool", None, None),
        P(("decode", "pool"), None, None),
        P("decode", None),
        P("decode"),
        P("decode", None),
        P("decode", None),
        P("decode", None),
    )
    out_specs = P("decode", "pool")
    return jax.shard_map(local, mesh=mesh, in_specs=in_specs, out_specs=out_specs, check_vma=False)
```

time: 630 us -> 152 us (0.24); the launches traced: 622 us -> 151 us
  blocking collectives: 328 us -> 13.8 us
  matrix products: 113 us -> 0 us
  local copies, waits for them, and re-layouts: 119 us -> 10.3 us
  waiting for transfers between devices: 0.01 us -> 54.9 us
  Pallas kernels: 0 us -> 47.6 us
  other arithmetic: 34.9 us -> 0.45 us
  loops' own time: 21.3 us -> 0 us
  between operations: 0.15 us -> 13.6 us
    all_gather x1 -> x0, blocking collectives: 307 us -> none  [local(): prefix_all = lax.all_gather(prefix_latent, 'decode', axis=0, tiled=True)]
    dot_general x81 -> x0, matrix products: 113 us -> none  [the longest x24 53.4 us: against(): lax.dot_general(queries, keys, (((1,), (1,)), ((), ())), preferred_elemen...]
    gather x9 -> x0, local copies, waits for them, and re-layouts: 73.3 us -> none  [the longest x8 62 us: one_request(): jnp.take(fetched, slots[index], axis=0).reshape(pages_per * page_size, -1)]
    pallas_call x0 -> x5, Pallas kernels: none -> 47.6 us  [the longest x1 20.7 us: context(): pl.pallas_call(functools.partial(context_kernel, scale), grid_spec=grid_s...]
    another operation x1 -> x0, loops' own time: 21.3 us -> none  [local(): outputs = lax.map(one_request, jnp.arange(requests, dtype=jnp.int32))]
    all_to_all x1, waiting for transfers between devices: 0.01 us -> 19.6 us  [local(): lax.all_to_all(packed, ('decode', 'pool'), split_axis=0, concat_axis=0, t...]
    select_n x19 -> x1, other arithmetic: 19.5 us -> 0.02 us  [local(): asks = jnp.stack([first, last], axis=1) % pool_local]
    all_gather x0 -> x1, waiting for transfers between devices: none -> 19.1 us  [local(): lax.all_gather(mine.reshape(-1, 2 * width), 'pool', axis=0, tiled=False)]
  transfers between devices with their start and end apart: 1 -> 6, of which waited for: 0 -> 6; matrix products, arithmetic and copies ran while one was open for 2% -> 1% of each run, Pallas kernels for 0% -> 14%
where the time goes in v1:
time: 152 us; the launch traced here: 151 us
  waiting for transfers between devices  54.9 us (36%)
  Pallas kernels  47.6 us (31%)
  blocking collectives  13.8 us (9%)
  between operations  13.6 us (9%)
  local copies, waits for them, and re-layouts  10.3 us (7%)
  starting transfers between devices  10 us (7%)
    pallas_call x1, Pallas kernels, context(): pl.pallas_call(functools.partial(context_kernel, scale), grid_spec=grid_s...  20.7 us
    all_to_all x1, waiting for transfers between devices, local(): lax.all_to_all(packed, ('decode', 'pool'), split_axis=0, concat_axis=0, t...  19.6 us
    all_gather x1, waiting for transfers between devices, local(): lax.all_gather(mine.reshape(-1, 2 * width), 'pool', axis=0, tiled=False)  19.1 us
    ppermute x4, waiting for transfers between devices, local(): lax.ppermute(prefix, 'decode', pairs)  16.3 us
    all_to_all x1, blocking collectives, local(): lax.all_to_all(asks, 'decode', split_axis=0, concat_axis=0, tiled=True)  13.8 us
    pallas_call x1, Pallas kernels, base(): pl.pallas_call(functools.partial(base_kernel, scale), grid=(requests,), i...  12.9 us
    pallas_call x1, Pallas kernels, prepare(): pl.pallas_call(prepare_kernel, grid=(heads,), in_specs=[pl.BlockSpec((row...  8.72 us
    unnamed x33, local copies, waits for them, and re-layouts  8.4 us
  transfers between devices with their start and end apart: 6, of which 6 were waited for; matrix products, arithmetic and copies ran while one was open for 1% of the time, Pallas kernels for 14%

profile of v1, /device:TPU:1, one launch (start us, length us, event | category | flops | bytes accessed | tf_op | source)
XLA Modules:
  0.0 150.6 jit_solution(17378627387891399576)
XLA Ops:
  6.5 0.8 reshape.204
  7.6 13.8 %all_to_all.13 = s32[16,1,2]{2,1,0:T(1,128)S(1)} all-to-all(s32[16,1,2]{2,1,0:T(1,128)S(1)} %copy.22), channel_id=1, replica_groups=mesh['decode'=16,'pool'=8] {'decode'}, dimensions={0} | all-to-all | bytes 256 | tf_op jit(solution)/shard_map/all_to_all | solution.py:374
  21.4 1.7 %copy-done.1 = bf16[32,64,576]{2,1,0:T(8,128)(2,1)S(1)} copy-done((bf16[32,64,576]{2,1,0:T(8,128)(2,1)S(1)}, bf16[32,64,576]{2,1,0:T(8,128)(2,1)}, u32[]{:S(2)}) %copy-start.1) | copy-done | bytes 2359320
  23.1 2.0 %pack.1 = bf16[128,8,1152]{2,1,0:T(8,128)(2,1)S(1)} custom-call(s32[16,2]{1,0:T(8,128)S(1)} %bitcast.7, bf16[256,8,576]{2,1,0:T(8,128)(2,1)S(1)} %bitcast.6), custom_call_target="tpu_custom_call" | custom-call | bytes 5000000 | tf_op jit(solution)/shard_map/pack/pallas_call | solution.py:101
  25.1 1.4 copy-done
  26.5 8.3 %all-to-all-start.1 = ((bf16[128,8,1152]{2,1,0:T(8,128)(2,1)}), bf16[128,8,1152]{2,1,0:T(8,128)(2,1)S(1)}, u32[]{:S(2)}, u32[]{:S(2)}) async-start(bf16[128,8,1152]{2,1,0:T(8,128)(2,1)} %copy-done), calls=%async_computation.1 | async-start | bytes 4718592 | tf_op jit(solution)/shard_map/all_to_all | solution.py:389
  34.9 0.9 copy.21.parents_ref
  35.9 1.2 copy-done.3
  37.1 0.9 copy-done.4
  38.1 1.0 copy-done.5
  39.1 8.7 %prepare.1 = (bf16[8,512,768]{2,1,0:T(8,128)(2,1)}, f32[8,64,128]{2,1,0:T(8,128)S(1)}) custom-call(bf16[512,1024]{1,0:T(8,128)(2,1)S(1)} %copy-done.2, bf16[512,512]{1,0:T(8,128)(2,1)S(1)} %copy-done.5, bf16[8,128,512]{2,1,0:T(8,128)(2,1)S(1)} %copy-done.3, s32[8,64,1]{2,1,0:T(8,128)S(1)} %copy-done.4), custom_call_target="tpu_custom_call" | custom-call | flops 536870912 | bytes 10000000 | tf_op jit(solution)/shard_map/prepare/pallas_call | solution.py:52
  47.9 0.7 copy-done.6
  48.6 19.6 %all-to-all-done.1.got_ref = bf16[128,8,1152]{2,1,0:T(8,128)(2,1)S(1)} async-done(((bf16[128,8,1152]{2,1,0:T(8,128)(2,1)}), bf16[128,8,1152]{2,1,0:T(8,128)(2,1)S(1)}, u32[]{:S(2)}, u32[]{:S(2)}) %all-to-all-start.1) | async-done | bytes 2359328 | tf_op jit(solution)/shard_map/all_to_all | solution.py:389
  68.1 0.9 copy-done.7
  69.1 3.3 %compact.1 = bf16[64,8,1152]{2,1,0:T(8,128)(2,1)} custom-call(s32[128]{0:T(128)S(1)} %get-tuple-element.16.source_ref, s32[128]{0:T(128)S(1)} %convert_element_type.7.slot_ref, bf16[128,8,1152]{2,1,0:T(8,128)(2,1)S(1)} %all-to-all-done.1.got_ref, f32[8,64,128]{2,1,0:T(8,128)S(1)} %copy-done.7), custom_call_target="tpu_custom_call" | custom-call | bytes 4000000 | tf_op jit(solution)/shard_map/compact/pallas_call | solution.py:143
  72.5 2.7 %collective-permute-done = bf16[24,576]{1,0:T(8,128)(2,1)S(1)} collective-permute-done((bf16[24,576]{1,0:T(8,128)(2,1)S(1)}, bf16[24,576]{1,0:T(8,128)(2,1)S(1)}, u32[]{:S(2)}, u32[]{:S(2)}) %collective-permute-start) | collective-permute-done | bytes 27680 | tf_op jit(solution)/shard_map/ppermute | solution.py:383
  75.2 0.5 collective-permute-start.1
  76.1 3.8 %collective-permute-done.1 = bf16[48,576]{1,0:T(8,128)(2,1)S(1)} collective-permute-done((bf16[48,576]{1,0:T(8,128)(2,1)S(1)}, bf16[48,576]{1,0:T(8,128)(2,1)S(1)}, u32[]{:S(2)}, u32[]{:S(2)}) %collective-permute-start.1) | collective-permute-done | bytes 55328 | tf_op jit(solution)/shard_map/ppermute | solution.py:383
  80.3 3.8 %collective-permute-done.2 = bf16[96,576]{1,0:T(8,128)(2,1)S(1)} collective-permute-done((bf16[96,576]{1,0:T(8,128)(2,1)S(1)}, bf16[96,576]{1,0:T(8,128)(2,1)S(1)}, u32[]{:S(2)}, u32[]{:S(2)}) %collective-permute-start.2) | collective-permute-done | bytes 110624 | tf_op jit(solution)/shard_map/ppermute | solution.py:383
  84.1 0.8 collective-permute-start.3
  84.9 6.0 %collective-permute-done.3 = bf16[192,576]{1,0:T(8,128)(2,1)S(1)} collective-permute-done((bf16[192,576]{1,0:T(8,128)(2,1)S(1)}, bf16[192,576]{1,0:T(8,128)(2,1)S(1)}, u32[]{:S(2)}, u32[]{:S(2)}) %collective-permute-start.3) | collective-permute-done | bytes 221216 | tf_op jit(solution)/shard_map/ppermute | solution.py:383
  91.0 12.9 %base.1 = (f32[8,512,128]{2,1,0:T(8,128)S(1)}, f32[8,512,512]{2,1,0:T(8,128)}) custom-call(bf16[8,512,768]{2,1,0:T(8,128)(2,1)} %get-tuple-element.9.q_ref, bf16[384,640]{1,0:T(8,128)(2,1)S(1)} %pad.8.prefix_ref, bf16[512,640]{1,0:T(8,128)(2,1)S(1)} %pad.9.tree_ref, f32[8,64,128]{2,1,0:T(8,128)S(1)} %copy-done.8), custom_call_target="tpu_custom_call" | custom-call | flops 4563402752 | bytes 16777216 | tf_op jit(solution)/shard_map/base/pallas_call | solution.py:202
  104.0 19.1 %all-gather.2.cloned.1.call-done.pages_ref = bf16[8,512,1152]{2,1,0:T(8,128)(2,1)} async-done(((bf16[1,512,1152]{2,1,0:T(8,128)(2,1)}), bf16[8,512,1152]{2,1,0:T(8,128)(2,1)}) %all-gather.2.cloned.1.call-update) | async-done | bytes 9437200 | tf_op jit(solution)/shard_map/all_gather | solution.py:392
  123.1 20.7 %context.1 = bf16[512,1024]{1,0:T(8,128)(2,1)} custom-call(s32[8]{0:T(128)S(1)} %copy-done.10, bf16[8,512,768]{2,1,0:T(8,128)(2,1)} %get-tuple-element.9.q_ref, bf16[8,512,1152]{2,1,0:T(8,128)(2,1)} %all-gather.2.cloned.1.call-done.pages_ref, f32[8,512,128]{2,1,0:T(8,128)S(1)} %get-tuple-element.11.stats_ref, f32[8,512,512]{2,1,0:T(8,128)} %get-tuple-element.12.sum_ref, ...), custom_call_target="tpu_custom_call" | custom-call | flops 9126805504 | bytes 16777216 | tf_op jit(solution)/shard_map/context/pallas_call | solution.py:329
  (43 shorter events, 1.6 us)
Async XLA Ops:
  21.4 1.7 %copy-start.1 = (bf16[32,64,576]{2,1,0:T(8,128)(2,1)S(1)}, bf16[32,64,576]{2,1,0:T(8,128)(2,1)}, u32[]{:S(2)}) copy-start(bf16[32,64,576]{2,1,0:T(8,128)(2,1)} %param.14) | copy-start | bytes 7077892
  25.1 1.4 copy-start
  26.5 8.3 %copy-start.13 = (s32[8,64]{1,0:T(8,128)S(1)}, s32[8,64]{1,0:T(8,128)}, u32[]{:S(2)}) copy-start(s32[8,64]{1,0:T(8,128)} %param.19) | copy-start | bytes 6148
  26.5 9.4 %copy-start.2 = (bf16[512,1024]{1,0:T(8,128)(2,1)S(1)}, bf16[512,1024]{1,0:T(8,128)(2,1)}, u32[]{:S(2)}) copy-start(bf16[512,1024]{1,0:T(8,128)(2,1)} %rows_ref.1) | copy-start | bytes 3145732
  26.5 41.6 %all-to-all-start.1 = ((bf16[128,8,1152]{2,1,0:T(8,128)(2,1)}), bf16[128,8,1152]{2,1,0:T(8,128)(2,1)S(1)}, u32[]{:S(2)}, u32[]{:S(2)}) async-start(bf16[128,8,1152]{2,1,0:T(8,128)(2,1)} %copy-done), calls=%async_computation.1 | async-start | bytes 4718592 | tf_op jit(solution)/shard_map/all_to_all | solution.py:389
  34.8 88.3 %all-gather.2.cloned.1.call-start = ((), (), s32[]{:S(2)}) async-start(), calls=%async_computation.2 | async-start | bytes 10616832 | tf_op jit(solution)/shard_map/all_gather | solution.py:392
  35.9 1.2 copy-start.3
  37.1 0.9 copy-start.4
  38.1 1.0 copy-start.5
  39.1 33.2 %copy-start.12 = (bf16[24,576]{1,0:T(8,128)(2,1)S(1)}, bf16[24,576]{1,0:T(8,128)(2,1)}, u32[]{:S(2)}) copy-start(bf16[24,576]{1,0:T(8,128)(2,1)} %param.17) | copy-start | bytes 82948
  47.9 0.7 copy-start.6
  68.1 1.0 copy-start.7
  69.1 6.7 %copy-start.11 = (bf16[512,576]{0,1:T(8,128)(2,1)S(1)}, bf16[512,576]{0,1:T(8,128)(2,1)}, u32[]{:S(2)}) copy-start(bf16[512,576]{0,1:T(8,128)(2,1)} %param.18) | copy-start | bytes 1769476
  72.4 2.8 %collective-permute-start = (bf16[24,576]{1,0:T(8,128)(2,1)S(1)}, bf16[24,576]{1,0:T(8,128)(2,1)S(1)}, u32[]{:S(2)}, u32[]{:S(2)}) collective-permute-start(bf16[24,576]{1,0:T(8,128)(2,1)S(1)} %copy-done.12), channel_id=1, source_target_pairs={{0,8},{8,0},{16,24},{24,16},{32,40},{40,32},{48,56},{56,48},{64,72... | collective-permute-start | bytes 82952 | tf_op jit(solution)/shard_map/ppermute | solution.py:383
  75.2 15.8 %copy-start.8 = (f32[8,64,128]{2,1,0:T(8,128)S(1)}, f32[8,64,128]{2,1,0:T(8,128)}, u32[]{:S(2)}) copy-start(f32[8,64,128]{2,1,0:T(8,128)} %copy-done.6) | copy-start | bytes 786436
  75.2 4.7 %collective-permute-start.1 = (bf16[48,576]{1,0:T(8,128)(2,1)S(1)}, bf16[48,576]{1,0:T(8,128)(2,1)S(1)}, u32[]{:S(2)}, u32[]{:S(2)}) collective-permute-start(bf16[48,576]{1,0:T(8,128)(2,1)S(1)} %pad_maximum_fusion.2), channel_id=1, source_target_pairs={{0,16},{8,24},{16,0},{24,8},{32,48},{40,56},{48,32},{56,40},{64,80... | collective-permute-start | bytes 165896 | tf_op jit(solution)/shard_map/ppermute | solution.py:383
  79.9 4.2 %collective-permute-start.2 = (bf16[96,576]{1,0:T(8,128)(2,1)S(1)}, bf16[96,576]{1,0:T(8,128)(2,1)S(1)}, u32[]{:S(2)}, u32[]{:S(2)}) collective-permute-start(bf16[96,576]{1,0:T(8,128)(2,1)S(1)} %pad_maximum_fusion.1), channel_id=1, source_target_pairs={{0,32},{8,40},{16,48},{24,56},{32,0},{40,8},{48,16},{56,24},{64,96... | collective-permute-start | bytes 331784 | tf_op jit(solution)/shard_map/ppermute | solution.py:383
  84.1 6.8 %collective-permute-start.3 = (bf16[192,576]{1,0:T(8,128)(2,1)S(1)}, bf16[192,576]{1,0:T(8,128)(2,1)S(1)}, u32[]{:S(2)}, u32[]{:S(2)}) collective-permute-start(bf16[192,576]{1,0:T(8,128)(2,1)S(1)} %pad_maximum_fusion), channel_id=1, source_target_pairs={{0,64},{8,72},{16,80},{24,88},{32,96},{40,104},{48,112},{56,120},{... | collective-permute-start | bytes 663560 | tf_op jit(solution)/shard_map/ppermute | solution.py:383
  91.0 32.0 %copy-start.9 = (bf16[8,512,128]{2,1,0:T(8,128)(2,1)S(1)}, bf16[8,512,128]{2,1,0:T(8,128)(2,1)}, u32[]{:S(2)}) copy-start(bf16[8,512,128]{2,1,0:T(8,128)(2,1)} %values_ref.1) | copy-start | bytes 3145732
  91.0 32.0 %copy-start.10 = (s32[8]{0:T(128)S(1)}, s32[8]{0:T(128)}, u32[]{:S(2)}) copy-start(s32[8]{0:T(128)} %lengths_ref.1) | copy-start | bytes 100
Sparse Core Ops, SparseCore 0:
  72.5 50.5 all-gather.1

commit v2 on v1

v2 whole, which is shorter than its diff:
```python
import functools
import math

import jax
import jax.numpy as jnp
from jax import lax
from jax.experimental import pallas as pl
from jax.experimental.pallas import tpu as pltpu
from jax.sharding import PartitionSpec as P

F32 = jnp.float32
BF16 = jnp.bfloat16
VMEM_LIMIT = 48 * 1024 * 1024


def nt_dot(a, b):
    return lax.dot_general(a, b, (((1,), (1,)), ((), ())), preferred_element_type=F32)


def prepare_kernel(rows_ref, rope_ref, keys_ref, parents_ref, q_ref, seen_ref):
    head = pl.program_id(0)
    latent = keys_ref.shape[2]
    absorbed = jnp.dot(rows_ref[...], keys_ref[0], preferred_element_type=F32)
    q_ref[0, :, :latent] = absorbed.astype(BF16)
    pair = rope_ref[...].astype(F32)
    lane = lax.broadcasted_iota(jnp.int32, pair.shape, 1)
    half = pair.shape[1] // 2
    turned = pltpu.roll(pair, half, 1)
    even = lax.rem(head, 2) == 0
    source = jnp.where(even, pair, turned)
    other = jnp.where(even, turned, pair)
    q_ref[0, :, latent : latent + 2 * half] = jnp.where(lane < half, source, 0.0).astype(BF16)
    q_ref[0, :, latent + 2 * half :] = jnp.where(lane >= half, other, 0.0).astype(BF16)
    size = parents_ref.shape[1]
    columns = lax.broadcasted_iota(jnp.int32, (size, size), 1)
    rows = lax.broadcasted_iota(jnp.int32, (size, size), 0)
    links = (parents_ref[0] == columns) | (rows == columns)
    reach = links.astype(F32)
    for sweep in range(max(1, (size - 1).bit_length())):
        reach = jnp.minimum(
            jnp.dot(reach.astype(BF16), reach.astype(BF16), preferred_element_type=F32), 1.0
        )
    lowest = jnp.full((size, size), -jnp.inf, F32)
    seen_ref[0] = jnp.concatenate([jnp.where(reach > 0.5, 0.0, lowest), lowest], axis=1)


def prepare(q_nope, q_rope, up_keys, parents):
    heads, nope, latent = up_keys.shape
    rows = q_nope.shape[0]
    requests, size = parents.shape
    rope = q_rope.shape[1] // heads
    return pl.pallas_call(
        prepare_kernel,
        grid=(heads,),
        in_specs=[
            pl.BlockSpec((rows, nope), lambda h: (0, h)),
            pl.BlockSpec((rows, 2 * rope), lambda h: (0, h // 2)),
            pl.BlockSpec((1, nope, latent), lambda h: (h, 0, 0)),
            pl.BlockSpec((1, size, 1), lambda h: (h, 0, 0)),
        ],
        out_specs=[
            pl.BlockSpec((1, rows, latent + 4 * rope), lambda h: (h, 0, 0)),
            pl.BlockSpec((1, size, 2 * size), lambda h: (h, 0, 0)),
        ],
        out_shape=[
            jax.ShapeDtypeStruct((heads, rows, latent + 4 * rope), BF16),
            jax.ShapeDtypeStruct((requests, size, 2 * size), F32),
        ],
        cost_estimate=pl.CostEstimate(
            flops=2 * rows * heads * nope * latent, bytes_accessed=10_000_000, transcendentals=0
        ),
        compiler_params=pltpu.CompilerParams(vmem_limit_bytes=VMEM_LIMIT),
        name="prepare",
    )(q_nope, q_rope, up_keys, parents[:, :, None])


def pack_kernel(wanted_ref, pool_ref, out_ref):
    groups = wanted_ref.shape[0]
    shares = out_ref.shape[0] // groups
    latent = 512
    rope = pool_ref.shape[2] - latent

    def body(group, carry):
        first = pool_ref.at[pl.ds(wanted_ref[group, 0] * shares, shares)]
        second = pool_ref.at[pl.ds(wanted_ref[group, 1] * shares, shares)]
        out = out_ref.at[pl.ds(group * shares, shares)]
        out[:, :, :latent] = first[:, :, :latent]
        out[:, :, latent : 2 * latent] = second[:, :, :latent]
        out[:, :, 2 * latent :] = jnp.concatenate(
            [first[:, :, latent:], second[:, :, latent:]], axis=2
        )
        return carry

    lax.fori_loop(0, groups, body, 0)


def pack(wanted, pool, shares):
    groups = wanted.shape[0]
    eighth = pool.shape[1] // shares
    width = pool.shape[2]
    return pl.pallas_call(
        pack_kernel,
        in_specs=[
            pl.BlockSpec(memory_space=pltpu.SMEM),
            pl.BlockSpec(memory_space=pltpu.VMEM),
        ],
        out_specs=pl.BlockSpec(memory_space=pltpu.VMEM),
        out_shape=jax.ShapeDtypeStruct((groups * shares, eighth, 2 * width), BF16),
        cost_estimate=pl.CostEstimate(flops=0, bytes_accessed=5_000_000, transcendentals=0),
        compiler_params=pltpu.CompilerParams(vmem_limit_bytes=VMEM_LIMIT),
        name="pack",
    )(wanted, pool.reshape(pool.shape[0] * shares, eighth, width))


def compact_kernel(source_ref, slot_ref, got_ref, after_ref, out_ref):
    pairs = out_ref.shape[0]
    per = 8
    latent = 512
    half = (out_ref.shape[2] - 2 * latent) // 2

    def body(k, carry):
        request = k // per
        first = request * (2 * per) + lax.rem(k, per)
        ropes = []
        for side, entry in enumerate((first, first + per)):
            source = source_ref[entry]
            slot = slot_ref[entry]
            start = pl.multiple_of(slot * latent, latent)
            out_ref[k, :, side * latent : (side + 1) * latent] = got_ref[
                source, :, pl.ds(start, latent)
            ]
            both = got_ref[source, :, 2 * latent :].astype(F32)
            ropes.append(jnp.where(slot == side, both, pltpu.roll(both, half, 1)))
        lane = lax.broadcasted_iota(jnp.int32, ropes[0].shape, 1)
        out_ref[k, :, 2 * latent :] = jnp.where(lane < half, ropes[0], ropes[1]).astype(BF16)
        return carry

    lax.fori_loop(0, pairs, body, 0, unroll=4)


def compact(source, slot, got, after):
    entries = source.shape[0]
    return pl.pallas_call(
        compact_kernel,
        in_specs=[
            pl.BlockSpec(memory_space=pltpu.SMEM),
            pl.BlockSpec(memory_space=pltpu.SMEM),
            pl.BlockSpec(memory_space=pltpu.VMEM),
            pl.BlockSpec(memory_space=pltpu.SMEM),
        ],
        out_specs=pl.BlockSpec(memory_space=pltpu.VMEM),
        out_shape=jax.ShapeDtypeStruct((entries // 2,) + got.shape[1:], BF16),
        cost_estimate=pl.CostEstimate(flops=0, bytes_accessed=4_000_000, transcendentals=0),
        compiler_params=pltpu.CompilerParams(vmem_limit_bytes=VMEM_LIMIT),
        name="compact",
    )(source, slot, got, after)


def spread(column, width):
    if width <= 128:
        return column[:, :width]
    return jnp.concatenate([column] * (width // 128), axis=1)


def attend_kernel(scale, picks, shared, halves, finish, lengths_ref, shares_ref, q_ref, *refs):
    refs = list(refs)
    taken = [refs.pop(0) for _ in range(3)]
    pieces = [
        (refs.pop(0), refs.pop(0)) if halves else (refs.pop(0),) for _ in range(len(picks))
    ]
    values_ref = refs.pop(0) if finish else None
    if finish:
        out_ref, keys_ref, mixed_ref = refs
    else:
        top_out, total_out, sum_out, keys_ref = refs
    heads, size, wide = q_ref.shape
    latent = wide - 256
    part = pieces[0][0].shape[0] // 2
    section = len(picks) * part
    origin = keys_ref.shape[0] - 4 * section
    request = pl.program_id(0)
    length = lengths_ref[request]
    factor = scale * math.log2(math.e)
    lowest = F32(-jnp.inf)
    some = 8
    block = some * size

    @pl.when(request == 0)
    def _():
        keys_ref[:, latent:] = jnp.zeros((keys_ref.shape[0], 256), BF16)
        if shared:
            prompt = taken[0].shape[0]
            keys_ref[:prompt, : latent + 128] = taken[0][...]
            keys_ref[prompt + size : origin, :latent] = jnp.zeros(
                (origin - prompt - size, latent), BF16
            )

    if shared:
        prompt = taken[0].shape[0]
        keys_ref[prompt : prompt + size, : latent + 128] = taken[1][...]
    for which, refs_of in enumerate(pieces):
        piece = refs_of[0][...]
        if halves:
            piece = jnp.where(request < pl.num_programs(0) // 2, piece, refs_of[1][...])
        for index in range(4):
            side, half = index // 2, index % 2
            rows = slice(
                origin + index * section + which * part,
                origin + index * section + (which + 1) * part,
            )
            some_rows = piece[half * part : (half + 1) * part]
            keys_ref[rows, :latent] = some_rows[:, side * latent : (side + 1) * latent]
            keys_ref[rows, latent + side * 128 : latent + (side + 1) * 128] = some_rows[
                :, 2 * latent :
            ]

    def work(sections):
        count = sections * section
        column = lax.broadcasted_iota(jnp.int32, (1, count), 1)
        position = column // section * 256 + column % part // 8 * 64 + column % 8
        for which, pick in enumerate(picks):
            position = position + jnp.where(
                column // part % len(picks) == which, shares_ref[pick] * 8, 0
            )
        bias = jnp.where(position < length, 0.0, lowest)
        if shared:
            hidden = jnp.concatenate([taken[2][0]] * some, axis=0)
        for step in range(heads // some):
            which = slice(step * some, (step + 1) * some)
            rows = slice(step * block, (step + 1) * block)
            q = q_ref[which].reshape(block, wide)
            scores = nt_dot(q, keys_ref[origin : origin + count, :]) + bias
            if shared:
                first = nt_dot(q, keys_ref[:prompt, :])
                tree = nt_dot(q, keys_ref[prompt:origin, :]) + hidden
                scores = jnp.concatenate([first, tree, scores], axis=1)
            top = jnp.broadcast_to(jnp.max(scores, axis=1, keepdims=True), (block, 128))
            if not shared:
                before = taken[0][0, rows, :]
                top = jnp.maximum(top, before)
                fade = jnp.exp2((before - top) * factor)
            weights = jnp.exp2((scores - spread(top, scores.shape[1])) * factor)
            total = jnp.broadcast_to(jnp.sum(weights, axis=1, keepdims=True), (block, 128))
            mixed = jnp.dot(
                weights.astype(BF16),
                keys_ref[0 if shared else origin : origin + count, :latent],
                preferred_element_type=F32,
            )
            if not shared:
                total = total + taken[1][0, rows, :] * fade
                mixed = mixed + taken[2][0, rows, :] * spread(fade, latent)
            if finish:
                mixed = mixed * spread(1.0 / total, latent)
                mixed_ref[which, pl.ds(pl.multiple_of(request * size, size), size), :] = (
                    mixed.astype(BF16).reshape(some, size, latent)
                )
            else:
                top_out[0, rows, :] = top
                total_out[0, rows, :] = total
                sum_out[0, rows, :] = mixed

    needed = pl.cdiv(length, 256)
    steps = (1, 2, 3, 4) if section % 128 == 0 else (2, 4)
    for low, high in zip((0,) + steps, steps):

        @pl.when((needed > low) & (needed <= high))
        def _():
            work(high)

    if finish:
        value = values_ref.shape[2]

        @pl.when(request == pl.num_programs(0) - 1)
        def _():
            for head in range(heads):
                out_ref[:, head * value : (head + 1) * value] = jnp.dot(
                    mixed_ref[head], values_ref[head], preferred_element_type=F32
                ).astype(BF16)


def attend(name, scale, lengths, shares, picks, q, shared, given, pieces, up_values=None):
    heads, total_rows, wide = q.shape
    requests = lengths.shape[0]
    size = total_rows // requests
    rows = heads * size
    latent = wide - 256
    halves = isinstance(pieces[0], tuple)
    finish = up_values is not None
    flat = [array for piece in pieces for array in (piece if halves else (piece,))]
    per = flat[0].shape[0] * (2 if halves else 1) // requests
    width = flat[0].shape[1]
    half = requests // 2
    origin = given[0].shape[0] + 2 * size if shared else 0
    count = origin + 2 * per * len(pieces)

    state_specs = [
        pl.BlockSpec((1, rows, 128), lambda i, *_: (i, 0, 0)),
        pl.BlockSpec((1, rows, 128), lambda i, *_: (i, 0, 0)),
        pl.BlockSpec((1, rows, latent), lambda i, *_: (i, 0, 0)),
    ]
    in_specs = [pl.BlockSpec((heads, size, wide), lambda i, *_: (0, i, 0))]
    if shared:
        in_specs += [
            pl.BlockSpec(given[0].shape, lambda i, *_: (0, 0)),
            pl.BlockSpec((size, given[1].shape[1]), lambda i, *_: (i, 0)),
            pl.BlockSpec((1, size, 2 * size), lambda i, *_: (i, 0, 0)),
        ]
    else:
        in_specs += state_specs
    for _ in pieces:
        if halves:
            in_specs.append(
                pl.BlockSpec((per, width), lambda i, *_: (jnp.minimum(i, half - 1), 0))
            )
            in_specs.append(pl.BlockSpec((per, width), lambda i, *_: (jnp.maximum(i - half, 0), 0)))
        else:
            in_specs.append(pl.BlockSpec((per, width), lambda i, *_: (i, 0)))
    operands = [lengths, shares, q, *given, *flat]
    scratch = [pltpu.VMEM((count, wide), BF16)]
    if finish:
        value = up_values.shape[2]
        operands.append(up_values)
        in_specs.append(pl.BlockSpec(up_values.shape, lambda i, *_: (0, 0, 0)))
        out_specs = pl.BlockSpec((total_rows, heads * value), lambda i, *_: (0, 0))
        out_shape = jax.ShapeDtypeStruct((total_rows, heads * value), BF16)
        scratch.append(pltpu.VMEM((heads, total_rows, latent), BF16))
    else:
        out_specs = state_specs
        out_shape = [
            jax.ShapeDtypeStruct((requests, rows, 128), F32),
            jax.ShapeDtypeStruct((requests, rows, 128), F32),
            jax.ShapeDtypeStruct((requests, rows, latent), F32),
        ]
    return pl.pallas_call(
        functools.partial(attend_kernel, scale, picks, shared, halves, finish),
        grid_spec=pltpu.PrefetchScalarGridSpec(
            num_scalar_prefetch=2,
            grid=(requests,),
            in_specs=in_specs,
            out_specs=out_specs,
            scratch_shapes=scratch,
        ),
        out_shape=out_shape,
        cost_estimate=pl.CostEstimate(
            flops=2 * requests * rows * count * (2 * latent + 64),
            bytes_accessed=requests * rows * latent * 8,
            transcendentals=requests * rows * count,
        ),
        compiler_params=pltpu.CompilerParams(vmem_limit_bytes=VMEM_LIMIT),
        name=name,
    )(*operands)


def local(
    q_nope,
    q_rope,
    up_keys,
    up_values,
    page_pool,
    page_table,
    lengths,
    prefix_latent,
    tree_latent,
    parents,
):
    heads, nope_dim, latent_dim = up_keys.shape
    rope_dim = q_rope.shape[1] // heads
    scale = (nope_dim + rope_dim) ** (-0.5)
    groups = lax.axis_size("decode")
    shares = lax.axis_size("pool")
    pool_local = page_pool.shape[0]
    width = page_pool.shape[2]
    me = lax.axis_index("pool")

    flat = page_table.reshape(-1)
    entries = flat.shape[0]
    owner_of = flat // pool_local
    order = jnp.arange(entries, dtype=jnp.int32)
    owners = jnp.arange(groups, dtype=jnp.int32) * shares + me
    match = owner_of[None, :] == owners[:, None]
    code = order * pool_local + flat % pool_local
    first = jnp.min(jnp.where(match, code[None, :], entries * pool_local), axis=1)
    last = jnp.max(jnp.where(match, code[None, :], 0), axis=1)
    asks = jnp.stack([first, last], axis=1) % pool_local
    wanted = lax.all_to_all(asks, "decode", split_axis=0, concat_axis=0, tiled=True)
    earlier = (order[None, :] < order[:, None]) & (owner_of[None, :] == owner_of[:, None])
    slot_of = jnp.any(earlier, axis=1).astype(jnp.int32)

    wide = latent_dim + 2 * rope_dim
    prefix = prefix_latent
    step = 1
    while step < groups:
        pairs = [(i, i ^ step) for i in range(groups)]
        prefix = jnp.concatenate([prefix, lax.ppermute(prefix, "decode", pairs)], axis=0)
        step *= 2
    prefix = jnp.pad(prefix, ((0, 0), (0, wide - width)))
    tree = jnp.pad(tree_latent, ((0, 0), (0, wide - width)))

    packed = pack(wanted, page_pool, shares)
    got = lax.all_to_all(packed, ("decode", "pool"), split_axis=0, concat_axis=0, tiled=True)
    q, hidden = prepare(q_nope, q_rope, up_keys, parents)
    after = hidden[0, :1, :1] + prefix[-1:, :1].astype(F32)
    own = compact(owner_of, slot_of, got, after).reshape(-1, 2 * width)

    swap = [(i, i ^ 1) for i in range(shares)]
    up = [(i, (i + 2) % shares) for i in range(shares)]
    down = [(i, (i - 2) % shares) for i in range(shares)]
    me = lax.axis_index("pool")
    other = me + 1 - 2 * (me % 2)
    at = [me, other, me - 2, me + 2, other - 2, other + 2, me + 4, other + 4]
    at = jnp.stack([place % shares for place in at]).astype(jnp.int32)
    below = lax.ppermute(own, "pool", up)
    above = lax.ppermute(own, "pool", down)
    beside = lax.ppermute(own, "pool", swap)
    state = attend(
        "first", scale, lengths, at, (0, 1), q, True, (prefix, tree, hidden), [own, beside]
    )
    below, above, state = lax.optimization_barrier((below, above, state))
    middle = own.shape[0] // 2
    far_up = lax.ppermute(below[:middle], "pool", up)
    far_down = lax.ppermute(above[middle:], "pool", down)
    below_beside = lax.ppermute(below, "pool", swap)
    above_beside = lax.ppermute(above, "pool", swap)
    state = attend(
        "second",
        scale,
        lengths,
        at,
        (2, 3, 4, 5),
        q,
        False,
        state,
        [below, above, below_beside, above_beside],
    )
    far_up, far_down, state = lax.optimization_barrier((far_up, far_down, state))
    far_up_beside = lax.ppermute(far_up, "pool", swap)
    far_down_beside = lax.ppermute(far_down, "pool", swap)
    return attend(
        "third",
        scale,
        lengths,
        at,
        (6, 7),
        q,
        False,
        state,
        [(far_up, far_down), (far_up_beside, far_down_beside)],
        up_values,
    )


def solution(mesh):
    in_specs = (
        P("decode", "pool"),
        P("decode", "pool"),
        P("pool", None, None),
        P("pool", None, None),
        P(("decode", "pool"), None, None),
        P("decode", None),
        P("decode"),
        P("decode", None),
        P("decode", None),
        P("decode", None),
    )
    out_specs = P("decode", "pool")
    return jax.shard_map(local, mesh=mesh, in_specs=in_specs, out_specs=out_specs, check_vma=False)
```

time: 152 us -> 164 us (1.079)
  starting transfers between devices: 10 us -> 34.9 us
  waiting for transfers between devices: 54.9 us -> 35.2 us
  between operations: 13.6 us -> 1.45 us
  Pallas kernels: 47.6 us -> 58.9 us
  local copies, waits for them, and re-layouts: 10.3 us -> 17.4 us
    all_to_all x1, waiting for transfers between devices: 19.6 us -> 0.01 us  [local(): lax.all_to_all(packed, ('decode', 'pool'), split_axis=0, concat_axis=0, t...]
    all_gather x1 -> x0, waiting for transfers between devices: 19.1 us -> none  [local(): lax.all_gather(mine.reshape(-1, 2 * width), 'pool', axis=0, tiled=False)]
    ppermute x4, starting transfers between devices: 1.75 us -> 15.9 us  [local(): lax.ppermute(prefix, 'decode', pairs)]
    pallas_call x2 -> x3, Pallas kernels: 33.7 us -> 46.1 us  [attend(): pl.pallas_call(functools.partial(attend_kernel, scale, picks, shared, hal...]
    ppermute x0 -> x9, waiting for transfers between devices: none -> 12.3 us  [the longest x1 8.81 us: local(): below = lax.ppermute(own, 'pool', up)]
    ppermute x0 -> x9, starting transfers between devices: none -> 10.7 us  [the longest x1 3.26 us: local(): beside = lax.ppermute(own, 'pool', swap)]
    ppermute x4, waiting for transfers between devices: 16.3 us -> 22.9 us  [local(): lax.ppermute(prefix, 'decode', pairs)]
    unnamed x33 -> x47, local copies, waits for them, and re-layouts: 8.4 us -> 11.6 us
  transfers between devices with their start and end apart: 6 -> 14, of which waited for: 6 -> 7; matrix products, arithmetic and copies ran while one was open for 1% -> 5% of each run, Pallas kernels for 14% -> 25%
where the time goes in v2:
time: 164 us; the launch traced here: 163 us
  Pallas kernels  58.9 us (36%)
  waiting for transfers between devices  35.2 us (21%)
  starting transfers between devices  34.9 us (21%)
  local copies, waits for them, and re-layouts  17.4 us (11%)
  blocking collectives  13.8 us (8%)
    pallas_call x3, Pallas kernels, attend(): pl.pallas_call(functools.partial(attend_kernel, scale, picks, shared, hal...  46.1 us
    ppermute x4, waiting for transfers between devices, local(): lax.ppermute(prefix, 'decode', pairs)  22.9 us
    ppermute x4, starting transfers between devices, local(): lax.ppermute(prefix, 'decode', pairs)  15.9 us
    all_to_all x1, blocking collectives, local(): lax.all_to_all(asks, 'decode', split_axis=0, concat_axis=0, tiled=True)  13.8 us
    unnamed x47, local copies, waits for them, and re-layouts  11.6 us
    ppermute x1, waiting for transfers between devices, local(): below = lax.ppermute(own, 'pool', up)  8.81 us
    pallas_call x1, Pallas kernels, prepare(): pl.pallas_call(prepare_kernel, grid=(heads,), in_specs=[pl.BlockSpec((row...  8.73 us
    all_to_all x1, starting transfers between devices, local(): lax.all_to_all(packed, ('decode', 'pool'), split_axis=0, concat_axis=0, t...  8.25 us
  transfers between devices with their start and end apart: 14, of which 7 were waited for; matrix products, arithmetic and copies ran while one was open for 5% of the time, Pallas kernels for 25%

profile of v2, /device:TPU:1, one launch (start us, length us, event | category | flops | bytes accessed | tf_op | source)
XLA Modules:
  0.0 162.8 jit_solution(7440887259559652539)
XLA Ops:
  1.1 13.8 %all_to_all.13 = s32[16,1,2]{2,1,0:T(1,128)S(1)} all-to-all(s32[16,1,2]{2,1,0:T(1,128)S(1)} %copy.22), channel_id=1, replica_groups=mesh['decode'=16,'pool'=8] {'decode'}, dimensions={0} | all-to-all | bytes 256 | tf_op jit(solution)/shard_map/all_to_all | solution.py:385
  14.9 1.7 %copy-done.1 = bf16[32,64,576]{2,1,0:T(8,128)(2,1)S(1)} copy-done((bf16[32,64,576]{2,1,0:T(8,128)(2,1)S(1)}, bf16[32,64,576]{2,1,0:T(8,128)(2,1)}, u32[]{:S(2)}) %copy-start.1) | copy-done | bytes 2359320
  16.6 2.0 %pack.1 = bf16[128,8,1152]{2,1,0:T(8,128)(2,1)S(1)} custom-call(s32[16,2]{1,0:T(8,128)S(1)} %bitcast.20, bf16[256,8,576]{2,1,0:T(8,128)(2,1)S(1)} %bitcast.15), custom_call_target="tpu_custom_call" | custom-call | bytes 5000000 | tf_op jit(solution)/shard_map/pack/pallas_call | solution.py:101
  18.6 1.4 copy-done
  20.0 8.3 %all-to-all-start.1 = ((bf16[128,8,1152]{2,1,0:T(8,128)(2,1)}), bf16[128,8,1152]{2,1,0:T(8,128)(2,1)S(1)}, u32[]{:S(2)}, u32[]{:S(2)}) async-start(bf16[128,8,1152]{2,1,0:T(8,128)(2,1)} %copy-done), calls=%async_computation.1 | async-start | bytes 4718592 | tf_op jit(solution)/shard_map/all_to_all | solution.py:400
  28.2 1.5 collective-permute-start
  29.7 14.3 %collective-permute-done = bf16[24,576]{1,0:T(8,128)(2,1)S(1)} collective-permute-done((bf16[24,576]{1,0:T(8,128)(2,1)S(1)}, bf16[24,576]{1,0:T(8,128)(2,1)S(1)}, u32[]{:S(2)}, u32[]{:S(2)}) %collective-permute-start) | collective-permute-done | bytes 27680 | tf_op jit(solution)/shard_map/ppermute | solution.py:394
  44.1 9.8 %collective-permute-start.1 = (bf16[48,576]{1,0:T(8,128)(2,1)S(1)}, bf16[48,576]{1,0:T(8,128)(2,1)S(1)}, u32[]{:S(2)}, u32[]{:S(2)}) collective-permute-start(bf16[48,576]{1,0:T(8,128)(2,1)S(1)} %pad_maximum_fusion.2), channel_id=1, source_target_pairs={{0,16},{8,24},{16,0},{24,8},{32,48},{40,56},{48,32},{56,40},{64,80... | collective-permute-start | bytes 165896 | tf_op jit(solution)/shard_map/ppermute | solution.py:394
  53.9 6.1 %collective-permute-done.1 = bf16[48,576]{1,0:T(8,128)(2,1)S(1)} collective-permute-done((bf16[48,576]{1,0:T(8,128)(2,1)S(1)}, bf16[48,576]{1,0:T(8,128)(2,1)S(1)}, u32[]{:S(2)}, u32[]{:S(2)}) %collective-permute-start.1) | collective-permute-done | bytes 55328 | tf_op jit(solution)/shard_map/ppermute | solution.py:394
  61.4 2.5 %collective-permute-done.2 = bf16[96,576]{1,0:T(8,128)(2,1)S(1)} collective-permute-done((bf16[96,576]{1,0:T(8,128)(2,1)S(1)}, bf16[96,576]{1,0:T(8,128)(2,1)S(1)}, u32[]{:S(2)}, u32[]{:S(2)}) %collective-permute-start.2) | collective-permute-done | bytes 110624 | tf_op jit(solution)/shard_map/ppermute | solution.py:394
  65.2 3.3 %collective-permute-start.3 = (bf16[192,576]{1,0:T(8,128)(2,1)}, bf16[192,576]{1,0:T(8,128)(2,1)}, u32[]{:S(2)}, u32[]{:S(2)}) collective-permute-start(bf16[192,576]{1,0:T(8,128)(2,1)} %pad_maximum_fusion), channel_id=1, source_target_pairs={{0,64},{8,72},{16,80},{24,88},{32,96},{40,104},{48,112},{56,120},{... | collective-permute-start | bytes 663560 | tf_op jit(solution)/shard_map/ppermute | solution.py:394
  72.6 8.7 %prepare.1 = (bf16[8,512,768]{2,1,0:T(8,128)(2,1)}, f32[8,64,128]{2,1,0:T(8,128)S(1)}) custom-call(bf16[512,1024]{1,0:T(8,128)(2,1)S(1)} %copy-done.5, bf16[512,512]{1,0:T(8,128)(2,1)S(1)} %copy-done.8, bf16[8,128,512]{2,1,0:T(8,128)(2,1)S(1)} %copy-done.6, s32[8,64,1]{2,1,0:T(8,128)S(1)} %copy-done.7), custom_call_target="tpu_custom_call" | custom-call | flops 536870912 | bytes 10000000 | tf_op jit(solution)/shard_map/prepare/pallas_call | solution.py:52
  85.2 2.2 %compact.1 = bf16[64,8,1152]{2,1,0:T(8,128)(2,1)S(1)} custom-call(s32[128]{0:T(128)S(1)} %get-tuple-element.44.source_ref, s32[128]{0:T(128)S(1)} %convert_element_type.10.slot_ref, bf16[128,8,1152]{2,1,0:T(8,128)(2,1)S(1)} %all-to-all-done.1.got_ref, f32[1,1]{1,0:T(1,128)S(6)} %add.120.after_ref), custom_call_target="tpu_custom_call" | custom-call | bytes 4000000 | tf_op jit(solution)/shard_map/compact/pallas_call | solution.py:143
  87.4 3.3 %collective-permute-start.6 = (bf16[512,1152]{1,0:T(8,128)(2,1)S(1)}, bf16[512,1152]{1,0:T(8,128)(2,1)S(1)}, u32[]{:S(2)}, u32[]{:S(2)}) collective-permute-start(bf16[512,1152]{1,0:T(8,128)(2,1)S(1)} %bitcast.16), channel_id=1, source_target_pairs={{0,1},{1,0},{2,3},{3,2},{4,5},{5,4},{6,7},{7,6},{8,9},{9,8},{10,11... | collective-permute-start | bytes 3538952 | tf_op jit(solution)/shard_map/ppermute | solution.py:414
  90.7 2.2 %copy.25 = bf16[512,576]{1,0:T(8,128)(2,1)} copy(bf16[512,576]{0,1:T(8,128)(2,1)} %param.18) | data formatting | bytes 1179648 | tf_op args[8]
  94.1 1.4 collective-permute-start.4
  95.5 1.8 %collective-permute-start.5 = (bf16[512,1152]{1,0:T(8,128)(2,1)S(1)}, bf16[512,1152]{1,0:T(8,128)(2,1)S(1)}, u32[]{:S(2)}, u32[]{:S(2)}) collective-permute-start(bf16[512,1152]{1,0:T(8,128)(2,1)S(1)} %bitcast.18), channel_id=1, source_target_pairs={{0,6},{1,7},{2,0},{3,1},{4,2},{5,3},{6,4},{7,5},{8,14},{9,15},{10,... | collective-permute-start | bytes 3538952 | tf_op jit(solution)/shard_map/ppermute | solution.py:413
  98.5 16.2 %first.1 = (f32[8,512,128]{2,1,0:T(8,128)S(1)}, f32[8,512,128]{2,1,0:T(8,128)}, f32[8,512,512]{2,1,0:T(8,128)}) custom-call(s32[8]{0:T(128)S(1)} %copy-done.9, s32[8]{0:T(128)S(1)} %stack.44.shares_ref, bf16[8,512,768]{2,1,0:T(8,128)(2,1)} %get-tuple-element.23.q_ref, bf16[384,640]{1,0:T(8,128)(2,1)S(1)} %pad.8.refs_0_, bf16[512,640]{1,0:T(8,128)(2,1)S(1)} %pad.9.refs_1_, ...), custom_call_target="tpu_custom_call" | custom-call | flops 6845104128 | bytes 16777216 | tf_op jit(solution)/shard_map/first/pallas_call | solution.py:334
  114.6 8.8 %collective-permute-done.4.refs_3_ = bf16[512,1152]{1,0:T(8,128)(2,1)S(1)} collective-permute-done((bf16[512,1152]{1,0:T(8,128)(2,1)S(1)}, bf16[512,1152]{1,0:T(8,128)(2,1)S(1)}, u32[]{:S(2)}, u32[]{:S(2)}) %collective-permute-start.4) | collective-permute-done | bytes 1179680 | tf_op jit(solution)/shard_map/ppermute | solution.py:412
  125.5 1.7 %collective-permute-start.8 = (bf16[256,1152]{1,0:T(8,128)(2,1)S(1)}, bf16[256,1152]{1,0:T(8,128)(2,1)S(1)}, u32[]{:S(2)}, u32[]{:S(2)}) collective-permute-start(bf16[256,1152]{1,0:T(8,128)(2,1)S(1)} %slice.17), channel_id=1, source_target_pairs={{0,6},{1,7},{2,0},{3,1},{4,2},{5,3},{6,4},{7,5},{8,14},{9,15},{10,... | collective-permute-start | bytes 1769480 | tf_op jit(solution)/shard_map/ppermute | solution.py:421
  128.3 16.0 %second.1 = (f32[8,512,128]{2,1,0:T(8,128)}, f32[8,512,128]{2,1,0:T(8,128)}, f32[8,512,512]{2,1,0:T(8,128)}) custom-call(s32[8]{0:T(128)S(1)} %copy-done.9, s32[8]{0:T(128)S(1)} %stack.44.shares_ref, bf16[8,512,768]{2,1,0:T(8,128)(2,1)} %get-tuple-element.23.q_ref, f32[8,512,128]{2,1,0:T(8,128)} %copy-done.2, f32[8,512,128]{2,1,0:T(8,128)} %get-tuple-element.31.refs_1_, ...), custom_call_target="tpu_custom_call" | custom-call | flops 4563402752 | bytes 16777216 | tf_op jit(solution)/shard_map/second/pallas_call | solution.py:334
  144.9 1.5 collective-permute-done.11.refs_5_
  147.3 1.6 copy-done.3
  148.9 13.9 %third.1 = bf16[512,1024]{1,0:T(8,128)(2,1)} custom-call(s32[8]{0:T(128)S(1)} %copy-done.9, s32[8]{0:T(128)S(1)} %stack.44.shares_ref, bf16[8,512,768]{2,1,0:T(8,128)(2,1)} %get-tuple-element.23.q_ref, f32[8,512,128]{2,1,0:T(8,128)S(1)} %copy-done.3, f32[8,512,128]{2,1,0:T(8,128)} %get-tuple-element.37.refs_1_, f32[8,512,512]{2,1,0:T(8,128)} %get-tuple-element.38.refs_2_, ...), custom_call_target="tpu_custom_call" | custom-call | flops 2281701376 | bytes 16777216 | tf_op jit(solution)/shard_map/third/pallas_call | solution.py:334
  (78 shorter events, 17.5 us)
Async XLA Ops:
  20.0 48.5 %copy-start.20 = (s32[8,64]{1,0:T(8,128)S(1)}, s32[8,64]{1,0:T(8,128)}, u32[]{:S(2)}) copy-start(s32[8,64]{1,0:T(8,128)} %param.19) | copy-start | bytes 6148
  20.0 49.4 %copy-start.5 = (bf16[512,1024]{1,0:T(8,128)(2,1)S(1)}, bf16[512,1024]{1,0:T(8,128)(2,1)}, u32[]{:S(2)}) copy-start(bf16[512,1024]{1,0:T(8,128)(2,1)} %rows_ref.1) | copy-start | bytes 3145732
  20.0 65.2 %all-to-all-start.1 = ((bf16[128,8,1152]{2,1,0:T(8,128)(2,1)}), bf16[128,8,1152]{2,1,0:T(8,128)(2,1)S(1)}, u32[]{:S(2)}, u32[]{:S(2)}) async-start(bf16[128,8,1152]{2,1,0:T(8,128)(2,1)} %copy-done), calls=%async_computation.1 | async-start | bytes 4718592 | tf_op jit(solution)/shard_map/all_to_all | solution.py:400
  28.2 15.8 %collective-permute-start = (bf16[24,576]{1,0:T(8,128)(2,1)S(1)}, bf16[24,576]{1,0:T(8,128)(2,1)S(1)}, u32[]{:S(2)}, u32[]{:S(2)}) collective-permute-start(bf16[24,576]{1,0:T(8,128)(2,1)S(1)} %copy-done.16), channel_id=1, source_target_pairs={{0,8},{8,0},{16,24},{24,16},{32,40},{40,32},{48,56},{56,48},{64,72... | collective-permute-start | bytes 82952 | tf_op jit(solution)/shard_map/ppermute | solution.py:394
  44.0 41.1 %copy-start.18 = (bf16[24,576]{1,0:T(8,128)(2,1)}, bf16[24,576]{1,0:T(8,128)(2,1)S(1)}, u32[]{:S(2)}) copy-start(bf16[24,576]{1,0:T(8,128)(2,1)S(1)} %collective-permute-done) | copy-start | bytes 82948
  44.1 15.9 %collective-permute-start.1 = (bf16[48,576]{1,0:T(8,128)(2,1)S(1)}, bf16[48,576]{1,0:T(8,128)(2,1)S(1)}, u32[]{:S(2)}, u32[]{:S(2)}) collective-permute-start(bf16[48,576]{1,0:T(8,128)(2,1)S(1)} %pad_maximum_fusion.2), channel_id=1, source_target_pairs={{0,16},{8,24},{16,0},{24,8},{32,48},{40,56},{48,32},{56,40},{64,80... | collective-permute-start | bytes 165896 | tf_op jit(solution)/shard_map/ppermute | solution.py:394
  60.0 25.2 %copy-start.12 = (bf16[48,576]{1,0:T(8,128)(2,1)}, bf16[48,576]{1,0:T(8,128)(2,1)S(1)}, u32[]{:S(2)}) copy-start(bf16[48,576]{1,0:T(8,128)(2,1)S(1)} %collective-permute-done.1) | copy-start | bytes 165892
  60.0 3.8 %collective-permute-start.2 = (bf16[96,576]{1,0:T(8,128)(2,1)S(1)}, bf16[96,576]{1,0:T(8,128)(2,1)S(1)}, u32[]{:S(2)}, u32[]{:S(2)}) collective-permute-start(bf16[96,576]{1,0:T(8,128)(2,1)S(1)} %pad_maximum_fusion.1), channel_id=1, source_target_pairs={{0,32},{8,40},{16,48},{24,56},{32,0},{40,8},{48,16},{56,24},{64,96... | collective-permute-start | bytes 331784 | tf_op jit(solution)/shard_map/ppermute | solution.py:394
  65.2 17.6 %collective-permute-start.3 = (bf16[192,576]{1,0:T(8,128)(2,1)}, bf16[192,576]{1,0:T(8,128)(2,1)}, u32[]{:S(2)}, u32[]{:S(2)}) collective-permute-start(bf16[192,576]{1,0:T(8,128)(2,1)} %pad_maximum_fusion), channel_id=1, source_target_pairs={{0,64},{8,72},{16,80},{24,88},{32,96},{40,104},{48,112},{56,120},{... | collective-permute-start | bytes 663560 | tf_op jit(solution)/shard_map/ppermute | solution.py:394
  87.4 9.9 %copy-start.17 = (bf16[24,576]{1,0:T(8,128)(2,1)S(1)}, bf16[24,576]{1,0:T(8,128)(2,1)}, u32[]{:S(2)}) copy-start(bf16[24,576]{1,0:T(8,128)(2,1)} %param.17) | copy-start | bytes 82948
  87.4 9.9 %copy-start.19 = (bf16[24,576]{1,0:T(8,128)(2,1)S(1)}, bf16[24,576]{1,0:T(8,128)(2,1)}, u32[]{:S(2)}) copy-start(bf16[24,576]{1,0:T(8,128)(2,1)} %copy-done.18) | copy-start | bytes 82948
  87.4 10.0 %copy-start.13 = (bf16[48,576]{1,0:T(8,128)(2,1)S(1)}, bf16[48,576]{1,0:T(8,128)(2,1)}, u32[]{:S(2)}) copy-start(bf16[48,576]{1,0:T(8,128)(2,1)} %copy-done.12) | copy-start | bytes 165892
  87.4 10.0 %copy-start.15 = (bf16[96,576]{1,0:T(8,128)(2,1)S(1)}, bf16[96,576]{1,0:T(8,128)(2,1)}, u32[]{:S(2)}) copy-start(bf16[96,576]{1,0:T(8,128)(2,1)} %copy-done.14) | copy-start | bytes 331780
  87.4 11.0 %collective-permute-start.6 = (bf16[512,1152]{1,0:T(8,128)(2,1)S(1)}, bf16[512,1152]{1,0:T(8,128)(2,1)S(1)}, u32[]{:S(2)}, u32[]{:S(2)}) collective-permute-start(bf16[512,1152]{1,0:T(8,128)(2,1)S(1)} %bitcast.16), channel_id=1, source_target_pairs={{0,1},{1,0},{2,3},{3,2},{4,5},{5,4},{6,7},{7,6},{8,9},{9,8},{10,11... | collective-permute-start | bytes 3538952 | tf_op jit(solution)/shard_map/ppermute | solution.py:414
  94.1 29.3 %collective-permute-start.4 = (bf16[512,1152]{1,0:T(8,128)(2,1)S(1)}, bf16[512,1152]{1,0:T(8,128)(2,1)S(1)}, u32[]{:S(2)}, u32[]{:S(2)}) collective-permute-start(bf16[512,1152]{1,0:T(8,128)(2,1)S(1)} %bitcast.17), channel_id=1, source_target_pairs={{0,2},{1,3},{2,4},{3,5},{4,6},{5,7},{6,0},{7,1},{8,10},{9,11},{10,... | collective-permute-start | bytes 3538952 | tf_op jit(solution)/shard_map/ppermute | solution.py:412
  95.5 28.0 %collective-permute-start.5 = (bf16[512,1152]{1,0:T(8,128)(2,1)S(1)}, bf16[512,1152]{1,0:T(8,128)(2,1)S(1)}, u32[]{:S(2)}, u32[]{:S(2)}) collective-permute-start(bf16[512,1152]{1,0:T(8,128)(2,1)S(1)} %bitcast.18), channel_id=1, source_target_pairs={{0,6},{1,7},{2,0},{3,1},{4,2},{5,3},{6,4},{7,5},{8,14},{9,15},{10,... | collective-permute-start | bytes 3538952 | tf_op jit(solution)/shard_map/ppermute | solution.py:413
  114.6 13.7 %copy-start.2 = (f32[8,512,128]{2,1,0:T(8,128)}, f32[8,512,128]{2,1,0:T(8,128)S(1)}, u32[]{:S(2)}) copy-start(f32[8,512,128]{2,1,0:T(8,128)S(1)} %get-tuple-element.30.refs_0_) | copy-start | bytes 6291460
  123.4 3.7 %collective-permute-start.10 = (bf16[512,1152]{1,0:T(8,128)(2,1)S(1)}, bf16[512,1152]{1,0:T(8,128)(2,1)S(1)}, u32[]{:S(2)}, u32[]{:S(2)}) collective-permute-start(bf16[512,1152]{1,0:T(8,128)(2,1)S(1)} %collective-permute-done.5.refs_4_), channel_id=1, source_target_pairs={{0,1},{1,0},{2,3},{3,2},{4,5},{5,4},{6,7},{7,6},{8,9},{9,8},{10,11... | collective-permute-start | bytes 3538952 | tf_op jit(solution)/shard_map/ppermute | solution.py:423
  124.1 4.2 %collective-permute-start.9 = (bf16[512,1152]{1,0:T(8,128)(2,1)S(1)}, bf16[512,1152]{1,0:T(8,128)(2,1)S(1)}, u32[]{:S(2)}, u32[]{:S(2)}) collective-permute-start(bf16[512,1152]{1,0:T(8,128)(2,1)S(1)} %collective-permute-done.4.refs_3_), channel_id=1, source_target_pairs={{0,1},{1,0},{2,3},{3,2},{4,5},{5,4},{6,7},{7,6},{8,9},{9,8},{10,11... | collective-permute-start | bytes 3538952 | tf_op jit(solution)/shard_map/ppermute | solution.py:422
  124.3 23.0 %copy-start.4 = (bf16[8,512,128]{2,1,0:T(8,128)(2,1)S(1)}, bf16[8,512,128]{2,1,0:T(8,128)(2,1)}, u32[]{:S(2)}) copy-start(bf16[8,512,128]{2,1,0:T(8,128)(2,1)} %refs_7_.1) | copy-start | bytes 3145732
  124.3 20.1 %collective-permute-start.7 = (bf16[256,1152]{1,0:T(8,128)(2,1)S(1)}, bf16[256,1152]{1,0:T(8,128)(2,1)S(1)}, u32[]{:S(2)}, u32[]{:S(2)}) collective-permute-start(bf16[256,1152]{1,0:T(8,128)(2,1)S(1)} %slice.16), channel_id=1, source_target_pairs={{0,2},{1,3},{2,4},{3,5},{4,6},{5,7},{6,0},{7,1},{8,10},{9,11},{10,... | collective-permute-start | bytes 1769480 | tf_op jit(solution)/shard_map/ppermute | solution.py:420
  125.5 18.8 %collective-permute-start.8 = (bf16[256,1152]{1,0:T(8,128)(2,1)S(1)}, bf16[256,1152]{1,0:T(8,128)(2,1)S(1)}, u32[]{:S(2)}, u32[]{:S(2)}) collective-permute-start(bf16[256,1152]{1,0:T(8,128)(2,1)S(1)} %slice.17), channel_id=1, source_target_pairs={{0,6},{1,7},{2,0},{3,1},{4,2},{5,3},{6,4},{7,5},{8,14},{9,15},{10,... | collective-permute-start | bytes 1769480 | tf_op jit(solution)/shard_map/ppermute | solution.py:421
  144.3 2.1 %collective-permute-start.11 = (bf16[256,1152]{1,0:T(8,128)(2,1)S(1)}, bf16[256,1152]{1,0:T(8,128)(2,1)S(1)}, u32[]{:S(2)}, u32[]{:S(2)}) collective-permute-start(bf16[256,1152]{1,0:T(8,128)(2,1)S(1)} %collective-permute-done.7.refs_3_), channel_id=1, source_target_pairs={{0,1},{1,0},{2,3},{3,2},{4,5},{5,4},{6,7},{7,6},{8,9},{9,8},{10,11... | collective-permute-start | bytes 1769480 | tf_op jit(solution)/shard_map/ppermute | solution.py:436
  144.8 2.5 %collective-permute-start.12 = (bf16[256,1152]{1,0:T(8,128)(2,1)S(1)}, bf16[256,1152]{1,0:T(8,128)(2,1)S(1)}, u32[]{:S(2)}, u32[]{:S(2)}) collective-permute-start(bf16[256,1152]{1,0:T(8,128)(2,1)S(1)} %collective-permute-done.8.refs_4_), channel_id=1, source_target_pairs={{0,1},{1,0},{2,3},{3,2},{4,5},{5,4},{6,7},{7,6},{8,9},{9,8},{10,11... | collective-permute-start | bytes 1769480 | tf_op jit(solution)/shard_map/ppermute | solution.py:437
  (11 other events, 33.2 us)

commit v3 on v2

--- a/solution.py
+++ b/solution.py
@@ -10,7 +10,7 @@
 
 F32 = jnp.float32
 BF16 = jnp.bfloat16
-VMEM_LIMIT = 48 * 1024 * 1024
+VMEM_LIMIT = 24 * 1024 * 1024
 
 
 def nt_dot(a, b):
@@ -173,7 +173,8 @@
         out_ref, keys_ref, mixed_ref = refs
     else:
         top_out, total_out, sum_out, keys_ref = refs
-    heads, size, wide = q_ref.shape
+    heads, total_rows, wide = q_ref.shape
+    size = total_rows // lengths_ref.shape[0]
     latent = wide - 256
     part = pieces[0][0].shape[0] // 2
     section = len(picks) * part
@@ -228,7 +229,8 @@
         for step in range(heads // some):
             which = slice(step * some, (step + 1) * some)
             rows = slice(step * block, (step + 1) * block)
-            q = q_ref[which].reshape(block, wide)
+            q = q_ref[which, pl.ds(pl.multiple_of(request * size, size), size), :]
+            q = q.reshape(block, wide)
             scores = nt_dot(q, keys_ref[origin : origin + count, :]) + bias
             if shared:
                 first = nt_dot(q, keys_ref[:prompt, :])
@@ -236,7 +238,7 @@
                 scores = jnp.concatenate([first, tree, scores], axis=1)
             top = jnp.broadcast_to(jnp.max(scores, axis=1, keepdims=True), (block, 128))
             if not shared:
-                before = taken[0][0, rows, :]
+                before = taken[0][request, rows, :]
                 top = jnp.maximum(top, before)
                 fade = jnp.exp2((before - top) * factor)
             weights = jnp.exp2((scores - spread(top, scores.shape[1])) * factor)
@@ -247,17 +249,17 @@
                 preferred_element_type=F32,
             )
             if not shared:
-                total = total + taken[1][0, rows, :] * fade
-                mixed = mixed + taken[2][0, rows, :] * spread(fade, latent)
+                total = total + taken[1][request, rows, :] * fade
+                mixed = mixed + taken[2][request, rows, :].astype(F32) * spread(fade, latent)
             if finish:
                 mixed = mixed * spread(1.0 / total, latent)
                 mixed_ref[which, pl.ds(pl.multiple_of(request * size, size), size), :] = (
                     mixed.astype(BF16).reshape(some, size, latent)
                 )
             else:
-                top_out[0, rows, :] = top
-                total_out[0, rows, :] = total
-                sum_out[0, rows, :] = mixed
+                top_out[request, rows, :] = top
+                total_out[request, rows, :] = total
+                sum_out[request, rows, :] = mixed.astype(BF16)
 
     needed = pl.cdiv(length, 256)
     steps = (1, 2, 3, 4) if section % 128 == 0 else (2, 4)
@@ -293,12 +295,9 @@
     origin = given[0].shape[0] + 2 * size if shared else 0
     count = origin + 2 * per * len(pieces)
 
-    state_specs = [
-        pl.BlockSpec((1, rows, 128), lambda i, *_: (i, 0, 0)),
-        pl.BlockSpec((1, rows, 128), lambda i, *_: (i, 0, 0)),
-        pl.BlockSpec((1, rows, latent), lambda i, *_: (i, 0, 0)),
-    ]
-    in_specs = [pl.BlockSpec((heads, size, wide), lambda i, *_: (0, i, 0))]
+    whole = pl.BlockSpec(memory_space=pltpu.VMEM)
+    state_specs = [whole, whole, whole]
+    in_specs = [whole]
     if shared:
         in_specs += [
             pl.BlockSpec(given[0].shape, lambda i, *_: (0, 0)),
@@ -320,7 +319,7 @@
     if finish:
         value = up_values.shape[2]
         operands.append(up_values)
-        in_specs.append(pl.BlockSpec(up_values.shape, lambda i, *_: (0, 0, 0)))
+        in_specs.append(whole)
         out_specs = pl.BlockSpec((total_rows, heads * value), lambda i, *_: (0, 0))
         out_shape = jax.ShapeDtypeStruct((total_rows, heads * value), BF16)
         scratch.append(pltpu.VMEM((heads, total_rows, latent), BF16))
@@ -329,7 +328,7 @@
         out_shape = [
             jax.ShapeDtypeStruct((requests, rows, 128), F32),
             jax.ShapeDtypeStruct((requests, rows, 128), F32),
-            jax.ShapeDtypeStruct((requests, rows, latent), F32),
+            jax.ShapeDtypeStruct((requests, rows, latent), BF16),
         ]
     return pl.pallas_call(
         functools.partial(attend_kernel, scale, picks, shared, halves, finish),
@@ -341,6 +340,7 @@
             scratch_shapes=scratch,
         ),
         out_shape=out_shape,
+        input_output_aliases={} if shared or finish else {3: 0, 4: 1, 5: 2},
         cost_estimate=pl.CostEstimate(
             flops=2 * requests * rows * count * (2 * latent + 64),
             bytes_accessed=requests * rows * latent * 8,
@@ -382,24 +382,29 @@
     first = jnp.min(jnp.where(match, code[None, :], entries * pool_local), axis=1)
     last = jnp.max(jnp.where(match, code[None, :], 0), axis=1)
     asks = jnp.stack([first, last], axis=1) % pool_local
-    wanted = lax.all_to_all(asks, "decode", split_axis=0, concat_axis=0, tiled=True)
+    prompt = prefix_latent.reshape(-1, 128)
+    held = prompt.shape[0]
+    message = jnp.concatenate(
+        [
+            jnp.broadcast_to(prompt[None], (groups,) + prompt.shape),
+            jnp.pad(asks.astype(BF16)[:, None, :], ((0, 0), (0, 3), (0, 126))),
+        ],
+        axis=1,
+    )
+    message = lax.all_to_all(message, "decode", split_axis=0, concat_axis=0, tiled=True)
+    wanted = message[:, held, :2].astype(jnp.int32)
+    prefix = message[:, :held].reshape(-1, width)
     earlier = (order[None, :] < order[:, None]) & (owner_of[None, :] == owner_of[:, None])
     slot_of = jnp.any(earlier, axis=1).astype(jnp.int32)
 
     wide = latent_dim + 2 * rope_dim
-    prefix = prefix_latent
-    step = 1
-    while step < groups:
-        pairs = [(i, i ^ step) for i in range(groups)]
-        prefix = jnp.concatenate([prefix, lax.ppermute(prefix, "decode", pairs)], axis=0)
-        step *= 2
-    prefix = jnp.pad(prefix, ((0, 0), (0, wide - width)))
     tree = jnp.pad(tree_latent, ((0, 0), (0, wide - width)))
 
     packed = pack(wanted, page_pool, shares)
     got = lax.all_to_all(packed, ("decode", "pool"), split_axis=0, concat_axis=0, tiled=True)
     q, hidden = prepare(q_nope, q_rope, up_keys, parents)
-    after = hidden[0, :1, :1] + prefix[-1:, :1].astype(F32)
+    prefix = jnp.pad(prefix, ((0, 0), (0, wide - width)))
+    after = hidden[0, :1, :1] + (prefix[:1, :1] + tree[:1, :1]).astype(F32)
     own = compact(owner_of, slot_of, got, after).reshape(-1, 2 * width)
 
     swap = [(i, i ^ 1) for i in range(shares)]

time: 164 us -> 131 us (0.80)
  starting transfers between devices: 34.9 us -> 17.6 us
  waiting for transfers between devices: 35.2 us -> 19.2 us
  Pallas kernels: 58.9 us -> 46.5 us
  local copies, waits for them, and re-layouts: 17.4 us -> 27.3 us
  blocking collectives: 13.8 us -> 16.9 us
    ppermute x4 -> x0, waiting for transfers between devices: 22.9 us -> none  [local(): lax.ppermute(prefix, 'decode', pairs)]
    ppermute x4 -> x0, starting transfers between devices: 15.9 us -> none  [local(): lax.ppermute(prefix, 'decode', pairs)]
    pallas_call x3, Pallas kernels: 46.1 us -> 34.6 us  [attend(): pl.pallas_call(functools.partial(attend_kernel, scale, picks, shared, hal...]
    all_to_all x1, waiting for transfers between devices: 0.01 us -> 10.2 us  [local(): lax.all_to_all(packed, ('decode', 'pool'), split_axis=0, concat_axis=0, t...]
    unnamed x47 -> x35, local copies, waits for them, and re-layouts: 11.6 us -> 17.6 us
    ppermute x1, waiting for transfers between devices: 8.81 us -> 3.16 us  [local(): below = lax.ppermute(own, 'pool', up)]
    all_to_all x1, blocking collectives: 13.8 us -> 16.9 us  [local(): lax.all_to_all(message, 'decode', split_axis=0, concat_axis=0, tiled=True)]
    ppermute x1, waiting for transfers between devices: 0.01 us -> 2.17 us  [local(): far_up = lax.ppermute(below[:middle], 'pool', up)]
  transfers between devices with their start and end apart: 14 -> 10, of which waited for: 7 -> 6; matrix products, arithmetic and copies ran while one was open for 5% -> 8% of each run, Pallas kernels for 25% -> 25%
where the time goes in v3:
time: 131 us; the launch traced here: 130 us
  Pallas kernels  46.5 us (35%)
  local copies, waits for them, and re-layouts  27.3 us (21%)
  waiting for transfers between devices  19.2 us (15%)
  starting transfers between devices  17.6 us (13%)
  blocking collectives  16.9 us (13%)
  between operations  2 us (2%)
    pallas_call x3, Pallas kernels, attend(): pl.pallas_call(functools.partial(attend_kernel, scale, picks, shared, hal...  34.6 us
    unnamed x35, local copies, waits for them, and re-layouts  17.6 us
    all_to_all x1, blocking collectives, local(): lax.all_to_all(message, 'decode', split_axis=0, concat_axis=0, tiled=True)  16.9 us
    all_to_all x1, waiting for transfers between devices, local(): lax.all_to_all(packed, ('decode', 'pool'), split_axis=0, concat_axis=0, t...  10.2 us
    all_to_all x1, starting transfers between devices, local(): lax.all_to_all(packed, ('decode', 'pool'), split_axis=0, concat_axis=0, t...  8.64 us
    pallas_call x1, Pallas kernels, prepare(): pl.pallas_call(prepare_kernel, grid=(heads,), in_specs=[pl.BlockSpec((row...  7.78 us
    ppermute x1, waiting for transfers between devices, local(): below = lax.ppermute(own, 'pool', up)  3.16 us
    ppermute x1, starting transfers between devices, local(): far_down = lax.ppermute(above[middle:], 'pool', down)  2.74 us
  transfers between devices with their start and end apart: 10, of which 6 were waited for; matrix products, arithmetic and copies ran while one was open for 8% of the time, Pallas kernels for 25%

profile of v3, /device:TPU:1, one launch (start us, length us, event | category | flops | bytes accessed | tf_op | source)
XLA Modules:
  0.0 130.1 jit_solution(15338318189341201996)
XLA Ops:
  2.1 16.9 %all_to_all.10 = bf16[16,112,128]{2,1,0:T(8,128)(2,1)S(1)} all-to-all(bf16[16,112,128]{2,1,0:T(8,128)(2,1)S(1)} %fusion.1), channel_id=1, replica_groups=mesh['decode'=16,'pool'=8] {'decode'}, dimensions={0} | all-to-all | bytes 917504 | tf_op jit(solution)/shard_map/all_to_all | solution.py:394
  19.9 1.7 %copy-done.3 = bf16[32,64,576]{2,1,0:T(8,128)(2,1)S(1)} copy-done((bf16[32,64,576]{2,1,0:T(8,128)(2,1)S(1)}, bf16[32,64,576]{2,1,0:T(8,128)(2,1)}, u32[]{:S(2)}) %copy-start.3) | copy-done | bytes 2359320
  21.7 2.0 %pack.1 = bf16[128,8,1152]{2,1,0:T(8,128)(2,1)S(1)} custom-call(s32[16,2]{1,0:T(8,128)S(1)} %copy.38.wanted_ref, bf16[256,8,576]{2,1,0:T(8,128)(2,1)S(1)} %bitcast.18), custom_call_target="tpu_custom_call" | custom-call | bytes 5000000 | tf_op jit(solution)/shard_map/pack/pallas_call | solution.py:101
  23.6 1.5 %copy-done.2 = bf16[128,8,1152]{2,1,0:T(8,128)(2,1)} copy-done((bf16[128,8,1152]{2,1,0:T(8,128)(2,1)}, bf16[128,8,1152]{2,1,0:T(8,128)(2,1)S(1)}, u32[]{:S(2)}) %copy-start.2) | copy-done | bytes 2359320
  25.1 8.6 %all-to-all-start.1 = ((bf16[128,8,1152]{2,1,0:T(8,128)(2,1)}), bf16[128,8,1152]{2,1,0:T(8,128)(2,1)S(1)}, u32[]{:S(2)}, u32[]{:S(2)}) async-start(bf16[128,8,1152]{2,1,0:T(8,128)(2,1)} %copy-done.2), calls=%async_computation.1 | async-start | bytes 4718592 | tf_op jit(solution)/shard_map/all_to_all | solution.py:404
  33.8 2.1 %copy.39 = bf16[512,576]{1,0:T(8,128)(2,1)} copy(bf16[512,576]{0,1:T(8,128)(2,1)} %param.18) | data formatting | bytes 1179648 | tf_op args[8]
  35.9 1.2 slice.33
  41.2 7.8 %prepare.1 = (bf16[8,512,768]{2,1,0:T(8,128)(2,1)S(1)}, f32[8,64,128]{2,1,0:T(8,128)S(1)}) custom-call(bf16[512,1024]{1,0:T(8,128)(2,1)S(1)} %copy-done.5, bf16[512,512]{1,0:T(8,128)(2,1)S(1)} %copy-done.9, bf16[8,128,512]{2,1,0:T(8,128)(2,1)S(1)} %copy-done.6, s32[8,64,1]{2,1,0:T(8,128)S(1)} %copy-done.7), custom_call_target="tpu_custom_call" | custom-call | flops 536870912 | bytes 10000000 | tf_op jit(solution)/shard_map/prepare/pallas_call | solution.py:52
  49.0 2.6 %copy-done = bf16[8,512,768]{2,1,0:T(8,128)(2,1)} copy-done((bf16[8,512,768]{2,1,0:T(8,128)(2,1)}, bf16[8,512,768]{2,1,0:T(8,128)(2,1)S(1)}, u32[]{:S(2)}) %copy-start) | copy-done | bytes 6291480
  53.0 1.4 %reshape.216 = bf16[384,576]{1,0:T(8,128)(2,1)S(1)} reshape(bf16[16,108,128]{2,1,0:T(8,128)(2,1)} %bitcast.23) | data formatting | bytes 884736 | tf_op jit(solution)/shard_map/reshape | solution.py:396
  56.9 10.2 %all-to-all-done.1.got_ref = bf16[128,8,1152]{2,1,0:T(8,128)(2,1)S(1)} async-done(((bf16[128,8,1152]{2,1,0:T(8,128)(2,1)}), bf16[128,8,1152]{2,1,0:T(8,128)(2,1)S(1)}, u32[]{:S(2)}, u32[]{:S(2)}) %all-to-all-start.1) | async-done | bytes 2359328 | tf_op jit(solution)/shard_map/all_to_all | solution.py:404
  67.1 2.2 %compact.1 = bf16[64,8,1152]{2,1,0:T(8,128)(2,1)S(1)} custom-call(s32[128]{0:T(128)S(1)} %get-tuple-element.44.source_ref, s32[128]{0:T(128)S(1)} %convert_element_type.27.slot_ref, bf16[128,8,1152]{2,1,0:T(8,128)(2,1)S(1)} %all-to-all-done.1.got_ref, f32[1,1]{1,0:T(1,128)S(6)} %add.126.after_ref), custom_call_target="tpu_custom_call" | custom-call | bytes 4000000 | tf_op jit(solution)/shard_map/compact/pallas_call | solution.py:143
  69.2 1.2 collective-permute-start.2
  70.5 2.7 %collective-permute-start.1 = (bf16[512,1152]{1,0:T(8,128)(2,1)S(1)}, bf16[512,1152]{1,0:T(8,128)(2,1)S(1)}, u32[]{:S(2)}, u32[]{:S(2)}) collective-permute-start(bf16[512,1152]{1,0:T(8,128)(2,1)S(1)} %bitcast.21), channel_id=1, source_target_pairs={{0,6},{1,7},{2,0},{3,1},{4,2},{5,3},{6,4},{7,5},{8,14},{9,15},{10,... | collective-permute-start | bytes 3538952 | tf_op jit(solution)/shard_map/ppermute | solution.py:418
  73.2 2.0 %pad.14.refs_1_ = bf16[512,640]{1,0:T(8,128)(2,1)} pad(bf16[512,576]{1,0:T(8,128)(2,1)} %copy.39, bf16[]{:T(256)} %constant.107.clone.1), padding=0_0x0_64 | pad | bytes 1245186 | tf_op jit(solution)/shard_map/jit(_pad)/pad | solution.py:401
  76.4 2.8 %copy-done.1 = bf16[8,512,768]{2,1,0:T(8,128)(2,1)S(1)} copy-done((bf16[8,512,768]{2,1,0:T(8,128)(2,1)S(1)}, bf16[8,512,768]{2,1,0:T(8,128)(2,1)}, u32[]{:S(2)}) %copy-start.1) | copy-done | bytes 6291480
  81.2 14.8 %first.1 = (f32[8,512,128]{2,1,0:T(8,128)S(1)}, f32[8,512,128]{2,1,0:T(8,128)S(1)}, bf16[8,512,512]{2,1,0:T(8,128)(2,1)S(1)}) custom-call(s32[8]{0:T(128)S(1)} %copy-done.10, s32[8]{0:T(128)S(1)} %stack.44.shares_ref, bf16[8,512,768]{2,1,0:T(8,128)(2,1)S(1)} %copy-done.1, bf16[384,640]{1,0:T(8,128)(2,1)S(1)} %pad.13.refs_0_, bf16[512,640]{1,0:T(8,128)(2,1)S(1)} %copy-done.8, ...), custom_call_target="tpu_custom_call" | custom-call | flops 6845104128 | bytes 16777216 | tf_op jit(solution)/shard_map/first/pallas_call | solution.py:333
  96.1 3.2 %collective-permute-done.refs_3_ = bf16[512,1152]{1,0:T(8,128)(2,1)S(1)} collective-permute-done((bf16[512,1152]{1,0:T(8,128)(2,1)S(1)}, bf16[512,1152]{1,0:T(8,128)(2,1)S(1)}, u32[]{:S(2)}, u32[]{:S(2)}) %collective-permute-start) | collective-permute-done | bytes 1179680 | tf_op jit(solution)/shard_map/ppermute | solution.py:417
  100.3 2.7 %collective-permute-start.4 = (bf16[256,1152]{1,0:T(8,128)(2,1)S(1)}, bf16[256,1152]{1,0:T(8,128)(2,1)S(1)}, u32[]{:S(2)}, u32[]{:S(2)}) collective-permute-start(bf16[256,1152]{1,0:T(8,128)(2,1)S(1)} %slice.29), channel_id=1, source_target_pairs={{0,6},{1,7},{2,0},{3,1},{4,2},{5,3},{6,4},{7,5},{8,14},{9,15},{10,... | collective-permute-start | bytes 1769480 | tf_op jit(solution)/shard_map/ppermute | solution.py:426
  104.3 9.4 %second.1 = (f32[8,512,128]{2,1,0:T(8,128)S(1)}, f32[8,512,128]{2,1,0:T(8,128)S(1)}, bf16[8,512,512]{2,1,0:T(8,128)(2,1)S(1)}) custom-call(s32[8]{0:T(128)S(1)} %copy-done.10, s32[8]{0:T(128)S(1)} %stack.44.shares_ref, bf16[8,512,768]{2,1,0:T(8,128)(2,1)S(1)} %copy-done.1, ...), custom_call_target="tpu_custom_call", output_to_operand_aliasing={{0}: (3, {}), {1}: (4, {}), {2}: (5, {})} | custom-call | flops 4563402752 | bytes 16777216 | tf_op jit(solution)/shard_map/second/pallas_call | solution.py:333
  113.7 2.2 %collective-permute-done.3.refs_3_ = bf16[256,1152]{1,0:T(8,128)(2,1)S(1)} collective-permute-done((bf16[256,1152]{1,0:T(8,128)(2,1)S(1)}, bf16[256,1152]{1,0:T(8,128)(2,1)S(1)}, u32[]{:S(2)}, u32[]{:S(2)}) %collective-permute-start.3) | collective-permute-done | bytes 589856 | tf_op jit(solution)/shard_map/ppermute | solution.py:425
  115.9 1.4 %collective-permute-start.7 = (bf16[256,1152]{1,0:T(8,128)(2,1)S(1)}, bf16[256,1152]{1,0:T(8,128)(2,1)S(1)}, u32[]{:S(2)}, u32[]{:S(2)}) collective-permute-start(bf16[256,1152]{1,0:T(8,128)(2,1)S(1)} %collective-permute-done.3.refs_3_), channel_id=1, source_target_pairs={{0,1},{1,0},{2,3},{3,2},{4,5},{5,4},{6,7},{7,6},{8,9},{9,8},{10,11... | collective-permute-start | bytes 1769480 | tf_op jit(solution)/shard_map/ppermute | solution.py:441
  117.3 1.6 %collective-permute-done.7.refs_5_ = bf16[256,1152]{1,0:T(8,128)(2,1)S(1)} collective-permute-done((bf16[256,1152]{1,0:T(8,128)(2,1)S(1)}, bf16[256,1152]{1,0:T(8,128)(2,1)S(1)}, u32[]{:S(2)}, u32[]{:S(2)}) %collective-permute-start.7) | collective-permute-done | bytes 589856 | tf_op jit(solution)/shard_map/ppermute | solution.py:441
  119.7 10.3 %third.1 = bf16[512,1024]{1,0:T(8,128)(2,1)} custom-call(s32[8]{0:T(128)S(1)} %copy-done.10, s32[8]{0:T(128)S(1)} %stack.44.shares_ref, bf16[8,512,768]{2,1,0:T(8,128)(2,1)S(1)} %copy-done.1, f32[8,512,128]{2,1,0:T(8,128)S(1)} %get-tuple-element.36.refs_0_, f32[8,512,128]{2,1,0:T(8,128)S(1)} %get-tuple-element.37.refs_1_, ...), custom_call_target="tpu_custom_call" | custom-call | flops 2281701376 | bytes 16777216 | tf_op jit(solution)/shard_map/third/pallas_call | solution.py:333
  (61 shorter events, 15.3 us)
Async XLA Ops:
  19.9 1.7 %copy-start.3 = (bf16[32,64,576]{2,1,0:T(8,128)(2,1)S(1)}, bf16[32,64,576]{2,1,0:T(8,128)(2,1)}, u32[]{:S(2)}) copy-start(bf16[32,64,576]{2,1,0:T(8,128)(2,1)} %param.14) | copy-start | bytes 7077892
  23.6 1.5 %copy-start.2 = (bf16[128,8,1152]{2,1,0:T(8,128)(2,1)}, bf16[128,8,1152]{2,1,0:T(8,128)(2,1)S(1)}, u32[]{:S(2)}) copy-start(bf16[128,8,1152]{2,1,0:T(8,128)(2,1)S(1)} %pack.1) | copy-start | bytes 7077892
  25.1 12.0 %copy-start.15 = (s32[8,64]{1,0:T(8,128)S(1)}, s32[8,64]{1,0:T(8,128)}, u32[]{:S(2)}) copy-start(s32[8,64]{1,0:T(8,128)} %param.19) | copy-start | bytes 6148
  25.1 12.9 %copy-start.5 = (bf16[512,1024]{1,0:T(8,128)(2,1)S(1)}, bf16[512,1024]{1,0:T(8,128)(2,1)}, u32[]{:S(2)}) copy-start(bf16[512,1024]{1,0:T(8,128)(2,1)} %rows_ref.1) | copy-start | bytes 3145732
  25.1 42.0 %all-to-all-start.1 = ((bf16[128,8,1152]{2,1,0:T(8,128)(2,1)}), bf16[128,8,1152]{2,1,0:T(8,128)(2,1)S(1)}, u32[]{:S(2)}, u32[]{:S(2)}) async-start(bf16[128,8,1152]{2,1,0:T(8,128)(2,1)} %copy-done.2), calls=%async_computation.1 | async-start | bytes 4718592 | tf_op jit(solution)/shard_map/all_to_all | solution.py:404
  38.0 1.2 copy-start.6
  39.2 0.9 copy-start.7
  40.2 1.0 copy-start.9
  49.0 2.7 %copy-start = (bf16[8,512,768]{2,1,0:T(8,128)(2,1)}, bf16[8,512,768]{2,1,0:T(8,128)(2,1)S(1)}, u32[]{:S(2)}) copy-start(bf16[8,512,768]{2,1,0:T(8,128)(2,1)S(1)} %get-tuple-element.23.q_ref) | copy-start | bytes 18874372
  54.5 2.4 %copy-start.13 = (bf16[384,576]{1,0:T(8,128)(2,1)}, bf16[384,576]{1,0:T(8,128)(2,1)S(1)}, u32[]{:S(2)}) copy-start(bf16[384,576]{1,0:T(8,128)(2,1)S(1)} %reshape.216) | copy-start | bytes 1327108
  69.2 7.2 %copy-start.10 = (s32[8]{0:T(128)S(1)}, s32[8]{0:T(128)}, u32[]{:S(2)}) copy-start(s32[8]{0:T(128)} %lengths_ref.5) | copy-start | bytes 100
  69.2 7.1 %collective-permute-start.2 = (bf16[512,1152]{1,0:T(8,128)(2,1)S(1)}, bf16[512,1152]{1,0:T(8,128)(2,1)}, u32[]{:S(2)}, u32[]{:S(2)}) collective-permute-start(bf16[512,1152]{1,0:T(8,128)(2,1)S(1)} %bitcast.19), channel_id=1, source_target_pairs={{0,1},{1,0},{2,3},{3,2},{4,5},{5,4},{6,7},{7,6},{8,9},{9,8},{10,11... | collective-permute-start | bytes 3538952 | tf_op jit(solution)/shard_map/ppermute | solution.py:419
  70.5 28.7 %collective-permute-start = (bf16[512,1152]{1,0:T(8,128)(2,1)S(1)}, bf16[512,1152]{1,0:T(8,128)(2,1)S(1)}, u32[]{:S(2)}, u32[]{:S(2)}) collective-permute-start(bf16[512,1152]{1,0:T(8,128)(2,1)S(1)} %bitcast.20), channel_id=1, source_target_pairs={{0,2},{1,3},{2,4},{3,5},{4,6},{5,7},{6,0},{7,1},{8,10},{9,11},{10,... | collective-permute-start | bytes 3538952 | tf_op jit(solution)/shard_map/ppermute | solution.py:417
  70.5 28.7 %collective-permute-start.1 = (bf16[512,1152]{1,0:T(8,128)(2,1)S(1)}, bf16[512,1152]{1,0:T(8,128)(2,1)S(1)}, u32[]{:S(2)}, u32[]{:S(2)}) collective-permute-start(bf16[512,1152]{1,0:T(8,128)(2,1)S(1)} %bitcast.21), channel_id=1, source_target_pairs={{0,6},{1,7},{2,0},{3,1},{4,2},{5,3},{6,4},{7,5},{8,14},{9,15},{10,... | collective-permute-start | bytes 3538952 | tf_op jit(solution)/shard_map/ppermute | solution.py:418
  76.4 2.8 %copy-start.1 = (bf16[8,512,768]{2,1,0:T(8,128)(2,1)S(1)}, bf16[8,512,768]{2,1,0:T(8,128)(2,1)}, u32[]{:S(2)}) copy-start(bf16[8,512,768]{2,1,0:T(8,128)(2,1)} %copy-done) | copy-start | bytes 18874372
  79.2 1.1 copy-start.8
  80.3 0.9 copy-start.12
  99.2 3.8 %collective-permute-start.5 = (bf16[512,1152]{1,0:T(8,128)(2,1)S(1)}, bf16[512,1152]{1,0:T(8,128)(2,1)S(1)}, u32[]{:S(2)}, u32[]{:S(2)}) collective-permute-start(bf16[512,1152]{1,0:T(8,128)(2,1)S(1)} %collective-permute-done.refs_3_), channel_id=1, source_target_pairs={{0,1},{1,0},{2,3},{3,2},{4,5},{5,4},{6,7},{7,6},{8,9},{9,8},{10,11... | collective-permute-start | bytes 3538952 | tf_op jit(solution)/shard_map/ppermute | solution.py:427
  100.1 4.2 %collective-permute-start.6 = (bf16[512,1152]{1,0:T(8,128)(2,1)S(1)}, bf16[512,1152]{1,0:T(8,128)(2,1)S(1)}, u32[]{:S(2)}, u32[]{:S(2)}) collective-permute-start(bf16[512,1152]{1,0:T(8,128)(2,1)S(1)} %collective-permute-done.1.refs_4_), channel_id=1, source_target_pairs={{0,1},{1,0},{2,3},{3,2},{4,5},{5,4},{6,7},{7,6},{8,9},{9,8},{10,11... | collective-permute-start | bytes 3538952 | tf_op jit(solution)/shard_map/ppermute | solution.py:428
  100.2 19.5 %copy-start.4 = (bf16[8,512,128]{2,1,0:T(8,128)(2,1)S(1)}, bf16[8,512,128]{2,1,0:T(8,128)(2,1)}, u32[]{:S(2)}) copy-start(bf16[8,512,128]{2,1,0:T(8,128)(2,1)} %refs_7_.1) | copy-start | bytes 3145732
  100.2 15.7 %collective-permute-start.3 = (bf16[256,1152]{1,0:T(8,128)(2,1)S(1)}, bf16[256,1152]{1,0:T(8,128)(2,1)S(1)}, u32[]{:S(2)}, u32[]{:S(2)}) collective-permute-start(bf16[256,1152]{1,0:T(8,128)(2,1)S(1)} %slice.28), channel_id=1, source_target_pairs={{0,2},{1,3},{2,4},{3,5},{4,6},{5,7},{6,0},{7,1},{8,10},{9,11},{10,... | collective-permute-start | bytes 1769480 | tf_op jit(solution)/shard_map/ppermute | solution.py:425
  100.3 15.6 %collective-permute-start.4 = (bf16[256,1152]{1,0:T(8,128)(2,1)S(1)}, bf16[256,1152]{1,0:T(8,128)(2,1)S(1)}, u32[]{:S(2)}, u32[]{:S(2)}) collective-permute-start(bf16[256,1152]{1,0:T(8,128)(2,1)S(1)} %slice.29), channel_id=1, source_target_pairs={{0,6},{1,7},{2,0},{3,1},{4,2},{5,3},{6,4},{7,5},{8,14},{9,15},{10,... | collective-permute-start | bytes 1769480 | tf_op jit(solution)/shard_map/ppermute | solution.py:426
  115.9 3.0 %collective-permute-start.7 = (bf16[256,1152]{1,0:T(8,128)(2,1)S(1)}, bf16[256,1152]{1,0:T(8,128)(2,1)S(1)}, u32[]{:S(2)}, u32[]{:S(2)}) collective-permute-start(bf16[256,1152]{1,0:T(8,128)(2,1)S(1)} %collective-permute-done.3.refs_3_), channel_id=1, source_target_pairs={{0,1},{1,0},{2,3},{3,2},{4,5},{5,4},{6,7},{7,6},{8,9},{9,8},{10,11... | collective-permute-start | bytes 1769480 | tf_op jit(solution)/shard_map/ppermute | solution.py:441
  117.3 2.5 %collective-permute-start.8 = (bf16[256,1152]{1,0:T(8,128)(2,1)S(1)}, bf16[256,1152]{1,0:T(8,128)(2,1)S(1)}, u32[]{:S(2)}, u32[]{:S(2)}) collective-permute-start(bf16[256,1152]{1,0:T(8,128)(2,1)S(1)} %collective-permute-done.4.refs_4_), channel_id=1, source_target_pairs={{0,1},{1,0},{2,3},{3,2},{4,5},{5,4},{6,7},{7,6},{8,9},{9,8},{10,11... | collective-permute-start | bytes 1769480 | tf_op jit(solution)/shard_map/ppermute | solution.py:442
  (2 other events, 1.5 us)

commit v4 on v3

--- a/solution.py
+++ b/solution.py
@@ -75,41 +75,39 @@
 
 
 def pack_kernel(wanted_ref, pool_ref, out_ref):
-    groups = wanted_ref.shape[0]
-    shares = out_ref.shape[0] // groups
+    size = pool_ref.shape[1]
+    some = out_ref.shape[0] // size
     latent = 512
-    rope = pool_ref.shape[2] - latent
-
-    def body(group, carry):
-        first = pool_ref.at[pl.ds(wanted_ref[group, 0] * shares, shares)]
-        second = pool_ref.at[pl.ds(wanted_ref[group, 1] * shares, shares)]
-        out = out_ref.at[pl.ds(group * shares, shares)]
-        out[:, :, :latent] = first[:, :, :latent]
-        out[:, :, latent : 2 * latent] = second[:, :, :latent]
-        out[:, :, 2 * latent :] = jnp.concatenate(
-            [first[:, :, latent:], second[:, :, latent:]], axis=2
+    for index in range(some):
+        group = pl.program_id(0) * some + index
+        first = pool_ref.at[wanted_ref[group, 0]]
+        second = pool_ref.at[wanted_ref[group, 1]]
+        rows = slice(index * size, (index + 1) * size)
+        out_ref[rows, :latent] = first[:, :latent]
+        out_ref[rows, latent : 2 * latent] = second[:, :latent]
+        out_ref[rows, 2 * latent :] = jnp.concatenate(
+            [first[:, latent:], second[:, latent:]], axis=1
         )
-        return carry
-
-    lax.fori_loop(0, groups, body, 0)
 
 
 def pack(wanted, pool, shares):
     groups = wanted.shape[0]
-    eighth = pool.shape[1] // shares
-    width = pool.shape[2]
-    return pl.pallas_call(
+    size, width = pool.shape[1:]
+    steps = 4
+    packed = pl.pallas_call(
         pack_kernel,
+        grid=(steps,),
         in_specs=[
             pl.BlockSpec(memory_space=pltpu.SMEM),
             pl.BlockSpec(memory_space=pltpu.VMEM),
         ],
-        out_specs=pl.BlockSpec(memory_space=pltpu.VMEM),
-        out_shape=jax.ShapeDtypeStruct((groups * shares, eighth, 2 * width), BF16),
+        out_specs=pl.BlockSpec((groups // steps * size, 2 * width), lambda i: (i, 0)),
+        out_shape=pltpu.HBM((groups * size, 2 * width), BF16),
         cost_estimate=pl.CostEstimate(flops=0, bytes_accessed=5_000_000, transcendentals=0),
         compiler_params=pltpu.CompilerParams(vmem_limit_bytes=VMEM_LIMIT),
         name="pack",
-    )(wanted, pool.reshape(pool.shape[0] * shares, eighth, width))
+    )(wanted, pool)
+    return packed.reshape(groups * shares, size // shares, 2 * width)
 
 
 def compact_kernel(source_ref, slot_ref, got_ref, after_ref, out_ref):
@@ -176,46 +174,47 @@
     heads, total_rows, wide = q_ref.shape
     size = total_rows // lengths_ref.shape[0]
     latent = wide - 256
-    part = pieces[0][0].shape[0] // 2
+    part = pieces[0][0].shape[0] // 2 // keys_ref.shape[0]
     section = len(picks) * part
-    origin = keys_ref.shape[0] - 4 * section
-    request = pl.program_id(0)
-    length = lengths_ref[request]
+    origin = keys_ref.shape[1] - 4 * section
+    step_requests = keys_ref.shape[0]
     factor = scale * math.log2(math.e)
     lowest = F32(-jnp.inf)
     some = 8
     block = some * size
 
-    @pl.when(request == 0)
+    @pl.when(pl.program_id(0) == 0)
     def _():
-        keys_ref[:, latent:] = jnp.zeros((keys_ref.shape[0], 256), BF16)
+        for turn in range(step_requests):
+            keys_ref[turn, :, latent:] = jnp.zeros((keys_ref.shape[1], 256), BF16)
+            if shared:
+                prompt = taken[0].shape[0]
+                keys_ref[turn, :prompt, : latent + 128] = taken[0][...]
+                keys_ref[turn, prompt + size : origin, :latent] = jnp.zeros(
+                    (origin - prompt - size, latent), BF16
+                )
+
+    for turn in range(step_requests):
         if shared:
             prompt = taken[0].shape[0]
-            keys_ref[:prompt, : latent + 128] = taken[0][...]
-            keys_ref[prompt + size : origin, :latent] = jnp.zeros(
-                (origin - prompt - size, latent), BF16
-            )
-
-    if shared:
-        prompt = taken[0].shape[0]
-        keys_ref[prompt : prompt + size, : latent + 128] = taken[1][...]
-    for which, refs_of in enumerate(pieces):
-        piece = refs_of[0][...]
-        if halves:
-            piece = jnp.where(request < pl.num_programs(0) // 2, piece, refs_of[1][...])
-        for index in range(4):
-            side, half = index // 2, index % 2
-            rows = slice(
-                origin + index * section + which * part,
-                origin + index * section + (which + 1) * part,
-            )
-            some_rows = piece[half * part : (half + 1) * part]
-            keys_ref[rows, :latent] = some_rows[:, side * latent : (side + 1) * latent]
-            keys_ref[rows, latent + side * 128 : latent + (side + 1) * 128] = some_rows[
-                :, 2 * latent :
-            ]
-
-    def work(sections):
+            keys_ref[turn, prompt : prompt + size, : latent + 128] = taken[1][turn * size : (turn + 1) * size]
+        for which, refs_of in enumerate(pieces):
+            piece = refs_of[0][turn * 2 * part : (turn + 1) * 2 * part]
+            if halves:
+                piece = jnp.where(pl.program_id(0) < pl.num_programs(0) // 2, piece, refs_of[1][turn * 2 * part : (turn + 1) * 2 * part])
+            for index in range(4):
+                side, half = index // 2, index % 2
+                rows = slice(
+                    origin + index * section + which * part,
+                    origin + index * section + (which + 1) * part,
+                )
+                some_rows = piece[half * part : (half + 1) * part]
+                keys_ref[turn, rows, :latent] = some_rows[:, side * latent : (side + 1) * latent]
+                keys_ref[turn, rows, latent + side * 128 : latent + (side + 1) * 128] = some_rows[
+                    :, 2 * latent :
+                ]
+
+    def work(turn, request, length, sections):
         count = sections * section
         column = lax.broadcasted_iota(jnp.int32, (1, count), 1)
         position = column // section * 256 + column % part // 8 * 64 + column % 8
@@ -225,16 +224,16 @@
             )
         bias = jnp.where(position < length, 0.0, lowest)
         if shared:
-            hidden = jnp.concatenate([taken[2][0]] * some, axis=0)
+            hidden = jnp.concatenate([taken[2][turn]] * some, axis=0)
         for step in range(heads // some):
             which = slice(step * some, (step + 1) * some)
             rows = slice(step * block, (step + 1) * block)
             q = q_ref[which, pl.ds(pl.multiple_of(request * size, size), size), :]
             q = q.reshape(block, wide)
-            scores = nt_dot(q, keys_ref[origin : origin + count, :]) + bias
+            scores = nt_dot(q, keys_ref[turn, origin : origin + count, :]) + bias
             if shared:
-                first = nt_dot(q, keys_ref[:prompt, :])
-                tree = nt_dot(q, keys_ref[prompt:origin, :]) + hidden
+                first = nt_dot(q, keys_ref[turn, :prompt, :])
+                tree = nt_dot(q, keys_ref[turn, prompt:origin, :]) + hidden
                 scores = jnp.concatenate([first, tree, scores], axis=1)
             top = jnp.broadcast_to(jnp.max(scores, axis=1, keepdims=True), (block, 128))
             if not shared:
@@ -245,7 +244,7 @@
             total = jnp.broadcast_to(jnp.sum(weights, axis=1, keepdims=True), (block, 128))
             mixed = jnp.dot(
                 weights.astype(BF16),
-                keys_ref[0 if shared else origin : origin + count, :latent],
+                keys_ref[turn, 0 if shared else origin : origin + count, :latent],
                 preferred_element_type=F32,
             )
             if not shared:
@@ -261,18 +260,24 @@
                 total_out[request, rows, :] = total
                 sum_out[request, rows, :] = mixed.astype(BF16)
 
-    needed = pl.cdiv(length, 256)
-    steps = (1, 2, 3, 4) if section % 128 == 0 else (2, 4)
-    for low, high in zip((0,) + steps, steps):
-
-        @pl.when((needed > low) & (needed <= high))
-        def _():
-            work(high)
+    steps = (4,) if step_requests > 1 else (1, 2, 3, 4) if section % 128 == 0 else (2, 4)
+    for turn in range(step_requests):
+        request = pl.program_id(0) * step_requests + turn
+        length = lengths_ref[request]
+        needed = pl.cdiv(length, 256)
+        if len(steps) == 1:
+            work(turn, request, length, steps[0])
+        else:
+            for low, high in zip((0,) + steps, steps):
+
+                @pl.when((needed > low) & (needed <= high))
+                def _():
+                    work(turn, request, length, high)
 
     if finish:
         value = values_ref.shape[2]
 
-        @pl.when(request == pl.num_programs(0) - 1)
+        @pl.when(pl.program_id(0) == pl.num_programs(0) - 1)
         def _():
             for head in range(heads):
                 out_ref[:, head * value : (head + 1) * value] = jnp.dot(
@@ -280,7 +285,7 @@
                 ).astype(BF16)
 
 
-def attend(name, scale, lengths, shares, picks, q, shared, given, pieces, up_values=None):
+def attend(name, scale, lengths, shares, picks, q, shared, given, pieces, up_values=None, at_once=1):
     heads, total_rows, wide = q.shape
     requests = lengths.shape[0]
     size = total_rows // requests
@@ -291,7 +296,7 @@
     flat = [array for piece in pieces for array in (piece if halves else (piece,))]
     per = flat[0].shape[0] * (2 if halves else 1) // requests
     width = flat[0].shape[1]
-    half = requests // 2
+    half = requests // 2 // at_once
     origin = given[0].shape[0] + 2 * size if shared else 0
     count = origin + 2 * per * len(pieces)
 
@@ -301,21 +306,21 @@
     if shared:
         in_specs += [
             pl.BlockSpec(given[0].shape, lambda i, *_: (0, 0)),
-            pl.BlockSpec((size, given[1].shape[1]), lambda i, *_: (i, 0)),
-            pl.BlockSpec((1, size, 2 * size), lambda i, *_: (i, 0, 0)),
+            pl.BlockSpec((at_once * size, given[1].shape[1]), lambda i, *_: (i, 0)),
+            pl.BlockSpec((at_once, size, 2 * size), lambda i, *_: (i, 0, 0)),
         ]
     else:
         in_specs += state_specs
     for _ in pieces:
         if halves:
             in_specs.append(
-                pl.BlockSpec((per, width), lambda i, *_: (jnp.minimum(i, half - 1), 0))
+                pl.BlockSpec((at_once * per, width), lambda i, *_: (jnp.minimum(i, half - 1), 0))
             )
-            in_specs.append(pl.BlockSpec((per, width), lambda i, *_: (jnp.maximum(i - half, 0), 0)))
+            in_specs.append(pl.BlockSpec((at_once * per, width), lambda i, *_: (jnp.maximum(i - half, 0), 0)))
         else:
-            in_specs.append(pl.BlockSpec((per, width), lambda i, *_: (i, 0)))
+            in_specs.append(pl.BlockSpec((at_once * per, width), lambda i, *_: (i, 0)))
     operands = [lengths, shares, q, *given, *flat]
-    scratch = [pltpu.VMEM((count, wide), BF16)]
+    scratch = [pltpu.VMEM((at_once, count, wide), BF16)]
     if finish:
         value = up_values.shape[2]
         operands.append(up_values)
@@ -334,7 +339,7 @@
         functools.partial(attend_kernel, scale, picks, shared, halves, finish),
         grid_spec=pltpu.PrefetchScalarGridSpec(
             num_scalar_prefetch=2,
-            grid=(requests,),
+            grid=(requests // at_once,),
             in_specs=in_specs,
             out_specs=out_specs,
             scratch_shapes=scratch,
@@ -404,6 +409,7 @@
     got = lax.all_to_all(packed, ("decode", "pool"), split_axis=0, concat_axis=0, tiled=True)
     q, hidden = prepare(q_nope, q_rope, up_keys, parents)
     prefix = jnp.pad(prefix, ((0, 0), (0, wide - width)))
+    prefix, tree = lax.optimization_barrier((prefix, tree))
     after = hidden[0, :1, :1] + (prefix[:1, :1] + tree[:1, :1]).astype(F32)
     own = compact(owner_of, slot_of, got, after).reshape(-1, 2 * width)
 
@@ -414,43 +420,36 @@
     other = me + 1 - 2 * (me % 2)
     at = [me, other, me - 2, me + 2, other - 2, other + 2, me + 4, other + 4]
     at = jnp.stack([place % shares for place in at]).astype(jnp.int32)
-    below = lax.ppermute(own, "pool", up)
-    above = lax.ppermute(own, "pool", down)
-    beside = lax.ppermute(own, "pool", swap)
-    state = attend(
-        "first", scale, lengths, at, (0, 1), q, True, (prefix, tree, hidden), [own, beside]
-    )
+    def turn(array, pairs):
+        return lax.ppermute(array, "pool", pairs)
+
+    def call(name, picks, given, pieces, **more):
+        return attend(
+            name, scale, lengths, at, picks, q, name == "first", given, pieces, **more
+        )
+
+    below = turn(own, up)
+    above = turn(own, down)
+    state = call("first", (0, 1), (prefix, tree, hidden), [own, turn(own, swap)], at_once=2)
     below, above, state = lax.optimization_barrier((below, above, state))
     middle = own.shape[0] // 2
-    far_up = lax.ppermute(below[:middle], "pool", up)
-    far_down = lax.ppermute(above[middle:], "pool", down)
-    below_beside = lax.ppermute(below, "pool", swap)
-    above_beside = lax.ppermute(above, "pool", swap)
-    state = attend(
+    far_low = turn(below[:middle], up)
+    far_high = turn(above[middle:], down)
+    state = call(
         "second",
-        scale,
-        lengths,
-        at,
         (2, 3, 4, 5),
-        q,
-        False,
         state,
-        [below, above, below_beside, above_beside],
+        [below, above, turn(below, swap), turn(above, swap)],
+        at_once=2,
     )
-    far_up, far_down, state = lax.optimization_barrier((far_up, far_down, state))
-    far_up_beside = lax.ppermute(far_up, "pool", swap)
-    far_down_beside = lax.ppermute(far_down, "pool", swap)
-    return attend(
+    far_low, far_high, state = lax.optimization_barrier((far_low, far_high, state))
+    return call(
         "third",
-        scale,
-        lengths,
-        at,
         (6, 7),
-        q,
-        False,
         state,
-        [(far_up, far_down), (far_up_beside, far_down_beside)],
-        up_values,
+        [(far_low, far_high), (turn(far_low, swap), turn(far_high, swap))],
+        up_values=up_values,
+        at_once=4,
     )
 
 

time: 131 us -> 129 us (0.985)
  waiting for transfers between devices: 19.2 us -> 23 us
  local copies, waits for them, and re-layouts: 27.3 us -> 24.3 us
  Pallas kernels: 46.5 us -> 44.1 us
    ppermute x9, waiting for transfers between devices: 9.03 us -> 13.3 us  [turn(): return lax.ppermute(array, 'pool', pairs)]
    pallas_call x3, Pallas kernels: 34.6 us -> 31.3 us  [attend(): pl.pallas_call(functools.partial(attend_kernel, scale, picks, shared, hal...]
    pad x1, local copies, waits for them, and re-layouts: 2.03 us -> 0.06 us  [local(): tree = jnp.pad(tree_latent, ((0, 0), (0, wide - width)))]
    unnamed x35 -> x37, local copies, waits for them, and re-layouts: 17.6 us -> 17.3 us
  transfers between devices with their start and end apart: 10 -> 10, of which waited for: 6 -> 6; matrix products, arithmetic and copies ran while one was open for 8% -> 5% of each run, Pallas kernels for 25% -> 23%
where the time goes in v4:
time: 129 us
  Pallas kernels  44.1 us (34%)
  local copies, waits for them, and re-layouts  24.3 us (19%)
  waiting for transfers between devices  23 us (18%)
  starting transfers between devices  17.6 us (14%)
  blocking collectives  17 us (13%)
  between operations  2.04 us (2%)
    pallas_call x3, Pallas kernels, attend(): pl.pallas_call(functools.partial(attend_kernel, scale, picks, shared, hal...  31.3 us
    unnamed x37, local copies, waits for them, and re-layouts  17.3 us
    all_to_all x1, blocking collectives, local(): lax.all_to_all(message, 'decode', split_axis=0, concat_axis=0, tiled=True)  17 us
    ppermute x9, waiting for transfers between devices, turn(): return lax.ppermute(array, 'pool', pairs)  13.3 us
    all_to_all x1, waiting for transfers between devices, local(): lax.all_to_all(packed, ('decode', 'pool'), split_axis=0, concat_axis=0, t...  9.67 us
    ppermute x9, starting transfers between devices, turn(): return lax.ppermute(array, 'pool', pairs)  8.98 us
    all_to_all x1, starting transfers between devices, local(): lax.all_to_all(packed, ('decode', 'pool'), split_axis=0, concat_axis=0, t...  8.64 us
    pallas_call x1, Pallas kernels, prepare(): pl.pallas_call(prepare_kernel, grid=(heads,), in_specs=[pl.BlockSpec((row...  7.77 us
  transfers between devices with their start and end apart: 10, of which 6 were waited for; matrix products, arithmetic and copies ran while one was open for 5% of the time, Pallas kernels for 23%

profile of v4, /device:TPU:1, one launch (start us, length us, event | category | flops | bytes accessed | tf_op | source)
XLA Modules:
  0.0 128.5 jit_solution(4819654749185389001)
XLA Ops:
  2.1 17.0 %all_to_all.10 = bf16[16,112,128]{2,1,0:T(8,128)(2,1)} all-to-all(bf16[16,112,128]{2,1,0:T(8,128)(2,1)S(1)} %fusion.1), channel_id=1, replica_groups=mesh['decode'=16,'pool'=8] {'decode'}, dimensions={0} | all-to-all | bytes 917504 | tf_op jit(solution)/shard_map/all_to_all | solution.py:399
  20.1 1.7 %copy-done.2 = bf16[32,64,576]{2,1,0:T(8,128)(2,1)S(1)} copy-done((bf16[32,64,576]{2,1,0:T(8,128)(2,1)S(1)}, bf16[32,64,576]{2,1,0:T(8,128)(2,1)}, u32[]{:S(2)}) %copy-start.2) | copy-done | bytes 2359320
  21.8 2.8 %pack.1 = bf16[1024,1152]{1,0:T(8,128)(2,1)} custom-call(s32[16,2]{1,0:T(8,128)S(1)} %copy.34.wanted_ref, bf16[32,64,576]{2,1,0:T(8,128)(2,1)S(1)} %copy-done.2), custom_call_target="tpu_custom_call" | custom-call | bytes 5000000 | tf_op jit(solution)/shard_map/pack/pallas_call | solution.py:97
  24.7 8.6 %all-to-all-start.1 = ((bf16[128,8,1152]{2,1,0:T(8,128)(2,1)}), bf16[128,8,1152]{2,1,0:T(8,128)(2,1)S(1)}, u32[]{:S(2)}, u32[]{:S(2)}) async-start(bf16[128,8,1152]{2,1,0:T(8,128)(2,1)} %bitcast.22), calls=%async_computation.1 | async-start | bytes 4718592 | tf_op jit(solution)/shard_map/all_to_all | solution.py:409
  33.3 2.1 %copy.35 = bf16[512,576]{1,0:T(8,128)(2,1)} copy(bf16[512,576]{0,1:T(8,128)(2,1)} %param.18) | data formatting | bytes 1179648 | tf_op args[8]
  36.3 1.2 copy-done.5
  39.6 7.8 %prepare.1 = (bf16[8,512,768]{2,1,0:T(8,128)(2,1)S(1)}, f32[8,64,128]{2,1,0:T(8,128)S(1)}) custom-call(bf16[512,1024]{1,0:T(8,128)(2,1)S(1)} %copy-done.4, bf16[512,512]{1,0:T(8,128)(2,1)S(1)} %copy-done.9, bf16[8,128,512]{2,1,0:T(8,128)(2,1)S(1)} %copy-done.5, s32[8,64,1]{2,1,0:T(8,128)S(1)} %copy-done.6), custom_call_target="tpu_custom_call" | custom-call | flops 536870912 | bytes 10000000 | tf_op jit(solution)/shard_map/prepare/pallas_call | solution.py:52
  47.3 2.7 %copy-done = bf16[8,512,768]{2,1,0:T(8,128)(2,1)} copy-done((bf16[8,512,768]{2,1,0:T(8,128)(2,1)}, bf16[8,512,768]{2,1,0:T(8,128)(2,1)S(1)}, u32[]{:S(2)}) %copy-start) | copy-done | bytes 6291480
  51.5 1.7 %reshape.216 = bf16[384,576]{1,0:T(8,128)(2,1)S(1)} reshape(bf16[16,108,128]{2,1,0:T(8,128)(2,1)} %bitcast.17) | data formatting | bytes 884736 | tf_op jit(solution)/shard_map/reshape | solution.py:401
  57.0 9.7 %all-to-all-done.1.got_ref = bf16[128,8,1152]{2,1,0:T(8,128)(2,1)S(1)} async-done(((bf16[128,8,1152]{2,1,0:T(8,128)(2,1)}), bf16[128,8,1152]{2,1,0:T(8,128)(2,1)S(1)}, u32[]{:S(2)}, u32[]{:S(2)}) %all-to-all-start.1) | async-done | bytes 2359328 | tf_op jit(solution)/shard_map/all_to_all | solution.py:409
  66.6 2.2 %compact.1 = bf16[64,8,1152]{2,1,0:T(8,128)(2,1)S(1)} custom-call(s32[128]{0:T(128)S(1)} %get-tuple-element.48.source_ref, s32[128]{0:T(128)S(1)} %convert_element_type.27.slot_ref, bf16[128,8,1152]{2,1,0:T(8,128)(2,1)S(1)} %all-to-all-done.1.got_ref, f32[1,1]{1,0:T(1,128)S(6)} %add.126.after_ref), custom_call_target="tpu_custom_call" | custom-call | bytes 4000000 | tf_op jit(solution)/shard_map/compact/pallas_call | solution.py:141
  68.8 1.2 collective-permute-start.2
  70.0 2.7 %collective-permute-start.1 = (bf16[512,1152]{1,0:T(8,128)(2,1)S(1)}, bf16[512,1152]{1,0:T(8,128)(2,1)S(1)}, u32[]{:S(2)}, u32[]{:S(2)}) collective-permute-start(bf16[512,1152]{1,0:T(8,128)(2,1)S(1)} %bitcast.20), channel_id=1, source_target_pairs={{0,6},{1,7},{2,0},{3,1},{4,2},{5,3},{6,4},{7,5},{8,14},{9,15},{10,... | collective-permute-start | bytes 3538952 | tf_op jit(solution)/shard_map/ppermute | solution.py:424
  72.8 2.8 %copy-done.1 = bf16[8,512,768]{2,1,0:T(8,128)(2,1)S(1)} copy-done((bf16[8,512,768]{2,1,0:T(8,128)(2,1)S(1)}, bf16[8,512,768]{2,1,0:T(8,128)(2,1)}, u32[]{:S(2)}) %copy-start.1) | copy-done | bytes 6291480
  75.6 1.1 copy-done.8
  78.7 13.6 %first.1 = (f32[8,512,128]{2,1,0:T(8,128)S(1)}, f32[8,512,128]{2,1,0:T(8,128)S(1)}, bf16[8,512,512]{2,1,0:T(8,128)(2,1)S(1)}) custom-call(s32[8]{0:T(128)S(1)} %copy-done.12, s32[8]{0:T(128)S(1)} %stack.44.shares_ref, bf16[8,512,768]{2,1,0:T(8,128)(2,1)S(1)} %copy-done.1, bf16[384,640]{1,0:T(8,128)(2,1)S(1)} %copy-done.11, bf16[512,640]{1,0:T(8,128)(2,1)S(1)} %copy-done.8, ...), custom_call_target="tpu_custom_call" | custom-call | flops 6845104128 | bytes 16777216 | tf_op jit(solution)/shard_map/first/pallas_call | solution.py:338
  92.2 6.5 %collective-permute-done.refs_3_ = bf16[512,1152]{1,0:T(8,128)(2,1)S(1)} collective-permute-done((bf16[512,1152]{1,0:T(8,128)(2,1)S(1)}, bf16[512,1152]{1,0:T(8,128)(2,1)S(1)}, u32[]{:S(2)}, u32[]{:S(2)}) %collective-permute-start) | collective-permute-done | bytes 1179680 | tf_op jit(solution)/shard_map/ppermute | solution.py:424
  99.9 2.7 %collective-permute-start.4 = (bf16[256,1152]{1,0:T(8,128)(2,1)S(1)}, bf16[256,1152]{1,0:T(8,128)(2,1)S(1)}, u32[]{:S(2)}, u32[]{:S(2)}) collective-permute-start(bf16[256,1152]{1,0:T(8,128)(2,1)S(1)} %slice.27), channel_id=1, source_target_pairs={{0,6},{1,7},{2,0},{3,1},{4,2},{5,3},{6,4},{7,5},{8,14},{9,15},{10,... | collective-permute-start | bytes 1769480 | tf_op jit(solution)/shard_map/ppermute | solution.py:424
  102.6 1.2 collective-permute-done.6.refs_6_
  103.8 8.5 %second.1 = (f32[8,512,128]{2,1,0:T(8,128)S(1)}, f32[8,512,128]{2,1,0:T(8,128)S(1)}, bf16[8,512,512]{2,1,0:T(8,128)(2,1)S(1)}) custom-call(s32[8]{0:T(128)S(1)} %copy-done.12, s32[8]{0:T(128)S(1)} %stack.44.shares_ref, bf16[8,512,768]{2,1,0:T(8,128)(2,1)S(1)} %copy-done.1, ...), custom_call_target="tpu_custom_call", output_to_operand_aliasing={{0}: (3, {}), {1}: (4, {}), {2}: (5, {})} | custom-call | flops 4563402752 | bytes 16777216 | tf_op jit(solution)/shard_map/second/pallas_call | solution.py:338
  112.3 3.1 %collective-permute-done.3.refs_3_ = bf16[256,1152]{1,0:T(8,128)(2,1)S(1)} collective-permute-done((bf16[256,1152]{1,0:T(8,128)(2,1)S(1)}, bf16[256,1152]{1,0:T(8,128)(2,1)S(1)}, u32[]{:S(2)}, u32[]{:S(2)}) %collective-permute-start.3) | collective-permute-done | bytes 589856 | tf_op jit(solution)/shard_map/ppermute | solution.py:424
  115.4 1.4 %collective-permute-start.7 = (bf16[256,1152]{1,0:T(8,128)(2,1)S(1)}, bf16[256,1152]{1,0:T(8,128)(2,1)S(1)}, u32[]{:S(2)}, u32[]{:S(2)}) collective-permute-start(bf16[256,1152]{1,0:T(8,128)(2,1)S(1)} %collective-permute-done.3.refs_3_), channel_id=1, source_target_pairs={{0,1},{1,0},{2,3},{3,2},{4,5},{5,4},{6,7},{7,6},{8,9},{9,8},{10,11... | collective-permute-start | bytes 1769480 | tf_op jit(solution)/shard_map/ppermute | solution.py:424
  116.8 1.6 %collective-permute-done.7.refs_5_ = bf16[256,1152]{1,0:T(8,128)(2,1)S(1)} collective-permute-done((bf16[256,1152]{1,0:T(8,128)(2,1)S(1)}, bf16[256,1152]{1,0:T(8,128)(2,1)S(1)}, u32[]{:S(2)}, u32[]{:S(2)}) %collective-permute-start.7) | collective-permute-done | bytes 589856 | tf_op jit(solution)/shard_map/ppermute | solution.py:424
  119.3 9.3 %third.1 = bf16[512,1024]{1,0:T(8,128)(2,1)} custom-call(s32[8]{0:T(128)S(1)} %copy-done.12, s32[8]{0:T(128)S(1)} %stack.44.shares_ref, bf16[8,512,768]{2,1,0:T(8,128)(2,1)S(1)} %copy-done.1, f32[8,512,128]{2,1,0:T(8,128)S(1)} %get-tuple-element.40.refs_0_, f32[8,512,128]{2,1,0:T(8,128)S(1)} %get-tuple-element.41.refs_1_, ...), custom_call_target="tpu_custom_call" | custom-call | flops 2281701376 | bytes 16777216 | tf_op jit(solution)/shard_map/third/pallas_call | solution.py:338
  (63 shorter events, 13.3 us)
Async XLA Ops:
  20.1 1.7 %copy-start.2 = (bf16[32,64,576]{2,1,0:T(8,128)(2,1)S(1)}, bf16[32,64,576]{2,1,0:T(8,128)(2,1)}, u32[]{:S(2)}) copy-start(bf16[32,64,576]{2,1,0:T(8,128)(2,1)} %pool_ref.1) | copy-start | bytes 7077892
  24.7 10.8 %copy-start.16 = (s32[8,64]{1,0:T(8,128)S(1)}, s32[8,64]{1,0:T(8,128)}, u32[]{:S(2)}) copy-start(s32[8,64]{1,0:T(8,128)} %param.19) | copy-start | bytes 6148
  24.7 11.7 %copy-start.4 = (bf16[512,1024]{1,0:T(8,128)(2,1)S(1)}, bf16[512,1024]{1,0:T(8,128)(2,1)}, u32[]{:S(2)}) copy-start(bf16[512,1024]{1,0:T(8,128)(2,1)} %rows_ref.1) | copy-start | bytes 3145732
  24.7 42.0 %all-to-all-start.1 = ((bf16[128,8,1152]{2,1,0:T(8,128)(2,1)}), bf16[128,8,1152]{2,1,0:T(8,128)(2,1)S(1)}, u32[]{:S(2)}, u32[]{:S(2)}) async-start(bf16[128,8,1152]{2,1,0:T(8,128)(2,1)} %bitcast.22), calls=%async_computation.1 | async-start | bytes 4718592 | tf_op jit(solution)/shard_map/all_to_all | solution.py:409
  36.3 1.2 copy-start.5
  37.6 0.9 copy-start.6
  38.5 1.0 copy-start.9
  39.5 11.8 %copy-start.15 = (bf16[512,576]{1,0:T(8,128)(2,1)S(1)}, bf16[512,576]{1,0:T(8,128)(2,1)}, u32[]{:S(2)}) copy-start(bf16[512,576]{1,0:T(8,128)(2,1)} %copy.35) | copy-start | bytes 1769476
  47.3 2.7 %copy-start = (bf16[8,512,768]{2,1,0:T(8,128)(2,1)}, bf16[8,512,768]{2,1,0:T(8,128)(2,1)S(1)}, u32[]{:S(2)}) copy-start(bf16[8,512,768]{2,1,0:T(8,128)(2,1)S(1)} %get-tuple-element.25.q_ref) | copy-start | bytes 18874372
  51.5 5.5 %copy-start.7 = (bf16[512,640]{1,0:T(8,128)(2,1)}, bf16[512,640]{1,0:T(8,128)(2,1)S(1)}, u32[]{:S(2)}) copy-start(bf16[512,640]{1,0:T(8,128)(2,1)S(1)} %pad.14.refs_1_) | copy-start | bytes 1966084
  53.2 19.6 %copy-start.12 = (s32[8]{0:T(128)S(1)}, s32[8]{0:T(128)}, u32[]{:S(2)}) copy-start(s32[8]{0:T(128)} %lengths_ref.5) | copy-start | bytes 100
  68.8 4.0 %collective-permute-start.2 = (bf16[512,1152]{1,0:T(8,128)(2,1)S(1)}, bf16[512,1152]{1,0:T(8,128)(2,1)}, u32[]{:S(2)}, u32[]{:S(2)}) collective-permute-start(bf16[512,1152]{1,0:T(8,128)(2,1)S(1)} %bitcast.18), channel_id=1, source_target_pairs={{0,1},{1,0},{2,3},{3,2},{4,5},{5,4},{6,7},{7,6},{8,9},{9,8},{10,11... | collective-permute-start | bytes 3538952 | tf_op jit(solution)/shard_map/ppermute | solution.py:424
  70.0 28.7 %collective-permute-start = (bf16[512,1152]{1,0:T(8,128)(2,1)S(1)}, bf16[512,1152]{1,0:T(8,128)(2,1)S(1)}, u32[]{:S(2)}, u32[]{:S(2)}) collective-permute-start(bf16[512,1152]{1,0:T(8,128)(2,1)S(1)} %bitcast.19), channel_id=1, source_target_pairs={{0,2},{1,3},{2,4},{3,5},{4,6},{5,7},{6,0},{7,1},{8,10},{9,11},{10,... | collective-permute-start | bytes 3538952 | tf_op jit(solution)/shard_map/ppermute | solution.py:424
  70.0 28.7 %collective-permute-start.1 = (bf16[512,1152]{1,0:T(8,128)(2,1)S(1)}, bf16[512,1152]{1,0:T(8,128)(2,1)S(1)}, u32[]{:S(2)}, u32[]{:S(2)}) collective-permute-start(bf16[512,1152]{1,0:T(8,128)(2,1)S(1)} %bitcast.20), channel_id=1, source_target_pairs={{0,6},{1,7},{2,0},{3,1},{4,2},{5,3},{6,4},{7,5},{8,14},{9,15},{10,... | collective-permute-start | bytes 3538952 | tf_op jit(solution)/shard_map/ppermute | solution.py:424
  72.8 2.8 %copy-start.1 = (bf16[8,512,768]{2,1,0:T(8,128)(2,1)S(1)}, bf16[8,512,768]{2,1,0:T(8,128)(2,1)}, u32[]{:S(2)}) copy-start(bf16[8,512,768]{2,1,0:T(8,128)(2,1)} %copy-done) | copy-start | bytes 18874372
  75.6 1.1 copy-start.8
  76.7 1.0 copy-start.11
  98.8 3.8 %collective-permute-start.5 = (bf16[512,1152]{1,0:T(8,128)(2,1)S(1)}, bf16[512,1152]{1,0:T(8,128)(2,1)S(1)}, u32[]{:S(2)}, u32[]{:S(2)}) collective-permute-start(bf16[512,1152]{1,0:T(8,128)(2,1)S(1)} %collective-permute-done.refs_3_), channel_id=1, source_target_pairs={{0,1},{1,0},{2,3},{3,2},{4,5},{5,4},{6,7},{7,6},{8,9},{9,8},{10,11... | collective-permute-start | bytes 3538952 | tf_op jit(solution)/shard_map/ppermute | solution.py:424
  99.6 4.2 %collective-permute-start.6 = (bf16[512,1152]{1,0:T(8,128)(2,1)S(1)}, bf16[512,1152]{1,0:T(8,128)(2,1)S(1)}, u32[]{:S(2)}, u32[]{:S(2)}) collective-permute-start(bf16[512,1152]{1,0:T(8,128)(2,1)S(1)} %collective-permute-done.1.refs_4_), channel_id=1, source_target_pairs={{0,1},{1,0},{2,3},{3,2},{4,5},{5,4},{6,7},{7,6},{8,9},{9,8},{10,11... | collective-permute-start | bytes 3538952 | tf_op jit(solution)/shard_map/ppermute | solution.py:424
  99.8 19.5 %copy-start.3 = (bf16[8,512,128]{2,1,0:T(8,128)(2,1)S(1)}, bf16[8,512,128]{2,1,0:T(8,128)(2,1)}, u32[]{:S(2)}) copy-start(bf16[8,512,128]{2,1,0:T(8,128)(2,1)} %refs_7_.1) | copy-start | bytes 3145732
  99.8 15.7 %collective-permute-start.3 = (bf16[256,1152]{1,0:T(8,128)(2,1)S(1)}, bf16[256,1152]{1,0:T(8,128)(2,1)S(1)}, u32[]{:S(2)}, u32[]{:S(2)}) collective-permute-start(bf16[256,1152]{1,0:T(8,128)(2,1)S(1)} %slice.26), channel_id=1, source_target_pairs={{0,2},{1,3},{2,4},{3,5},{4,6},{5,7},{6,0},{7,1},{8,10},{9,11},{10,... | collective-permute-start | bytes 1769480 | tf_op jit(solution)/shard_map/ppermute | solution.py:424
  99.9 15.6 %collective-permute-start.4 = (bf16[256,1152]{1,0:T(8,128)(2,1)S(1)}, bf16[256,1152]{1,0:T(8,128)(2,1)S(1)}, u32[]{:S(2)}, u32[]{:S(2)}) collective-permute-start(bf16[256,1152]{1,0:T(8,128)(2,1)S(1)} %slice.27), channel_id=1, source_target_pairs={{0,6},{1,7},{2,0},{3,1},{4,2},{5,3},{6,4},{7,5},{8,14},{9,15},{10,... | collective-permute-start | bytes 1769480 | tf_op jit(solution)/shard_map/ppermute | solution.py:424
  115.4 3.0 %collective-permute-start.7 = (bf16[256,1152]{1,0:T(8,128)(2,1)S(1)}, bf16[256,1152]{1,0:T(8,128)(2,1)S(1)}, u32[]{:S(2)}, u32[]{:S(2)}) collective-permute-start(bf16[256,1152]{1,0:T(8,128)(2,1)S(1)} %collective-permute-done.3.refs_3_), channel_id=1, source_target_pairs={{0,1},{1,0},{2,3},{3,2},{4,5},{5,4},{6,7},{7,6},{8,9},{9,8},{10,11... | collective-permute-start | bytes 1769480 | tf_op jit(solution)/shard_map/ppermute | solution.py:424
  116.8 2.5 %collective-permute-start.8 = (bf16[256,1152]{1,0:T(8,128)(2,1)S(1)}, bf16[256,1152]{1,0:T(8,128)(2,1)S(1)}, u32[]{:S(2)}, u32[]{:S(2)}) collective-permute-start(bf16[256,1152]{1,0:T(8,128)(2,1)S(1)} %collective-permute-done.4.refs_4_), channel_id=1, source_target_pairs={{0,1},{1,0},{2,3},{3,2},{4,5},{5,4},{6,7},{7,6},{8,9},{9,8},{10,11... | collective-permute-start | bytes 1769480 | tf_op jit(solution)/shard_map/ppermute | solution.py:424
  (3 other events, 2.5 us)

commit v5 on v4

--- a/solution.py
+++ b/solution.py
@@ -72,6 +72,32 @@
         compiler_params=pltpu.CompilerParams(vmem_limit_bytes=VMEM_LIMIT),
         name="prepare",
     )(q_nope, q_rope, up_keys, parents[:, :, None])
+
+
+def compose_kernel(prompt_ref, asks_ref, pool_ref, out_ref, held_ref):
+    held = prompt_ref.shape[0]
+    rows = lax.broadcasted_iota(jnp.int32, (out_ref.shape[1] - held, 128), 0)
+    for group in range(out_ref.shape[0]):
+        out_ref[group, :held, :] = prompt_ref[...]
+        asks = jnp.pad(asks_ref[group : group + 1, :].astype(F32), ((0, 0), (0, 126)))
+        out_ref[group, held:, :] = jnp.where(rows == 0, asks, 0.0).astype(BF16)
+
+
+def compose(prompt, asks, pool):
+    rows = prompt.shape[0]
+    return pl.pallas_call(
+        compose_kernel,
+        in_specs=[pl.BlockSpec(memory_space=pltpu.VMEM)] * 3,
+        out_specs=[pl.BlockSpec(memory_space=pltpu.VMEM)] * 2,
+        out_shape=[
+            jax.ShapeDtypeStruct((asks.shape[0], rows + 16 - rows % 16, 128), BF16),
+            jax.ShapeDtypeStruct(pool.shape, pool.dtype),
+        ],
+        input_output_aliases={2: 1},
+        cost_estimate=pl.CostEstimate(flops=0, bytes_accessed=1_000_000, transcendentals=0),
+        compiler_params=pltpu.CompilerParams(vmem_limit_bytes=VMEM_LIMIT),
+        name="compose",
+    )(prompt, asks, pool)
 
 
 def pack_kernel(wanted_ref, pool_ref, out_ref):
@@ -387,15 +413,11 @@
     first = jnp.min(jnp.where(match, code[None, :], entries * pool_local), axis=1)
     last = jnp.max(jnp.where(match, code[None, :], 0), axis=1)
     asks = jnp.stack([first, last], axis=1) % pool_local
+    core = me % 2
     prompt = prefix_latent.reshape(-1, 128)
-    held = prompt.shape[0]
-    message = jnp.concatenate(
-        [
-            jnp.broadcast_to(prompt[None], (groups,) + prompt.shape),
-            jnp.pad(asks.astype(BF16)[:, None, :], ((0, 0), (0, 3), (0, 126))),
-        ],
-        axis=1,
-    )
+    held = prompt.shape[0] // 2
+    prompt = jnp.where(core == 0, prompt[:held], prompt[held:])
+    message, held_pool = compose(prompt, asks.astype(BF16), page_pool)
     message = lax.all_to_all(message, "decode", split_axis=0, concat_axis=0, tiled=True)
     wanted = message[:, held, :2].astype(jnp.int32)
     prefix = message[:, :held].reshape(-1, width)
@@ -403,13 +425,11 @@
     slot_of = jnp.any(earlier, axis=1).astype(jnp.int32)
 
     wide = latent_dim + 2 * rope_dim
-    tree = jnp.pad(tree_latent, ((0, 0), (0, wide - width)))
-
-    packed = pack(wanted, page_pool, shares)
+
+    packed = pack(wanted, held_pool, shares)
     got = lax.all_to_all(packed, ("decode", "pool"), split_axis=0, concat_axis=0, tiled=True)
     q, hidden = prepare(q_nope, q_rope, up_keys, parents)
-    prefix = jnp.pad(prefix, ((0, 0), (0, wide - width)))
-    prefix, tree = lax.optimization_barrier((prefix, tree))
+    tree = lax.optimization_barrier(jnp.pad(tree_latent, ((0, 0), (0, wide - width))))
     after = hidden[0, :1, :1] + (prefix[:1, :1] + tree[:1, :1]).astype(F32)
     own = compact(owner_of, slot_of, got, after).reshape(-1, 2 * width)
 
@@ -430,7 +450,11 @@
 
     below = turn(own, up)
     above = turn(own, down)
-    state = call("first", (0, 1), (prefix, tree, hidden), [own, turn(own, swap)], at_once=2)
+    beside = turn(own, swap)
+    beside, prefix = lax.optimization_barrier((beside, prefix))
+    prefix = jnp.concatenate([prefix, turn(prefix, swap)], axis=0)
+    prefix = jnp.pad(prefix, ((0, 0), (0, wide - width)))
+    state = call("first", (0, 1), (prefix, tree, hidden), [own, beside], at_once=2)
     below, above, state = lax.optimization_barrier((below, above, state))
     middle = own.shape[0] // 2
     far_low = turn(below[:middle], up)

time: 129 us -> 125 us (0.969)
  waiting for transfers between devices: 23 us -> 19.7 us
  blocking collectives: 17 us -> 14.8 us
    all_to_all x1, blocking collectives: 17 us -> 14.8 us  [local(): lax.all_to_all(message, 'decode', split_axis=0, concat_axis=0, tiled=True)]
    ppermute x9 -> x10, waiting for transfers between devices: 13.3 us -> 11.4 us  [turn(): return lax.ppermute(array, 'pool', pairs)]
    unnamed x37 -> x40, local copies, waits for them, and re-layouts: 17.3 us -> 18.5 us
    ppermute x9 -> x10, starting transfers between devices: 8.98 us -> 9.6 us  [turn(): return lax.ppermute(array, 'pool', pairs)]
  transfers between devices with their start and end apart: 10 -> 11, of which waited for: 6 -> 7; matrix products, arithmetic and copies ran while one was open for 5% -> 7% of each run, Pallas kernels for 23% -> 23%
where the time goes in v5:
time: 125 us; the launch traced here: 124 us
  Pallas kernels  43.2 us (35%)
  local copies, waits for them, and re-layouts  24.3 us (19%)
  waiting for transfers between devices  19.7 us (16%)
  starting transfers between devices  18.2 us (15%)
  blocking collectives  14.8 us (12%)
  between operations  2.14 us (2%)
  other arithmetic  1.56 us (1%)
    pallas_call x3, Pallas kernels, attend(): pl.pallas_call(functools.partial(attend_kernel, scale, picks, shared, hal...  30.3 us
    unnamed x40, local copies, waits for them, and re-layouts  18.5 us
    all_to_all x1, blocking collectives, local(): lax.all_to_all(message, 'decode', split_axis=0, concat_axis=0, tiled=True)  14.8 us
    ppermute x10, waiting for transfers between devices, turn(): return lax.ppermute(array, 'pool', pairs)  11.4 us
    ppermute x10, starting transfers between devices, turn(): return lax.ppermute(array, 'pool', pairs)  9.6 us
    all_to_all x1, starting transfers between devices, local(): lax.all_to_all(packed, ('decode', 'pool'), split_axis=0, concat_axis=0, t...  8.6 us
    all_to_all x1, waiting for transfers between devices, local(): lax.all_to_all(packed, ('decode', 'pool'), split_axis=0, concat_axis=0, t...  8.39 us
    pallas_call x1, Pallas kernels, prepare(): pl.pallas_call(prepare_kernel, grid=(heads,), in_specs=[pl.BlockSpec((row...  7.77 us
  transfers between devices with their start and end apart: 11, of which 7 were waited for; matrix products, arithmetic and copies ran while one was open for 7% of the time, Pallas kernels for 23%

profile of v5, /device:TPU:1, one launch (start us, length us, event | category | flops | bytes accessed | tf_op | source)
XLA Modules:
  0.0 123.9 jit_solution(10828288920754587228)
XLA Ops:
  0.0 1.8 %copy.53.pool_ref = bf16[32,64,576]{2,1,0:T(8,128)(2,1)S(1)} copy(bf16[32,64,576]{2,1,0:T(8,128)(2,1)} %param.14) | data formatting | bytes 4718592
  2.3 14.8 %all_to_all.10 = bf16[16,64,128]{2,1,0:T(8,128)(2,1)S(1)} all-to-all(bf16[16,64,128]{2,1,0:T(8,128)(2,1)S(1)} %get-tuple-element.28), channel_id=1, replica_groups=mesh['decode'=16,'pool'=8] {'decode'}, dimensions={0} | all-to-all | bytes 524288 | tf_op jit(solution)/shard_map/all_to_all | solution.py:421
  17.2 2.9 %pack.1 = bf16[1024,1152]{1,0:T(8,128)(2,1)} custom-call(s32[16,2]{1,0:T(8,128)S(1)} %bitcast.19, bf16[32,64,576]{2,1,0:T(8,128)(2,1)S(1)} %get-tuple-element.29.pool_ref), custom_call_target="tpu_custom_call" | custom-call | bytes 5000000 | tf_op jit(solution)/shard_map/pack/pallas_call | solution.py:123
  20.1 8.6 %all-to-all-start.1 = ((bf16[128,8,1152]{2,1,0:T(8,128)(2,1)}), bf16[128,8,1152]{2,1,0:T(8,128)(2,1)S(1)}, u32[]{:S(2)}, u32[]{:S(2)}) async-start(bf16[128,8,1152]{2,1,0:T(8,128)(2,1)} %bitcast.20), calls=%async_computation.1 | async-start | bytes 4718592 | tf_op jit(solution)/shard_map/all_to_all | solution.py:430
  28.7 2.2 %copy.46 = bf16[512,576]{1,0:T(8,128)(2,1)} copy(bf16[512,576]{0,1:T(8,128)(2,1)} %param.18) | data formatting | bytes 1179648 | tf_op args[8]
  34.3 1.2 copy-done.4
  37.5 7.8 %prepare.1 = (bf16[8,512,768]{2,1,0:T(8,128)(2,1)S(1)}, f32[8,64,128]{2,1,0:T(8,128)S(1)}) custom-call(bf16[512,1024]{1,0:T(8,128)(2,1)S(1)} %copy-done.3, bf16[512,512]{1,0:T(8,128)(2,1)S(1)} %copy-done.8, bf16[8,128,512]{2,1,0:T(8,128)(2,1)S(1)} %copy-done.4, s32[8,64,1]{2,1,0:T(8,128)S(1)} %copy-done.5), custom_call_target="tpu_custom_call" | custom-call | flops 536870912 | bytes 10000000 | tf_op jit(solution)/shard_map/prepare/pallas_call | solution.py:52
  45.3 2.6 %copy-done = bf16[8,512,768]{2,1,0:T(8,128)(2,1)} copy-done((bf16[8,512,768]{2,1,0:T(8,128)(2,1)}, bf16[8,512,768]{2,1,0:T(8,128)(2,1)S(1)}, u32[]{:S(2)}) %copy-start) | copy-done | bytes 6291480
  50.4 1.2 %slice.40 = bf16[1,1]{1,0:T(2,128)(2,1)} slice(bf16[192,576]{1,0:T(8,128)(2,1)} %reshape.108), slice={[0:1], [0:1]} | slice | bytes 4 | tf_op jit(solution)/shard_map/slice | solution.py:433
  53.6 8.4 %all-to-all-done.1.got_ref = bf16[128,8,1152]{2,1,0:T(8,128)(2,1)S(1)} async-done(((bf16[128,8,1152]{2,1,0:T(8,128)(2,1)}), bf16[128,8,1152]{2,1,0:T(8,128)(2,1)S(1)}, u32[]{:S(2)}, u32[]{:S(2)}) %all-to-all-start.1) | async-done | bytes 2359328 | tf_op jit(solution)/shard_map/all_to_all | solution.py:430
  62.0 2.2 %compact.1 = bf16[64,8,1152]{2,1,0:T(8,128)(2,1)S(1)} custom-call(s32[128]{0:T(128)S(1)} %get-tuple-element.52.source_ref, s32[128]{0:T(128)S(1)} %convert_element_type.18.slot_ref, bf16[128,8,1152]{2,1,0:T(8,128)(2,1)S(1)} %all-to-all-done.1.got_ref, f32[1,1]{1,0:T(1,128)S(6)} %add.118.after_ref), custom_call_target="tpu_custom_call" | custom-call | bytes 4000000 | tf_op jit(solution)/shard_map/compact/pallas_call | solution.py:167
  64.2 1.2 %collective-permute-start.2 = (bf16[512,1152]{1,0:T(8,128)(2,1)S(1)}, bf16[512,1152]{1,0:T(8,128)(2,1)S(1)}, u32[]{:S(2)}, u32[]{:S(2)}) collective-permute-start(bf16[512,1152]{1,0:T(8,128)(2,1)S(1)} %bitcast.15), channel_id=1, source_target_pairs={{0,1},{1,0},{2,3},{3,2},{4,5},{5,4},{6,7},{7,6},{8,9},{9,8},{10,11... | collective-permute-start | bytes 3538952 | tf_op jit(solution)/shard_map/ppermute | solution.py:444
  65.4 2.7 %collective-permute-start.1 = (bf16[512,1152]{1,0:T(8,128)(2,1)S(1)}, bf16[512,1152]{1,0:T(8,128)(2,1)S(1)}, u32[]{:S(2)}, u32[]{:S(2)}) collective-permute-start(bf16[512,1152]{1,0:T(8,128)(2,1)S(1)} %bitcast.17), channel_id=1, source_target_pairs={{0,6},{1,7},{2,0},{3,1},{4,2},{5,3},{6,4},{7,5},{8,14},{9,15},{10,... | collective-permute-start | bytes 3538952 | tf_op jit(solution)/shard_map/ppermute | solution.py:444
  69.8 1.4 %collective-permute-done.3 = bf16[192,576]{1,0:T(8,128)(2,1)} collective-permute-done((bf16[192,576]{1,0:T(8,128)(2,1)}, bf16[192,576]{1,0:T(8,128)(2,1)}, u32[]{:S(2)}, u32[]{:S(2)}) %collective-permute-start.3) | collective-permute-done | bytes 221216 | tf_op jit(solution)/shard_map/ppermute | solution.py:444
  72.3 2.8 %copy-done.1 = bf16[8,512,768]{2,1,0:T(8,128)(2,1)S(1)} copy-done((bf16[8,512,768]{2,1,0:T(8,128)(2,1)S(1)}, bf16[8,512,768]{2,1,0:T(8,128)(2,1)}, u32[]{:S(2)}) %copy-start.1) | copy-done | bytes 6291480
  76.2 1.3 %copy-done.11 = bf16[512,1152]{1,0:T(8,128)(2,1)S(1)} copy-done((bf16[512,1152]{1,0:T(8,128)(2,1)S(1)}, bf16[512,1152]{1,0:T(8,128)(2,1)}, u32[]{:S(2)}) %copy-start.11) | copy-done | bytes 1179672
  78.4 12.5 %first.1 = (f32[8,512,128]{2,1,0:T(8,128)S(1)}, f32[8,512,128]{2,1,0:T(8,128)S(1)}, bf16[8,512,512]{2,1,0:T(8,128)(2,1)S(1)}) custom-call(s32[8]{0:T(128)S(1)} %copy-done.9, s32[8]{0:T(128)S(1)} %stack.44.shares_ref, bf16[8,512,768]{2,1,0:T(8,128)(2,1)S(1)} %copy-done.1, bf16[384,640]{1,0:T(8,128)(2,1)S(1)} %fusion.2.refs_0_, ...), custom_call_target="tpu_custom_call" | custom-call | flops 6845104128 | bytes 16777216 | tf_op jit(solution)/shard_map/first/pallas_call | solution.py:364
  91.0 3.2 %collective-permute-done.refs_3_ = bf16[512,1152]{1,0:T(8,128)(2,1)S(1)} collective-permute-done((bf16[512,1152]{1,0:T(8,128)(2,1)S(1)}, bf16[512,1152]{1,0:T(8,128)(2,1)S(1)}, u32[]{:S(2)}, u32[]{:S(2)}) %collective-permute-start) | collective-permute-done | bytes 1179680 | tf_op jit(solution)/shard_map/ppermute | solution.py:444
  95.2 2.7 %collective-permute-start.5 = (bf16[256,1152]{1,0:T(8,128)(2,1)S(1)}, bf16[256,1152]{1,0:T(8,128)(2,1)S(1)}, u32[]{:S(2)}, u32[]{:S(2)}) collective-permute-start(bf16[256,1152]{1,0:T(8,128)(2,1)S(1)} %slice.37), channel_id=1, source_target_pairs={{0,6},{1,7},{2,0},{3,1},{4,2},{5,3},{6,4},{7,5},{8,14},{9,15},{10,... | collective-permute-start | bytes 1769480 | tf_op jit(solution)/shard_map/ppermute | solution.py:444
  99.2 8.5 %second.1 = (f32[8,512,128]{2,1,0:T(8,128)S(1)}, f32[8,512,128]{2,1,0:T(8,128)S(1)}, bf16[8,512,512]{2,1,0:T(8,128)(2,1)S(1)}) custom-call(s32[8]{0:T(128)S(1)} %copy-done.9, s32[8]{0:T(128)S(1)} %stack.44.shares_ref, bf16[8,512,768]{2,1,0:T(8,128)(2,1)S(1)} %copy-done.1, ...), custom_call_target="tpu_custom_call", output_to_operand_aliasing={{0}: (3, {}), {1}: (4, {}), {2}: (5, {})} | custom-call | flops 4563402752 | bytes 16777216 | tf_op jit(solution)/shard_map/second/pallas_call | solution.py:364
  107.7 3.1 %collective-permute-done.4.refs_3_ = bf16[256,1152]{1,0:T(8,128)(2,1)S(1)} collective-permute-done((bf16[256,1152]{1,0:T(8,128)(2,1)S(1)}, bf16[256,1152]{1,0:T(8,128)(2,1)S(1)}, u32[]{:S(2)}, u32[]{:S(2)}) %collective-permute-start.4) | collective-permute-done | bytes 589856 | tf_op jit(solution)/shard_map/ppermute | solution.py:444
  110.8 1.4 %collective-permute-start.8 = (bf16[256,1152]{1,0:T(8,128)(2,1)S(1)}, bf16[256,1152]{1,0:T(8,128)(2,1)S(1)}, u32[]{:S(2)}, u32[]{:S(2)}) collective-permute-start(bf16[256,1152]{1,0:T(8,128)(2,1)S(1)} %collective-permute-done.4.refs_3_), channel_id=1, source_target_pairs={{0,1},{1,0},{2,3},{3,2},{4,5},{5,4},{6,7},{7,6},{8,9},{9,8},{10,11... | collective-permute-start | bytes 1769480 | tf_op jit(solution)/shard_map/ppermute | solution.py:444
  112.2 1.6 %collective-permute-done.8.refs_5_ = bf16[256,1152]{1,0:T(8,128)(2,1)S(1)} collective-permute-done((bf16[256,1152]{1,0:T(8,128)(2,1)S(1)}, bf16[256,1152]{1,0:T(8,128)(2,1)S(1)}, u32[]{:S(2)}, u32[]{:S(2)}) %collective-permute-start.8) | collective-permute-done | bytes 589856 | tf_op jit(solution)/shard_map/ppermute | solution.py:444
  114.6 9.3 %third.1 = bf16[512,1024]{1,0:T(8,128)(2,1)} custom-call(s32[8]{0:T(128)S(1)} %copy-done.9, s32[8]{0:T(128)S(1)} %stack.44.shares_ref, bf16[8,512,768]{2,1,0:T(8,128)(2,1)S(1)} %copy-done.1, f32[8,512,128]{2,1,0:T(8,128)S(1)} %get-tuple-element.44.refs_0_, f32[8,512,128]{2,1,0:T(8,128)S(1)} %get-tuple-element.45.refs_1_, ...), custom_call_target="tpu_custom_call" | custom-call | flops 2281701376 | bytes 16777216 | tf_op jit(solution)/shard_map/third/pallas_call | solution.py:364
  (69 shorter events, 16.4 us)
Async XLA Ops:
  0.0 1.9 %copy-start.18 = (s32[8,16]{1,0:T(8,128)S(1)}, s32[8,16]{1,0:T(8,128)}, u32[]{:S(2)}) copy-start(s32[8,16]{1,0:T(8,128)} %param.15) | copy-start | bytes 1540
  0.0 1.8 %copy-start.16 = (bf16[24,576]{1,0:T(8,128)(2,1)S(1)}, bf16[24,576]{1,0:T(8,128)(2,1)}, u32[]{:S(2)}) copy-start(bf16[24,576]{1,0:T(8,128)(2,1)} %param.17) | copy-start | bytes 82948
  17.2 2.9 %copy-start.14 = (bf16[16,64,128]{2,1,0:T(8,128)(2,1)}, bf16[16,64,128]{2,1,0:T(8,128)(2,1)S(1)}, u32[]{:S(2)}) copy-start(bf16[16,64,128]{2,1,0:T(8,128)(2,1)S(1)} %all_to_all.10) | copy-start | bytes 786436
  20.1 41.9 %all-to-all-start.1 = ((bf16[128,8,1152]{2,1,0:T(8,128)(2,1)}), bf16[128,8,1152]{2,1,0:T(8,128)(2,1)S(1)}, u32[]{:S(2)}, u32[]{:S(2)}) async-start(bf16[128,8,1152]{2,1,0:T(8,128)(2,1)} %bitcast.20), calls=%async_computation.1 | async-start | bytes 4718592 | tf_op jit(solution)/shard_map/all_to_all | solution.py:430
  28.7 4.8 %copy-start.17 = (s32[8,64]{1,0:T(8,128)S(1)}, s32[8,64]{1,0:T(8,128)}, u32[]{:S(2)}) copy-start(s32[8,64]{1,0:T(8,128)} %param.19) | copy-start | bytes 6148
  28.7 5.6 %copy-start.3 = (bf16[512,1024]{1,0:T(8,128)(2,1)S(1)}, bf16[512,1024]{1,0:T(8,128)(2,1)}, u32[]{:S(2)}) copy-start(bf16[512,1024]{1,0:T(8,128)(2,1)} %rows_ref.1) | copy-start | bytes 3145732
  34.3 1.2 copy-start.4
  37.5 11.9 %copy-start.15 = (bf16[16,64,128]{2,1,0:T(8,128)(2,1)S(1)}, bf16[16,64,128]{2,1,0:T(8,128)(2,1)}, u32[]{:S(2)}) copy-start(bf16[16,64,128]{2,1,0:T(8,128)(2,1)} %copy-done.14) | copy-start | bytes 786436
  45.3 2.6 %copy-start = (bf16[8,512,768]{2,1,0:T(8,128)(2,1)}, bf16[8,512,768]{2,1,0:T(8,128)(2,1)S(1)}, u32[]{:S(2)}) copy-start(bf16[8,512,768]{2,1,0:T(8,128)(2,1)S(1)} %get-tuple-element.27.q_ref) | copy-start | bytes 18874372
  53.6 18.7 %copy-start.9 = (s32[8]{0:T(128)S(1)}, s32[8]{0:T(128)}, u32[]{:S(2)}) copy-start(s32[8]{0:T(128)} %lengths_ref.5) | copy-start | bytes 100
  64.2 3.9 %collective-permute-start.2 = (bf16[512,1152]{1,0:T(8,128)(2,1)S(1)}, bf16[512,1152]{1,0:T(8,128)(2,1)S(1)}, u32[]{:S(2)}, u32[]{:S(2)}) collective-permute-start(bf16[512,1152]{1,0:T(8,128)(2,1)S(1)} %bitcast.15), channel_id=1, source_target_pairs={{0,1},{1,0},{2,3},{3,2},{4,5},{5,4},{6,7},{7,6},{8,9},{9,8},{10,11... | collective-permute-start | bytes 3538952 | tf_op jit(solution)/shard_map/ppermute | solution.py:444
  65.4 28.7 %collective-permute-start = (bf16[512,1152]{1,0:T(8,128)(2,1)S(1)}, bf16[512,1152]{1,0:T(8,128)(2,1)S(1)}, u32[]{:S(2)}, u32[]{:S(2)}) collective-permute-start(bf16[512,1152]{1,0:T(8,128)(2,1)S(1)} %bitcast.16), channel_id=1, source_target_pairs={{0,2},{1,3},{2,4},{3,5},{4,6},{5,7},{6,0},{7,1},{8,10},{9,11},{10,... | collective-permute-start | bytes 3538952 | tf_op jit(solution)/shard_map/ppermute | solution.py:444
  65.4 28.7 %collective-permute-start.1 = (bf16[512,1152]{1,0:T(8,128)(2,1)S(1)}, bf16[512,1152]{1,0:T(8,128)(2,1)S(1)}, u32[]{:S(2)}, u32[]{:S(2)}) collective-permute-start(bf16[512,1152]{1,0:T(8,128)(2,1)S(1)} %bitcast.17), channel_id=1, source_target_pairs={{0,6},{1,7},{2,0},{3,1},{4,2},{5,3},{6,4},{7,5},{8,14},{9,15},{10,... | collective-permute-start | bytes 3538952 | tf_op jit(solution)/shard_map/ppermute | solution.py:444
  69.1 2.1 %collective-permute-start.3 = (bf16[192,576]{1,0:T(8,128)(2,1)}, bf16[192,576]{1,0:T(8,128)(2,1)}, u32[]{:S(2)}, u32[]{:S(2)}) collective-permute-start(bf16[192,576]{1,0:T(8,128)(2,1)} %reshape.108), channel_id=1, source_target_pairs={{0,1},{1,0},{2,3},{3,2},{4,5},{5,4},{6,7},{7,6},{8,9},{9,8},{10,11... | collective-permute-start | bytes 663560 | tf_op jit(solution)/shard_map/ppermute | solution.py:444
  72.3 2.8 %copy-start.1 = (bf16[8,512,768]{2,1,0:T(8,128)(2,1)S(1)}, bf16[8,512,768]{2,1,0:T(8,128)(2,1)}, u32[]{:S(2)}) copy-start(bf16[8,512,768]{2,1,0:T(8,128)(2,1)} %copy-done) | copy-start | bytes 18874372
  75.1 1.1 copy-start.7
  76.2 1.3 %copy-start.11 = (bf16[512,1152]{1,0:T(8,128)(2,1)S(1)}, bf16[512,1152]{1,0:T(8,128)(2,1)}, u32[]{:S(2)}) copy-start(bf16[512,1152]{1,0:T(8,128)(2,1)} %copy-done.10) | copy-start | bytes 3538948
  94.2 3.8 %collective-permute-start.6 = (bf16[512,1152]{1,0:T(8,128)(2,1)S(1)}, bf16[512,1152]{1,0:T(8,128)(2,1)S(1)}, u32[]{:S(2)}, u32[]{:S(2)}) collective-permute-start(bf16[512,1152]{1,0:T(8,128)(2,1)S(1)} %collective-permute-done.refs_3_), channel_id=1, source_target_pairs={{0,1},{1,0},{2,3},{3,2},{4,5},{5,4},{6,7},{7,6},{8,9},{9,8},{10,11... | collective-permute-start | bytes 3538952 | tf_op jit(solution)/shard_map/ppermute | solution.py:444
  95.0 4.2 %collective-permute-start.7 = (bf16[512,1152]{1,0:T(8,128)(2,1)S(1)}, bf16[512,1152]{1,0:T(8,128)(2,1)S(1)}, u32[]{:S(2)}, u32[]{:S(2)}) collective-permute-start(bf16[512,1152]{1,0:T(8,128)(2,1)S(1)} %collective-permute-done.1.refs_4_), channel_id=1, source_target_pairs={{0,1},{1,0},{2,3},{3,2},{4,5},{5,4},{6,7},{7,6},{8,9},{9,8},{10,11... | collective-permute-start | bytes 3538952 | tf_op jit(solution)/shard_map/ppermute | solution.py:444
  95.1 19.5 %copy-start.2 = (bf16[8,512,128]{2,1,0:T(8,128)(2,1)S(1)}, bf16[8,512,128]{2,1,0:T(8,128)(2,1)}, u32[]{:S(2)}) copy-start(bf16[8,512,128]{2,1,0:T(8,128)(2,1)} %refs_7_.1) | copy-start | bytes 3145732
  95.1 15.7 %collective-permute-start.4 = (bf16[256,1152]{1,0:T(8,128)(2,1)S(1)}, bf16[256,1152]{1,0:T(8,128)(2,1)S(1)}, u32[]{:S(2)}, u32[]{:S(2)}) collective-permute-start(bf16[256,1152]{1,0:T(8,128)(2,1)S(1)} %slice.36), channel_id=1, source_target_pairs={{0,2},{1,3},{2,4},{3,5},{4,6},{5,7},{6,0},{7,1},{8,10},{9,11},{10,... | collective-permute-start | bytes 1769480 | tf_op jit(solution)/shard_map/ppermute | solution.py:444
  95.2 15.6 %collective-permute-start.5 = (bf16[256,1152]{1,0:T(8,128)(2,1)S(1)}, bf16[256,1152]{1,0:T(8,128)(2,1)S(1)}, u32[]{:S(2)}, u32[]{:S(2)}) collective-permute-start(bf16[256,1152]{1,0:T(8,128)(2,1)S(1)} %slice.37), channel_id=1, source_target_pairs={{0,6},{1,7},{2,0},{3,1},{4,2},{5,3},{6,4},{7,5},{8,14},{9,15},{10,... | collective-permute-start | bytes 1769480 | tf_op jit(solution)/shard_map/ppermute | solution.py:444
  110.8 3.0 %collective-permute-start.8 = (bf16[256,1152]{1,0:T(8,128)(2,1)S(1)}, bf16[256,1152]{1,0:T(8,128)(2,1)S(1)}, u32[]{:S(2)}, u32[]{:S(2)}) collective-permute-start(bf16[256,1152]{1,0:T(8,128)(2,1)S(1)} %collective-permute-done.4.refs_3_), channel_id=1, source_target_pairs={{0,1},{1,0},{2,3},{3,2},{4,5},{5,4},{6,7},{7,6},{8,9},{9,8},{10,11... | collective-permute-start | bytes 1769480 | tf_op jit(solution)/shard_map/ppermute | solution.py:444
  112.2 2.5 %collective-permute-start.9 = (bf16[256,1152]{1,0:T(8,128)(2,1)S(1)}, bf16[256,1152]{1,0:T(8,128)(2,1)S(1)}, u32[]{:S(2)}, u32[]{:S(2)}) collective-permute-start(bf16[256,1152]{1,0:T(8,128)(2,1)S(1)} %collective-permute-done.5.refs_4_), channel_id=1, source_target_pairs={{0,1},{1,0},{2,3},{3,2},{4,5},{5,4},{6,7},{7,6},{8,9},{9,8},{10,11... | collective-permute-start | bytes 1769480 | tf_op jit(solution)/shard_map/ppermute | solution.py:444
  (6 other events, 5.5 us)

commit v6 on v5

--- a/solution.py
+++ b/solution.py
@@ -74,23 +74,25 @@
     )(q_nope, q_rope, up_keys, parents[:, :, None])
 
 
-def compose_kernel(prompt_ref, asks_ref, pool_ref, out_ref, held_ref):
-    held = prompt_ref.shape[0]
-    rows = lax.broadcasted_iota(jnp.int32, (out_ref.shape[1] - held, 128), 0)
+def compose_kernel(held, prompt_ref, asks_ref, pool_ref, out_ref, pool_out_ref):
+    prompt = prompt_ref[...].astype(F32)
+    asks = asks_ref[...].astype(F32)
+    rows = lax.broadcasted_iota(jnp.int32, prompt.shape, 0)
     for group in range(out_ref.shape[0]):
-        out_ref[group, :held, :] = prompt_ref[...]
-        asks = jnp.pad(asks_ref[group : group + 1, :].astype(F32), ((0, 0), (0, 126)))
-        out_ref[group, held:, :] = jnp.where(rows == 0, asks, 0.0).astype(BF16)
+        out_ref[group] = jnp.where(rows == held, asks[group : group + 1, :], prompt).astype(BF16)
 
 
 def compose(prompt, asks, pool):
-    rows = prompt.shape[0]
+    held = prompt.shape[0]
+    rows = held + 16 - held % 16
+    prompt = jnp.pad(prompt, ((0, rows - held), (0, 0)))
+    asks = jnp.pad(asks, ((0, 0), (0, 126)))
     return pl.pallas_call(
-        compose_kernel,
+        functools.partial(compose_kernel, held),
         in_specs=[pl.BlockSpec(memory_space=pltpu.VMEM)] * 3,
         out_specs=[pl.BlockSpec(memory_space=pltpu.VMEM)] * 2,
         out_shape=[
-            jax.ShapeDtypeStruct((asks.shape[0], rows + 16 - rows % 16, 128), BF16),
+            jax.ShapeDtypeStruct((asks.shape[0], rows, 128), BF16),
             jax.ShapeDtypeStruct(pool.shape, pool.dtype),
         ],
         input_output_aliases={2: 1},
@@ -200,7 +202,8 @@
     heads, total_rows, wide = q_ref.shape
     size = total_rows // lengths_ref.shape[0]
     latent = wide - 256
-    part = pieces[0][0].shape[0] // 2 // keys_ref.shape[0]
+    whole = halves and keys_ref.shape[0] == lengths_ref.shape[0]
+    part = pieces[0][0].shape[0] // 2 // keys_ref.shape[0] * (2 if whole else 1)
     section = len(picks) * part
     origin = keys_ref.shape[1] - 4 * section
     step_requests = keys_ref.shape[0]
@@ -225,8 +228,9 @@
             prompt = taken[0].shape[0]
             keys_ref[turn, prompt : prompt + size, : latent + 128] = taken[1][turn * size : (turn + 1) * size]
         for which, refs_of in enumerate(pieces):
-            piece = refs_of[0][turn * 2 * part : (turn + 1) * 2 * part]
-            if halves:
+            half_of, place = divmod(turn, step_requests // 2) if whole else (0, turn)
+            piece = refs_of[half_of][place * 2 * part : (place + 1) * 2 * part]
+            if halves and not whole:
                 piece = jnp.where(pl.program_id(0) < pl.num_programs(0) // 2, piece, refs_of[1][turn * 2 * part : (turn + 1) * 2 * part])
             for index in range(4):
                 side, half = index // 2, index % 2
@@ -267,7 +271,12 @@
                 top = jnp.maximum(top, before)
                 fade = jnp.exp2((before - top) * factor)
             weights = jnp.exp2((scores - spread(top, scores.shape[1])) * factor)
-            total = jnp.broadcast_to(jnp.sum(weights, axis=1, keepdims=True), (block, 128))
+            if finish:
+                weights = weights.astype(BF16)
+                ones = jnp.ones((weights.shape[1], 128), BF16)
+                total = jnp.dot(weights, ones, preferred_element_type=F32)
+            else:
+                total = jnp.broadcast_to(jnp.sum(weights, axis=1, keepdims=True), (block, 128))
             mixed = jnp.dot(
                 weights.astype(BF16),
                 keys_ref[turn, 0 if shared else origin : origin + count, :latent],
@@ -338,7 +347,9 @@
     else:
         in_specs += state_specs
     for _ in pieces:
-        if halves:
+        if halves and half == 0:
+            in_specs += [whole, whole]
+        elif halves:
             in_specs.append(
                 pl.BlockSpec((at_once * per, width), lambda i, *_: (jnp.minimum(i, half - 1), 0))
             )
@@ -473,7 +484,7 @@
         state,
         [(far_low, far_high), (turn(far_low, swap), turn(far_high, swap))],
         up_values=up_values,
-        at_once=4,
+        at_once=8,
     )
 
 

time: 125 us -> 123 us (0.984)
  Pallas kernels: 43.2 us -> 41.8 us
    pallas_call x3, Pallas kernels: 30.3 us -> 29 us  [attend(): pl.pallas_call(functools.partial(attend_kernel, scale, picks, shared, hal...]
  transfers between devices with their start and end apart: 11 -> 11, of which waited for: 7 -> 7; matrix products, arithmetic and copies ran while one was open for 7% -> 7% of each run, Pallas kernels for 23% -> 24%
where the time goes in v6:
time: 123 us
  Pallas kernels  41.8 us (34%)
  local copies, waits for them, and re-layouts  24.3 us (20%)
  waiting for transfers between devices  19.8 us (16%)
  starting transfers between devices  18.2 us (15%)
  blocking collectives  14.8 us (12%)
  between operations  2.15 us (2%)
  other arithmetic  1.56 us (1%)
    pallas_call x3, Pallas kernels, attend(): pl.pallas_call(functools.partial(attend_kernel, scale, picks, shared, hal...  29 us
    unnamed x40, local copies, waits for them, and re-layouts  18.5 us
    all_to_all x1, blocking collectives, local(): lax.all_to_all(message, 'decode', split_axis=0, concat_axis=0, tiled=True)  14.8 us
    ppermute x10, waiting for transfers between devices, turn(): return lax.ppermute(array, 'pool', pairs)  11.3 us
    ppermute x10, starting transfers between devices, turn(): return lax.ppermute(array, 'pool', pairs)  9.6 us
    all_to_all x1, starting transfers between devices, local(): lax.all_to_all(packed, ('decode', 'pool'), split_axis=0, concat_axis=0, t...  8.6 us
    all_to_all x1, waiting for transfers between devices, local(): lax.all_to_all(packed, ('decode', 'pool'), split_axis=0, concat_axis=0, t...  8.4 us
    pallas_call x1, Pallas kernels, prepare(): pl.pallas_call(prepare_kernel, grid=(heads,), in_specs=[pl.BlockSpec((row...  7.77 us
  transfers between devices with their start and end apart: 11, of which 7 were waited for; matrix products, arithmetic and copies ran while one was open for 7% of the time, Pallas kernels for 24%

profile of v6, /device:TPU:1, one launch (start us, length us, event | category | flops | bytes accessed | tf_op | source)
XLA Modules:
  0.0 122.6 jit_solution(2104587026933606894)
XLA Ops:
  0.0 1.8 %copy.53.pool_ref = bf16[32,64,576]{2,1,0:T(8,128)(2,1)S(1)} copy(bf16[32,64,576]{2,1,0:T(8,128)(2,1)} %param.14) | data formatting | bytes 4718592
  2.4 14.8 %all_to_all.10 = bf16[16,64,128]{2,1,0:T(8,128)(2,1)S(1)} all-to-all(bf16[16,64,128]{2,1,0:T(8,128)(2,1)S(1)} %get-tuple-element.28), channel_id=1, replica_groups=mesh['decode'=16,'pool'=8] {'decode'}, dimensions={0} | all-to-all | bytes 524288 | tf_op jit(solution)/shard_map/all_to_all | solution.py:432
  17.2 2.9 %pack.1 = bf16[1024,1152]{1,0:T(8,128)(2,1)} custom-call(s32[16,2]{1,0:T(8,128)S(1)} %bitcast.19, bf16[32,64,576]{2,1,0:T(8,128)(2,1)S(1)} %get-tuple-element.29.pool_ref), custom_call_target="tpu_custom_call" | custom-call | bytes 5000000 | tf_op jit(solution)/shard_map/pack/pallas_call | solution.py:125
  20.1 8.6 %all-to-all-start.1 = ((bf16[128,8,1152]{2,1,0:T(8,128)(2,1)}), bf16[128,8,1152]{2,1,0:T(8,128)(2,1)S(1)}, u32[]{:S(2)}, u32[]{:S(2)}) async-start(bf16[128,8,1152]{2,1,0:T(8,128)(2,1)} %bitcast.20), calls=%async_computation.1 | async-start | bytes 4718592 | tf_op jit(solution)/shard_map/all_to_all | solution.py:441
  28.7 2.2 %copy.46 = bf16[512,576]{1,0:T(8,128)(2,1)} copy(bf16[512,576]{0,1:T(8,128)(2,1)} %param.18) | data formatting | bytes 1179648 | tf_op args[8]
  34.3 1.2 copy-done.4
  37.6 7.8 %prepare.1 = (bf16[8,512,768]{2,1,0:T(8,128)(2,1)S(1)}, f32[8,64,128]{2,1,0:T(8,128)S(1)}) custom-call(bf16[512,1024]{1,0:T(8,128)(2,1)S(1)} %copy-done.3, bf16[512,512]{1,0:T(8,128)(2,1)S(1)} %copy-done.8, bf16[8,128,512]{2,1,0:T(8,128)(2,1)S(1)} %copy-done.4, s32[8,64,1]{2,1,0:T(8,128)S(1)} %copy-done.5), custom_call_target="tpu_custom_call" | custom-call | flops 536870912 | bytes 10000000 | tf_op jit(solution)/shard_map/prepare/pallas_call | solution.py:52
  45.3 2.6 %copy-done = bf16[8,512,768]{2,1,0:T(8,128)(2,1)} copy-done((bf16[8,512,768]{2,1,0:T(8,128)(2,1)}, bf16[8,512,768]{2,1,0:T(8,128)(2,1)S(1)}, u32[]{:S(2)}) %copy-start) | copy-done | bytes 6291480
  50.4 1.2 %slice.40 = bf16[1,1]{1,0:T(2,128)(2,1)} slice(bf16[192,576]{1,0:T(8,128)(2,1)} %reshape.108), slice={[0:1], [0:1]} | slice | bytes 4 | tf_op jit(solution)/shard_map/slice | solution.py:444
  53.6 8.4 %all-to-all-done.1.got_ref = bf16[128,8,1152]{2,1,0:T(8,128)(2,1)S(1)} async-done(((bf16[128,8,1152]{2,1,0:T(8,128)(2,1)}), bf16[128,8,1152]{2,1,0:T(8,128)(2,1)S(1)}, u32[]{:S(2)}, u32[]{:S(2)}) %all-to-all-start.1) | async-done | bytes 2359328 | tf_op jit(solution)/shard_map/all_to_all | solution.py:441
  62.0 2.2 %compact.1 = bf16[64,8,1152]{2,1,0:T(8,128)(2,1)S(1)} custom-call(s32[128]{0:T(128)S(1)} %get-tuple-element.52.source_ref, s32[128]{0:T(128)S(1)} %convert_element_type.22.slot_ref, bf16[128,8,1152]{2,1,0:T(8,128)(2,1)S(1)} %all-to-all-done.1.got_ref, f32[1,1]{1,0:T(1,128)S(6)} %add.122.after_ref), custom_call_target="tpu_custom_call" | custom-call | bytes 4000000 | tf_op jit(solution)/shard_map/compact/pallas_call | solution.py:169
  64.2 1.2 %collective-permute-start.2 = (bf16[512,1152]{1,0:T(8,128)(2,1)S(1)}, bf16[512,1152]{1,0:T(8,128)(2,1)S(1)}, u32[]{:S(2)}, u32[]{:S(2)}) collective-permute-start(bf16[512,1152]{1,0:T(8,128)(2,1)S(1)} %bitcast.15), channel_id=1, source_target_pairs={{0,1},{1,0},{2,3},{3,2},{4,5},{5,4},{6,7},{7,6},{8,9},{9,8},{10,11... | collective-permute-start | bytes 3538952 | tf_op jit(solution)/shard_map/ppermute | solution.py:455
  65.4 2.7 %collective-permute-start.1 = (bf16[512,1152]{1,0:T(8,128)(2,1)S(1)}, bf16[512,1152]{1,0:T(8,128)(2,1)S(1)}, u32[]{:S(2)}, u32[]{:S(2)}) collective-permute-start(bf16[512,1152]{1,0:T(8,128)(2,1)S(1)} %bitcast.17), channel_id=1, source_target_pairs={{0,6},{1,7},{2,0},{3,1},{4,2},{5,3},{6,4},{7,5},{8,14},{9,15},{10,... | collective-permute-start | bytes 3538952 | tf_op jit(solution)/shard_map/ppermute | solution.py:455
  69.8 1.4 %collective-permute-done.3 = bf16[192,576]{1,0:T(8,128)(2,1)} collective-permute-done((bf16[192,576]{1,0:T(8,128)(2,1)}, bf16[192,576]{1,0:T(8,128)(2,1)}, u32[]{:S(2)}, u32[]{:S(2)}) %collective-permute-start.3) | collective-permute-done | bytes 221216 | tf_op jit(solution)/shard_map/ppermute | solution.py:455
  72.4 2.8 %copy-done.1 = bf16[8,512,768]{2,1,0:T(8,128)(2,1)S(1)} copy-done((bf16[8,512,768]{2,1,0:T(8,128)(2,1)S(1)}, bf16[8,512,768]{2,1,0:T(8,128)(2,1)}, u32[]{:S(2)}) %copy-start.1) | copy-done | bytes 6291480
  76.2 1.3 %copy-done.11 = bf16[512,1152]{1,0:T(8,128)(2,1)S(1)} copy-done((bf16[512,1152]{1,0:T(8,128)(2,1)S(1)}, bf16[512,1152]{1,0:T(8,128)(2,1)}, u32[]{:S(2)}) %copy-start.11) | copy-done | bytes 1179672
  78.5 12.6 %first.1 = (f32[8,512,128]{2,1,0:T(8,128)S(1)}, f32[8,512,128]{2,1,0:T(8,128)S(1)}, bf16[8,512,512]{2,1,0:T(8,128)(2,1)S(1)}) custom-call(s32[8]{0:T(128)S(1)} %copy-done.9, s32[8]{0:T(128)S(1)} %stack.44.shares_ref, bf16[8,512,768]{2,1,0:T(8,128)(2,1)S(1)} %copy-done.1, bf16[384,640]{1,0:T(8,128)(2,1)S(1)} %fusion.2.refs_0_, ...), custom_call_target="tpu_custom_call" | custom-call | flops 6845104128 | bytes 16777216 | tf_op jit(solution)/shard_map/first/pallas_call | solution.py:375
  91.0 3.2 %collective-permute-done.refs_3_ = bf16[512,1152]{1,0:T(8,128)(2,1)S(1)} collective-permute-done((bf16[512,1152]{1,0:T(8,128)(2,1)S(1)}, bf16[512,1152]{1,0:T(8,128)(2,1)S(1)}, u32[]{:S(2)}, u32[]{:S(2)}) %collective-permute-start) | collective-permute-done | bytes 1179680 | tf_op jit(solution)/shard_map/ppermute | solution.py:455
  95.2 2.7 %collective-permute-start.5 = (bf16[256,1152]{1,0:T(8,128)(2,1)S(1)}, bf16[256,1152]{1,0:T(8,128)(2,1)S(1)}, u32[]{:S(2)}, u32[]{:S(2)}) collective-permute-start(bf16[256,1152]{1,0:T(8,128)(2,1)S(1)} %slice.37), channel_id=1, source_target_pairs={{0,6},{1,7},{2,0},{3,1},{4,2},{5,3},{6,4},{7,5},{8,14},{9,15},{10,... | collective-permute-start | bytes 1769480 | tf_op jit(solution)/shard_map/ppermute | solution.py:455
  99.2 8.5 %second.1 = (f32[8,512,128]{2,1,0:T(8,128)S(1)}, f32[8,512,128]{2,1,0:T(8,128)S(1)}, bf16[8,512,512]{2,1,0:T(8,128)(2,1)S(1)}) custom-call(s32[8]{0:T(128)S(1)} %copy-done.9, s32[8]{0:T(128)S(1)} %stack.44.shares_ref, bf16[8,512,768]{2,1,0:T(8,128)(2,1)S(1)} %copy-done.1, ...), custom_call_target="tpu_custom_call", output_to_operand_aliasing={{0}: (3, {}), {1}: (4, {}), {2}: (5, {})} | custom-call | flops 4563402752 | bytes 16777216 | tf_op jit(solution)/shard_map/second/pallas_call | solution.py:375
  107.7 3.1 %collective-permute-done.4.refs_3_ = bf16[256,1152]{1,0:T(8,128)(2,1)S(1)} collective-permute-done((bf16[256,1152]{1,0:T(8,128)(2,1)S(1)}, bf16[256,1152]{1,0:T(8,128)(2,1)S(1)}, u32[]{:S(2)}, u32[]{:S(2)}) %collective-permute-start.4) | collective-permute-done | bytes 589856 | tf_op jit(solution)/shard_map/ppermute | solution.py:455
  110.8 1.4 %collective-permute-start.8 = (bf16[256,1152]{1,0:T(8,128)(2,1)S(1)}, bf16[256,1152]{1,0:T(8,128)(2,1)S(1)}, u32[]{:S(2)}, u32[]{:S(2)}) collective-permute-start(bf16[256,1152]{1,0:T(8,128)(2,1)S(1)} %collective-permute-done.4.refs_3_), channel_id=1, source_target_pairs={{0,1},{1,0},{2,3},{3,2},{4,5},{5,4},{6,7},{7,6},{8,9},{9,8},{10,11... | collective-permute-start | bytes 1769480 | tf_op jit(solution)/shard_map/ppermute | solution.py:455
  112.2 1.6 %collective-permute-done.8.refs_5_ = bf16[256,1152]{1,0:T(8,128)(2,1)S(1)} collective-permute-done((bf16[256,1152]{1,0:T(8,128)(2,1)S(1)}, bf16[256,1152]{1,0:T(8,128)(2,1)S(1)}, u32[]{:S(2)}, u32[]{:S(2)}) %collective-permute-start.8) | collective-permute-done | bytes 589856 | tf_op jit(solution)/shard_map/ppermute | solution.py:455
  114.7 7.9 %third.1 = bf16[512,1024]{1,0:T(8,128)(2,1)} custom-call(s32[8]{0:T(128)S(1)} %copy-done.9, s32[8]{0:T(128)S(1)} %stack.44.shares_ref, bf16[8,512,768]{2,1,0:T(8,128)(2,1)S(1)} %copy-done.1, f32[8,512,128]{2,1,0:T(8,128)S(1)} %get-tuple-element.44.refs_0_, f32[8,512,128]{2,1,0:T(8,128)S(1)} %get-tuple-element.45.refs_1_, ...), custom_call_target="tpu_custom_call" | custom-call | flops 2281701376 | bytes 16777216 | tf_op jit(solution)/shard_map/third/pallas_call | solution.py:375
  (71 shorter events, 16.4 us)
Async XLA Ops:
  0.0 1.9 %copy-start.18 = (s32[8,16]{1,0:T(8,128)S(1)}, s32[8,16]{1,0:T(8,128)}, u32[]{:S(2)}) copy-start(s32[8,16]{1,0:T(8,128)} %param.15) | copy-start | bytes 1540
  0.0 1.8 %copy-start.16 = (bf16[24,576]{1,0:T(8,128)(2,1)S(1)}, bf16[24,576]{1,0:T(8,128)(2,1)}, u32[]{:S(2)}) copy-start(bf16[24,576]{1,0:T(8,128)(2,1)} %param.17) | copy-start | bytes 82948
  17.2 2.9 %copy-start.14 = (bf16[16,64,128]{2,1,0:T(8,128)(2,1)}, bf16[16,64,128]{2,1,0:T(8,128)(2,1)S(1)}, u32[]{:S(2)}) copy-start(bf16[16,64,128]{2,1,0:T(8,128)(2,1)S(1)} %all_to_all.10) | copy-start | bytes 786436
  20.1 41.9 %all-to-all-start.1 = ((bf16[128,8,1152]{2,1,0:T(8,128)(2,1)}), bf16[128,8,1152]{2,1,0:T(8,128)(2,1)S(1)}, u32[]{:S(2)}, u32[]{:S(2)}) async-start(bf16[128,8,1152]{2,1,0:T(8,128)(2,1)} %bitcast.20), calls=%async_computation.1 | async-start | bytes 4718592 | tf_op jit(solution)/shard_map/all_to_all | solution.py:441
  28.7 4.8 %copy-start.17 = (s32[8,64]{1,0:T(8,128)S(1)}, s32[8,64]{1,0:T(8,128)}, u32[]{:S(2)}) copy-start(s32[8,64]{1,0:T(8,128)} %param.19) | copy-start | bytes 6148
  28.7 5.6 %copy-start.3 = (bf16[512,1024]{1,0:T(8,128)(2,1)S(1)}, bf16[512,1024]{1,0:T(8,128)(2,1)}, u32[]{:S(2)}) copy-start(bf16[512,1024]{1,0:T(8,128)(2,1)} %rows_ref.1) | copy-start | bytes 3145732
  34.3 1.2 copy-start.4
  37.6 11.9 %copy-start.15 = (bf16[16,64,128]{2,1,0:T(8,128)(2,1)S(1)}, bf16[16,64,128]{2,1,0:T(8,128)(2,1)}, u32[]{:S(2)}) copy-start(bf16[16,64,128]{2,1,0:T(8,128)(2,1)} %copy-done.14) | copy-start | bytes 786436
  45.3 2.6 %copy-start = (bf16[8,512,768]{2,1,0:T(8,128)(2,1)}, bf16[8,512,768]{2,1,0:T(8,128)(2,1)S(1)}, u32[]{:S(2)}) copy-start(bf16[8,512,768]{2,1,0:T(8,128)(2,1)S(1)} %get-tuple-element.27.q_ref) | copy-start | bytes 18874372
  53.6 18.8 %copy-start.9 = (s32[8]{0:T(128)S(1)}, s32[8]{0:T(128)}, u32[]{:S(2)}) copy-start(s32[8]{0:T(128)} %lengths_ref.5) | copy-start | bytes 100
  64.2 3.9 %collective-permute-start.2 = (bf16[512,1152]{1,0:T(8,128)(2,1)S(1)}, bf16[512,1152]{1,0:T(8,128)(2,1)S(1)}, u32[]{:S(2)}, u32[]{:S(2)}) collective-permute-start(bf16[512,1152]{1,0:T(8,128)(2,1)S(1)} %bitcast.15), channel_id=1, source_target_pairs={{0,1},{1,0},{2,3},{3,2},{4,5},{5,4},{6,7},{7,6},{8,9},{9,8},{10,11... | collective-permute-start | bytes 3538952 | tf_op jit(solution)/shard_map/ppermute | solution.py:455
  65.4 28.7 %collective-permute-start = (bf16[512,1152]{1,0:T(8,128)(2,1)S(1)}, bf16[512,1152]{1,0:T(8,128)(2,1)S(1)}, u32[]{:S(2)}, u32[]{:S(2)}) collective-permute-start(bf16[512,1152]{1,0:T(8,128)(2,1)S(1)} %bitcast.16), channel_id=1, source_target_pairs={{0,2},{1,3},{2,4},{3,5},{4,6},{5,7},{6,0},{7,1},{8,10},{9,11},{10,... | collective-permute-start | bytes 3538952 | tf_op jit(solution)/shard_map/ppermute | solution.py:455
  65.4 28.7 %collective-permute-start.1 = (bf16[512,1152]{1,0:T(8,128)(2,1)S(1)}, bf16[512,1152]{1,0:T(8,128)(2,1)S(1)}, u32[]{:S(2)}, u32[]{:S(2)}) collective-permute-start(bf16[512,1152]{1,0:T(8,128)(2,1)S(1)} %bitcast.17), channel_id=1, source_target_pairs={{0,6},{1,7},{2,0},{3,1},{4,2},{5,3},{6,4},{7,5},{8,14},{9,15},{10,... | collective-permute-start | bytes 3538952 | tf_op jit(solution)/shard_map/ppermute | solution.py:455
  69.1 2.1 %collective-permute-start.3 = (bf16[192,576]{1,0:T(8,128)(2,1)}, bf16[192,576]{1,0:T(8,128)(2,1)}, u32[]{:S(2)}, u32[]{:S(2)}) collective-permute-start(bf16[192,576]{1,0:T(8,128)(2,1)} %reshape.108), channel_id=1, source_target_pairs={{0,1},{1,0},{2,3},{3,2},{4,5},{5,4},{6,7},{7,6},{8,9},{9,8},{10,11... | collective-permute-start | bytes 663560 | tf_op jit(solution)/shard_map/ppermute | solution.py:455
  72.4 2.8 %copy-start.1 = (bf16[8,512,768]{2,1,0:T(8,128)(2,1)S(1)}, bf16[8,512,768]{2,1,0:T(8,128)(2,1)}, u32[]{:S(2)}) copy-start(bf16[8,512,768]{2,1,0:T(8,128)(2,1)} %copy-done) | copy-start | bytes 18874372
  75.1 1.1 copy-start.7
  76.2 1.3 %copy-start.11 = (bf16[512,1152]{1,0:T(8,128)(2,1)S(1)}, bf16[512,1152]{1,0:T(8,128)(2,1)}, u32[]{:S(2)}) copy-start(bf16[512,1152]{1,0:T(8,128)(2,1)} %copy-done.10) | copy-start | bytes 3538948
  94.2 3.8 %collective-permute-start.6 = (bf16[512,1152]{1,0:T(8,128)(2,1)S(1)}, bf16[512,1152]{1,0:T(8,128)(2,1)S(1)}, u32[]{:S(2)}, u32[]{:S(2)}) collective-permute-start(bf16[512,1152]{1,0:T(8,128)(2,1)S(1)} %collective-permute-done.refs_3_), channel_id=1, source_target_pairs={{0,1},{1,0},{2,3},{3,2},{4,5},{5,4},{6,7},{7,6},{8,9},{9,8},{10,11... | collective-permute-start | bytes 3538952 | tf_op jit(solution)/shard_map/ppermute | solution.py:455
  95.0 4.2 %collective-permute-start.7 = (bf16[512,1152]{1,0:T(8,128)(2,1)S(1)}, bf16[512,1152]{1,0:T(8,128)(2,1)S(1)}, u32[]{:S(2)}, u32[]{:S(2)}) collective-permute-start(bf16[512,1152]{1,0:T(8,128)(2,1)S(1)} %collective-permute-done.1.refs_4_), channel_id=1, source_target_pairs={{0,1},{1,0},{2,3},{3,2},{4,5},{5,4},{6,7},{7,6},{8,9},{9,8},{10,11... | collective-permute-start | bytes 3538952 | tf_op jit(solution)/shard_map/ppermute | solution.py:455
  95.1 19.5 %copy-start.2 = (bf16[8,512,128]{2,1,0:T(8,128)(2,1)S(1)}, bf16[8,512,128]{2,1,0:T(8,128)(2,1)}, u32[]{:S(2)}) copy-start(bf16[8,512,128]{2,1,0:T(8,128)(2,1)} %refs_7_.1) | copy-start | bytes 3145732
  95.2 15.7 %collective-permute-start.4 = (bf16[256,1152]{1,0:T(8,128)(2,1)S(1)}, bf16[256,1152]{1,0:T(8,128)(2,1)S(1)}, u32[]{:S(2)}, u32[]{:S(2)}) collective-permute-start(bf16[256,1152]{1,0:T(8,128)(2,1)S(1)} %slice.36), channel_id=1, source_target_pairs={{0,2},{1,3},{2,4},{3,5},{4,6},{5,7},{6,0},{7,1},{8,10},{9,11},{10,... | collective-permute-start | bytes 1769480 | tf_op jit(solution)/shard_map/ppermute | solution.py:455
  95.2 15.6 %collective-permute-start.5 = (bf16[256,1152]{1,0:T(8,128)(2,1)S(1)}, bf16[256,1152]{1,0:T(8,128)(2,1)S(1)}, u32[]{:S(2)}, u32[]{:S(2)}) collective-permute-start(bf16[256,1152]{1,0:T(8,128)(2,1)S(1)} %slice.37), channel_id=1, source_target_pairs={{0,6},{1,7},{2,0},{3,1},{4,2},{5,3},{6,4},{7,5},{8,14},{9,15},{10,... | collective-permute-start | bytes 1769480 | tf_op jit(solution)/shard_map/ppermute | solution.py:455
  110.8 3.0 %collective-permute-start.8 = (bf16[256,1152]{1,0:T(8,128)(2,1)S(1)}, bf16[256,1152]{1,0:T(8,128)(2,1)S(1)}, u32[]{:S(2)}, u32[]{:S(2)}) collective-permute-start(bf16[256,1152]{1,0:T(8,128)(2,1)S(1)} %collective-permute-done.4.refs_3_), channel_id=1, source_target_pairs={{0,1},{1,0},{2,3},{3,2},{4,5},{5,4},{6,7},{7,6},{8,9},{9,8},{10,11... | collective-permute-start | bytes 1769480 | tf_op jit(solution)/shard_map/ppermute | solution.py:455
  112.2 2.5 %collective-permute-start.9 = (bf16[256,1152]{1,0:T(8,128)(2,1)S(1)}, bf16[256,1152]{1,0:T(8,128)(2,1)S(1)}, u32[]{:S(2)}, u32[]{:S(2)}) collective-permute-start(bf16[256,1152]{1,0:T(8,128)(2,1)S(1)} %collective-permute-done.5.refs_4_), channel_id=1, source_target_pairs={{0,1},{1,0},{2,3},{3,2},{4,5},{5,4},{6,7},{7,6},{8,9},{9,8},{10,11... | collective-permute-start | bytes 1769480 | tf_op jit(solution)/shard_map/ppermute | solution.py:455
  (6 other events, 5.5 us)

commit v7 on v6

--- a/solution.py
+++ b/solution.py
@@ -121,7 +121,7 @@
 def pack(wanted, pool, shares):
     groups = wanted.shape[0]
     size, width = pool.shape[1:]
-    steps = 4
+    steps = 2
     packed = pl.pallas_call(
         pack_kernel,
         grid=(steps,),
@@ -161,7 +161,7 @@
         out_ref[k, :, 2 * latent :] = jnp.where(lane < half, ropes[0], ropes[1]).astype(BF16)
         return carry
 
-    lax.fori_loop(0, pairs, body, 0, unroll=4)
+    lax.fori_loop(0, pairs, body, 0, unroll=16)
 
 
 def compact(source, slot, got, after):

time: 123 us -> 122 us (level)
  Pallas kernels: 41.8 us -> 40.5 us
where the time goes in v7:
time: 122 us; the launch traced here: 121 us
  Pallas kernels  40.5 us (33%)
  local copies, waits for them, and re-layouts  24.3 us (20%)
  waiting for transfers between devices  19.7 us (16%)
  starting transfers between devices  18.2 us (15%)
  blocking collectives  14.8 us (12%)
  between operations  2.15 us (2%)
  other arithmetic  1.56 us (1%)
    pallas_call x3, Pallas kernels, attend(): pl.pallas_call(functools.partial(attend_kernel, scale, picks, shared, hal...  29 us
    unnamed x40, local copies, waits for them, and re-layouts  18.5 us
    all_to_all x1, blocking collectives, local(): lax.all_to_all(message, 'decode', split_axis=0, concat_axis=0, tiled=True)  14.8 us
    ppermute x10, waiting for transfers between devices, turn(): return lax.ppermute(array, 'pool', pairs)  11.3 us
    ppermute x10, starting transfers between devices, turn(): return lax.ppermute(array, 'pool', pairs)  9.61 us
    all_to_all x1, starting transfers between devices, local(): lax.all_to_all(packed, ('decode', 'pool'), split_axis=0, concat_axis=0, t...  8.6 us
    all_to_all x1, waiting for transfers between devices, local(): lax.all_to_all(packed, ('decode', 'pool'), split_axis=0, concat_axis=0, t...  8.4 us
    pallas_call x1, Pallas kernels, prepare(): pl.pallas_call(prepare_kernel, grid=(heads,), in_specs=[pl.BlockSpec((row...  7.76 us
  transfers between devices with their start and end apart: 11, of which 7 were waited for; matrix products, arithmetic and copies ran while one was open for 7% of the time, Pallas kernels for 24%

profile of v7, /device:TPU:1, one launch (start us, length us, event | category | flops | bytes accessed | tf_op | source)
XLA Modules:
  0.0 121.3 jit_solution(7944371877199885262)
XLA Ops:
  0.0 1.8 %copy.53.pool_ref = bf16[32,64,576]{2,1,0:T(8,128)(2,1)S(1)} copy(bf16[32,64,576]{2,1,0:T(8,128)(2,1)} %param.14) | data formatting | bytes 4718592
  2.4 14.8 %all_to_all.10 = bf16[16,64,128]{2,1,0:T(8,128)(2,1)S(1)} all-to-all(bf16[16,64,128]{2,1,0:T(8,128)(2,1)S(1)} %get-tuple-element.28), channel_id=1, replica_groups=mesh['decode'=16,'pool'=8] {'decode'}, dimensions={0} | all-to-all | bytes 524288 | tf_op jit(solution)/shard_map/all_to_all | solution.py:432
  17.2 2.3 %pack.1 = bf16[1024,1152]{1,0:T(8,128)(2,1)} custom-call(s32[16,2]{1,0:T(8,128)S(1)} %bitcast.19, bf16[32,64,576]{2,1,0:T(8,128)(2,1)S(1)} %get-tuple-element.29.pool_ref), custom_call_target="tpu_custom_call" | custom-call | bytes 5000000 | tf_op jit(solution)/shard_map/pack/pallas_call | solution.py:125
  19.5 8.6 %all-to-all-start.1 = ((bf16[128,8,1152]{2,1,0:T(8,128)(2,1)}), bf16[128,8,1152]{2,1,0:T(8,128)(2,1)S(1)}, u32[]{:S(2)}, u32[]{:S(2)}) async-start(bf16[128,8,1152]{2,1,0:T(8,128)(2,1)} %bitcast.20), calls=%async_computation.1 | async-start | bytes 4718592 | tf_op jit(solution)/shard_map/all_to_all | solution.py:441
  28.2 2.2 %copy.46 = bf16[512,576]{1,0:T(8,128)(2,1)} copy(bf16[512,576]{0,1:T(8,128)(2,1)} %param.18) | data formatting | bytes 1179648 | tf_op args[8]
  33.8 1.2 %copy-done.4 = bf16[8,128,512]{2,1,0:T(8,128)(2,1)S(1)} copy-done((bf16[8,128,512]{2,1,0:T(8,128)(2,1)S(1)}, bf16[8,128,512]{2,1,0:T(8,128)(2,1)}, u32[]{:S(2)}) %copy-start.4) | copy-done | bytes 1048600
  37.0 7.8 %prepare.1 = (bf16[8,512,768]{2,1,0:T(8,128)(2,1)S(1)}, f32[8,64,128]{2,1,0:T(8,128)S(1)}) custom-call(bf16[512,1024]{1,0:T(8,128)(2,1)S(1)} %copy-done.3, bf16[512,512]{1,0:T(8,128)(2,1)S(1)} %copy-done.8, bf16[8,128,512]{2,1,0:T(8,128)(2,1)S(1)} %copy-done.4, s32[8,64,1]{2,1,0:T(8,128)S(1)} %copy-done.5), custom_call_target="tpu_custom_call" | custom-call | flops 536870912 | bytes 10000000 | tf_op jit(solution)/shard_map/prepare/pallas_call | solution.py:52
  44.8 2.6 %copy-done = bf16[8,512,768]{2,1,0:T(8,128)(2,1)} copy-done((bf16[8,512,768]{2,1,0:T(8,128)(2,1)}, bf16[8,512,768]{2,1,0:T(8,128)(2,1)S(1)}, u32[]{:S(2)}) %copy-start) | copy-done | bytes 6291480
  49.9 1.2 %slice.40 = bf16[1,1]{1,0:T(2,128)(2,1)} slice(bf16[192,576]{1,0:T(8,128)(2,1)} %reshape.108), slice={[0:1], [0:1]} | slice | bytes 4 | tf_op jit(solution)/shard_map/slice | solution.py:444
  53.0 8.4 %all-to-all-done.1.got_ref = bf16[128,8,1152]{2,1,0:T(8,128)(2,1)S(1)} async-done(((bf16[128,8,1152]{2,1,0:T(8,128)(2,1)}), bf16[128,8,1152]{2,1,0:T(8,128)(2,1)S(1)}, u32[]{:S(2)}, u32[]{:S(2)}) %all-to-all-start.1) | async-done | bytes 2359328 | tf_op jit(solution)/shard_map/all_to_all | solution.py:441
  61.5 1.4 %compact.1 = bf16[64,8,1152]{2,1,0:T(8,128)(2,1)S(1)} custom-call(s32[128]{0:T(128)S(1)} %get-tuple-element.52.source_ref, s32[128]{0:T(128)S(1)} %convert_element_type.22.slot_ref, bf16[128,8,1152]{2,1,0:T(8,128)(2,1)S(1)} %all-to-all-done.1.got_ref, f32[1,1]{1,0:T(1,128)S(6)} %add.122.after_ref), custom_call_target="tpu_custom_call" | custom-call | bytes 4000000 | tf_op jit(solution)/shard_map/compact/pallas_call | solution.py:169
  62.9 1.2 %collective-permute-start.2 = (bf16[512,1152]{1,0:T(8,128)(2,1)S(1)}, bf16[512,1152]{1,0:T(8,128)(2,1)S(1)}, u32[]{:S(2)}, u32[]{:S(2)}) collective-permute-start(bf16[512,1152]{1,0:T(8,128)(2,1)S(1)} %bitcast.15), channel_id=1, source_target_pairs={{0,1},{1,0},{2,3},{3,2},{4,5},{5,4},{6,7},{7,6},{8,9},{9,8},{10,11... | collective-permute-start | bytes 3538952 | tf_op jit(solution)/shard_map/ppermute | solution.py:455
  64.2 2.7 %collective-permute-start.1 = (bf16[512,1152]{1,0:T(8,128)(2,1)S(1)}, bf16[512,1152]{1,0:T(8,128)(2,1)S(1)}, u32[]{:S(2)}, u32[]{:S(2)}) collective-permute-start(bf16[512,1152]{1,0:T(8,128)(2,1)S(1)} %bitcast.17), channel_id=1, source_target_pairs={{0,6},{1,7},{2,0},{3,1},{4,2},{5,3},{6,4},{7,5},{8,14},{9,15},{10,... | collective-permute-start | bytes 3538952 | tf_op jit(solution)/shard_map/ppermute | solution.py:455
  68.6 1.4 %collective-permute-done.3 = bf16[192,576]{1,0:T(8,128)(2,1)} collective-permute-done((bf16[192,576]{1,0:T(8,128)(2,1)}, bf16[192,576]{1,0:T(8,128)(2,1)}, u32[]{:S(2)}, u32[]{:S(2)}) %collective-permute-start.3) | collective-permute-done | bytes 221216 | tf_op jit(solution)/shard_map/ppermute | solution.py:455
  71.1 2.8 %copy-done.1 = bf16[8,512,768]{2,1,0:T(8,128)(2,1)S(1)} copy-done((bf16[8,512,768]{2,1,0:T(8,128)(2,1)S(1)}, bf16[8,512,768]{2,1,0:T(8,128)(2,1)}, u32[]{:S(2)}) %copy-start.1) | copy-done | bytes 6291480
  75.0 1.3 %copy-done.11 = bf16[512,1152]{1,0:T(8,128)(2,1)S(1)} copy-done((bf16[512,1152]{1,0:T(8,128)(2,1)S(1)}, bf16[512,1152]{1,0:T(8,128)(2,1)}, u32[]{:S(2)}) %copy-start.11) | copy-done | bytes 1179672
  77.2 12.6 %first.1 = (f32[8,512,128]{2,1,0:T(8,128)S(1)}, f32[8,512,128]{2,1,0:T(8,128)S(1)}, bf16[8,512,512]{2,1,0:T(8,128)(2,1)S(1)}) custom-call(s32[8]{0:T(128)S(1)} %copy-done.9, s32[8]{0:T(128)S(1)} %stack.44.shares_ref, bf16[8,512,768]{2,1,0:T(8,128)(2,1)S(1)} %copy-done.1, bf16[384,640]{1,0:T(8,128)(2,1)S(1)} %fusion.2.refs_0_, ...), custom_call_target="tpu_custom_call" | custom-call | flops 6845104128 | bytes 16777216 | tf_op jit(solution)/shard_map/first/pallas_call | solution.py:375
  89.7 3.1 %collective-permute-done.refs_3_ = bf16[512,1152]{1,0:T(8,128)(2,1)S(1)} collective-permute-done((bf16[512,1152]{1,0:T(8,128)(2,1)S(1)}, bf16[512,1152]{1,0:T(8,128)(2,1)S(1)}, u32[]{:S(2)}, u32[]{:S(2)}) %collective-permute-start) | collective-permute-done | bytes 1179680 | tf_op jit(solution)/shard_map/ppermute | solution.py:455
  94.0 2.7 %collective-permute-start.5 = (bf16[256,1152]{1,0:T(8,128)(2,1)S(1)}, bf16[256,1152]{1,0:T(8,128)(2,1)S(1)}, u32[]{:S(2)}, u32[]{:S(2)}) collective-permute-start(bf16[256,1152]{1,0:T(8,128)(2,1)S(1)} %slice.37), channel_id=1, source_target_pairs={{0,6},{1,7},{2,0},{3,1},{4,2},{5,3},{6,4},{7,5},{8,14},{9,15},{10,... | collective-permute-start | bytes 1769480 | tf_op jit(solution)/shard_map/ppermute | solution.py:455
  97.9 8.5 %second.1 = (f32[8,512,128]{2,1,0:T(8,128)S(1)}, f32[8,512,128]{2,1,0:T(8,128)S(1)}, bf16[8,512,512]{2,1,0:T(8,128)(2,1)S(1)}) custom-call(s32[8]{0:T(128)S(1)} %copy-done.9, s32[8]{0:T(128)S(1)} %stack.44.shares_ref, bf16[8,512,768]{2,1,0:T(8,128)(2,1)S(1)} %copy-done.1, ...), custom_call_target="tpu_custom_call", output_to_operand_aliasing={{0}: (3, {}), {1}: (4, {}), {2}: (5, {})} | custom-call | flops 4563402752 | bytes 16777216 | tf_op jit(solution)/shard_map/second/pallas_call | solution.py:375
  106.4 3.1 %collective-permute-done.4.refs_3_ = bf16[256,1152]{1,0:T(8,128)(2,1)S(1)} collective-permute-done((bf16[256,1152]{1,0:T(8,128)(2,1)S(1)}, bf16[256,1152]{1,0:T(8,128)(2,1)S(1)}, u32[]{:S(2)}, u32[]{:S(2)}) %collective-permute-start.4) | collective-permute-done | bytes 589856 | tf_op jit(solution)/shard_map/ppermute | solution.py:455
  109.5 1.4 %collective-permute-start.8 = (bf16[256,1152]{1,0:T(8,128)(2,1)S(1)}, bf16[256,1152]{1,0:T(8,128)(2,1)S(1)}, u32[]{:S(2)}, u32[]{:S(2)}) collective-permute-start(bf16[256,1152]{1,0:T(8,128)(2,1)S(1)} %collective-permute-done.4.refs_3_), channel_id=1, source_target_pairs={{0,1},{1,0},{2,3},{3,2},{4,5},{5,4},{6,7},{7,6},{8,9},{9,8},{10,11... | collective-permute-start | bytes 1769480 | tf_op jit(solution)/shard_map/ppermute | solution.py:455
  110.9 1.6 %collective-permute-done.8.refs_5_ = bf16[256,1152]{1,0:T(8,128)(2,1)S(1)} collective-permute-done((bf16[256,1152]{1,0:T(8,128)(2,1)S(1)}, bf16[256,1152]{1,0:T(8,128)(2,1)S(1)}, u32[]{:S(2)}, u32[]{:S(2)}) %collective-permute-start.8) | collective-permute-done | bytes 589856 | tf_op jit(solution)/shard_map/ppermute | solution.py:455
  113.4 7.9 %third.1 = bf16[512,1024]{1,0:T(8,128)(2,1)} custom-call(s32[8]{0:T(128)S(1)} %copy-done.9, s32[8]{0:T(128)S(1)} %stack.44.shares_ref, bf16[8,512,768]{2,1,0:T(8,128)(2,1)S(1)} %copy-done.1, f32[8,512,128]{2,1,0:T(8,128)S(1)} %get-tuple-element.44.refs_0_, f32[8,512,128]{2,1,0:T(8,128)S(1)} %get-tuple-element.45.refs_1_, ...), custom_call_target="tpu_custom_call" | custom-call | flops 2281701376 | bytes 16777216 | tf_op jit(solution)/shard_map/third/pallas_call | solution.py:375
  (71 shorter events, 16.4 us)
Async XLA Ops:
  0.0 1.9 %copy-start.18 = (s32[8,16]{1,0:T(8,128)S(1)}, s32[8,16]{1,0:T(8,128)}, u32[]{:S(2)}) copy-start(s32[8,16]{1,0:T(8,128)} %param.15) | copy-start | bytes 1540
  0.0 1.8 %copy-start.16 = (bf16[24,576]{1,0:T(8,128)(2,1)S(1)}, bf16[24,576]{1,0:T(8,128)(2,1)}, u32[]{:S(2)}) copy-start(bf16[24,576]{1,0:T(8,128)(2,1)} %param.17) | copy-start | bytes 82948
  17.2 2.3 %copy-start.14 = (bf16[16,64,128]{2,1,0:T(8,128)(2,1)}, bf16[16,64,128]{2,1,0:T(8,128)(2,1)S(1)}, u32[]{:S(2)}) copy-start(bf16[16,64,128]{2,1,0:T(8,128)(2,1)S(1)} %all_to_all.10) | copy-start | bytes 786436
  19.5 41.9 %all-to-all-start.1 = ((bf16[128,8,1152]{2,1,0:T(8,128)(2,1)}), bf16[128,8,1152]{2,1,0:T(8,128)(2,1)S(1)}, u32[]{:S(2)}, u32[]{:S(2)}) async-start(bf16[128,8,1152]{2,1,0:T(8,128)(2,1)} %bitcast.20), calls=%async_computation.1 | async-start | bytes 4718592 | tf_op jit(solution)/shard_map/all_to_all | solution.py:441
  28.1 4.8 %copy-start.17 = (s32[8,64]{1,0:T(8,128)S(1)}, s32[8,64]{1,0:T(8,128)}, u32[]{:S(2)}) copy-start(s32[8,64]{1,0:T(8,128)} %param.19) | copy-start | bytes 6148
  28.1 5.6 %copy-start.3 = (bf16[512,1024]{1,0:T(8,128)(2,1)S(1)}, bf16[512,1024]{1,0:T(8,128)(2,1)}, u32[]{:S(2)}) copy-start(bf16[512,1024]{1,0:T(8,128)(2,1)} %rows_ref.1) | copy-start | bytes 3145732
  33.8 1.2 %copy-start.4 = (bf16[8,128,512]{2,1,0:T(8,128)(2,1)S(1)}, bf16[8,128,512]{2,1,0:T(8,128)(2,1)}, u32[]{:S(2)}) copy-start(bf16[8,128,512]{2,1,0:T(8,128)(2,1)} %keys_ref.1) | copy-start | bytes 3145732
  37.0 11.9 %copy-start.15 = (bf16[16,64,128]{2,1,0:T(8,128)(2,1)S(1)}, bf16[16,64,128]{2,1,0:T(8,128)(2,1)}, u32[]{:S(2)}) copy-start(bf16[16,64,128]{2,1,0:T(8,128)(2,1)} %copy-done.14) | copy-start | bytes 786436
  44.8 2.6 %copy-start = (bf16[8,512,768]{2,1,0:T(8,128)(2,1)}, bf16[8,512,768]{2,1,0:T(8,128)(2,1)S(1)}, u32[]{:S(2)}) copy-start(bf16[8,512,768]{2,1,0:T(8,128)(2,1)S(1)} %get-tuple-element.27.q_ref) | copy-start | bytes 18874372
  53.0 18.0 %copy-start.9 = (s32[8]{0:T(128)S(1)}, s32[8]{0:T(128)}, u32[]{:S(2)}) copy-start(s32[8]{0:T(128)} %lengths_ref.5) | copy-start | bytes 100
  62.9 3.9 %collective-permute-start.2 = (bf16[512,1152]{1,0:T(8,128)(2,1)S(1)}, bf16[512,1152]{1,0:T(8,128)(2,1)S(1)}, u32[]{:S(2)}, u32[]{:S(2)}) collective-permute-start(bf16[512,1152]{1,0:T(8,128)(2,1)S(1)} %bitcast.15), channel_id=1, source_target_pairs={{0,1},{1,0},{2,3},{3,2},{4,5},{5,4},{6,7},{7,6},{8,9},{9,8},{10,11... | collective-permute-start | bytes 3538952 | tf_op jit(solution)/shard_map/ppermute | solution.py:455
  64.1 28.7 %collective-permute-start = (bf16[512,1152]{1,0:T(8,128)(2,1)S(1)}, bf16[512,1152]{1,0:T(8,128)(2,1)S(1)}, u32[]{:S(2)}, u32[]{:S(2)}) collective-permute-start(bf16[512,1152]{1,0:T(8,128)(2,1)S(1)} %bitcast.16), channel_id=1, source_target_pairs={{0,2},{1,3},{2,4},{3,5},{4,6},{5,7},{6,0},{7,1},{8,10},{9,11},{10,... | collective-permute-start | bytes 3538952 | tf_op jit(solution)/shard_map/ppermute | solution.py:455
  64.2 28.7 %collective-permute-start.1 = (bf16[512,1152]{1,0:T(8,128)(2,1)S(1)}, bf16[512,1152]{1,0:T(8,128)(2,1)S(1)}, u32[]{:S(2)}, u32[]{:S(2)}) collective-permute-start(bf16[512,1152]{1,0:T(8,128)(2,1)S(1)} %bitcast.17), channel_id=1, source_target_pairs={{0,6},{1,7},{2,0},{3,1},{4,2},{5,3},{6,4},{7,5},{8,14},{9,15},{10,... | collective-permute-start | bytes 3538952 | tf_op jit(solution)/shard_map/ppermute | solution.py:455
  67.8 2.1 %collective-permute-start.3 = (bf16[192,576]{1,0:T(8,128)(2,1)}, bf16[192,576]{1,0:T(8,128)(2,1)}, u32[]{:S(2)}, u32[]{:S(2)}) collective-permute-start(bf16[192,576]{1,0:T(8,128)(2,1)} %reshape.108), channel_id=1, source_target_pairs={{0,1},{1,0},{2,3},{3,2},{4,5},{5,4},{6,7},{7,6},{8,9},{9,8},{10,11... | collective-permute-start | bytes 663560 | tf_op jit(solution)/shard_map/ppermute | solution.py:455
  71.1 2.8 %copy-start.1 = (bf16[8,512,768]{2,1,0:T(8,128)(2,1)S(1)}, bf16[8,512,768]{2,1,0:T(8,128)(2,1)}, u32[]{:S(2)}) copy-start(bf16[8,512,768]{2,1,0:T(8,128)(2,1)} %copy-done) | copy-start | bytes 18874372
  73.9 1.1 copy-start.7
  75.0 1.3 %copy-start.11 = (bf16[512,1152]{1,0:T(8,128)(2,1)S(1)}, bf16[512,1152]{1,0:T(8,128)(2,1)}, u32[]{:S(2)}) copy-start(bf16[512,1152]{1,0:T(8,128)(2,1)} %copy-done.10) | copy-start | bytes 3538948
  92.9 3.8 %collective-permute-start.6 = (bf16[512,1152]{1,0:T(8,128)(2,1)S(1)}, bf16[512,1152]{1,0:T(8,128)(2,1)S(1)}, u32[]{:S(2)}, u32[]{:S(2)}) collective-permute-start(bf16[512,1152]{1,0:T(8,128)(2,1)S(1)} %collective-permute-done.refs_3_), channel_id=1, source_target_pairs={{0,1},{1,0},{2,3},{3,2},{4,5},{5,4},{6,7},{7,6},{8,9},{9,8},{10,11... | collective-permute-start | bytes 3538952 | tf_op jit(solution)/shard_map/ppermute | solution.py:455
  93.8 4.2 %collective-permute-start.7 = (bf16[512,1152]{1,0:T(8,128)(2,1)S(1)}, bf16[512,1152]{1,0:T(8,128)(2,1)S(1)}, u32[]{:S(2)}, u32[]{:S(2)}) collective-permute-start(bf16[512,1152]{1,0:T(8,128)(2,1)S(1)} %collective-permute-done.1.refs_4_), channel_id=1, source_target_pairs={{0,1},{1,0},{2,3},{3,2},{4,5},{5,4},{6,7},{7,6},{8,9},{9,8},{10,11... | collective-permute-start | bytes 3538952 | tf_op jit(solution)/shard_map/ppermute | solution.py:455
  93.9 19.5 %copy-start.2 = (bf16[8,512,128]{2,1,0:T(8,128)(2,1)S(1)}, bf16[8,512,128]{2,1,0:T(8,128)(2,1)}, u32[]{:S(2)}) copy-start(bf16[8,512,128]{2,1,0:T(8,128)(2,1)} %refs_7_.1) | copy-start | bytes 3145732
  93.9 15.7 %collective-permute-start.4 = (bf16[256,1152]{1,0:T(8,128)(2,1)S(1)}, bf16[256,1152]{1,0:T(8,128)(2,1)S(1)}, u32[]{:S(2)}, u32[]{:S(2)}) collective-permute-start(bf16[256,1152]{1,0:T(8,128)(2,1)S(1)} %slice.36), channel_id=1, source_target_pairs={{0,2},{1,3},{2,4},{3,5},{4,6},{5,7},{6,0},{7,1},{8,10},{9,11},{10,... | collective-permute-start | bytes 1769480 | tf_op jit(solution)/shard_map/ppermute | solution.py:455
  94.0 15.6 %collective-permute-start.5 = (bf16[256,1152]{1,0:T(8,128)(2,1)S(1)}, bf16[256,1152]{1,0:T(8,128)(2,1)S(1)}, u32[]{:S(2)}, u32[]{:S(2)}) collective-permute-start(bf16[256,1152]{1,0:T(8,128)(2,1)S(1)} %slice.37), channel_id=1, source_target_pairs={{0,6},{1,7},{2,0},{3,1},{4,2},{5,3},{6,4},{7,5},{8,14},{9,15},{10,... | collective-permute-start | bytes 1769480 | tf_op jit(solution)/shard_map/ppermute | solution.py:455
  109.5 3.0 %collective-permute-start.8 = (bf16[256,1152]{1,0:T(8,128)(2,1)S(1)}, bf16[256,1152]{1,0:T(8,128)(2,1)S(1)}, u32[]{:S(2)}, u32[]{:S(2)}) collective-permute-start(bf16[256,1152]{1,0:T(8,128)(2,1)S(1)} %collective-permute-done.4.refs_3_), channel_id=1, source_target_pairs={{0,1},{1,0},{2,3},{3,2},{4,5},{5,4},{6,7},{7,6},{8,9},{9,8},{10,11... | collective-permute-start | bytes 1769480 | tf_op jit(solution)/shard_map/ppermute | solution.py:455
  110.9 2.5 %collective-permute-start.9 = (bf16[256,1152]{1,0:T(8,128)(2,1)S(1)}, bf16[256,1152]{1,0:T(8,128)(2,1)S(1)}, u32[]{:S(2)}, u32[]{:S(2)}) collective-permute-start(bf16[256,1152]{1,0:T(8,128)(2,1)S(1)} %collective-permute-done.5.refs_4_), channel_id=1, source_target_pairs={{0,1},{1,0},{2,3},{3,2},{4,5},{5,4},{6,7},{7,6},{8,9},{9,8},{10,11... | collective-permute-start | bytes 1769480 | tf_op jit(solution)/shard_map/ppermute | solution.py:455
  (6 other events, 5.5 us)

commit v8 on v7

--- a/solution.py
+++ b/solution.py
@@ -196,7 +196,7 @@
     ]
     values_ref = refs.pop(0) if finish else None
     if finish:
-        out_ref, keys_ref, mixed_ref = refs
+        out_ref, keys_ref, mixed_ref, staged_ref, sems = refs
     else:
         top_out, total_out, sum_out, keys_ref = refs
     heads, total_rows, wide = q_ref.shape
@@ -312,12 +312,20 @@
     if finish:
         value = values_ref.shape[2]
 
+        def leave(head):
+            return pltpu.make_async_copy(
+                staged_ref.at[head], out_ref.at[:, pl.ds(head * value, value)], sems.at[head]
+            )
+
         @pl.when(pl.program_id(0) == pl.num_programs(0) - 1)
         def _():
             for head in range(heads):
-                out_ref[:, head * value : (head + 1) * value] = jnp.dot(
+                staged_ref[head] = jnp.dot(
                     mixed_ref[head], values_ref[head], preferred_element_type=F32
                 ).astype(BF16)
+                leave(head).start()
+            for head in range(heads):
+                leave(head).wait()
 
 
 def attend(name, scale, lengths, shares, picks, q, shared, given, pieces, up_values=None, at_once=1):
@@ -362,9 +370,11 @@
         value = up_values.shape[2]
         operands.append(up_values)
         in_specs.append(whole)
-        out_specs = pl.BlockSpec((total_rows, heads * value), lambda i, *_: (0, 0))
+        out_specs = pl.BlockSpec(memory_space=pltpu.HBM)
         out_shape = jax.ShapeDtypeStruct((total_rows, heads * value), BF16)
-        scratch.append(pltpu.VMEM((heads, total_rows, latent), BF16))
+        staged = pltpu.VMEM((heads, total_rows, value), BF16)
+        scratch += [pltpu.VMEM((heads, total_rows, latent), BF16), staged]
+        scratch.append(pltpu.SemaphoreType.DMA((heads,)))
     else:
         out_specs = state_specs
         out_shape = [

time: 122 us -> 122 us (level)
  no operation moved by 1% of the time
where the time goes in v8:
time: 122 us; the launch traced here: 121 us
  Pallas kernels  40.3 us (33%)
  local copies, waits for them, and re-layouts  24.3 us (20%)
  waiting for transfers between devices  19.7 us (16%)
  starting transfers between devices  18.2 us (15%)
  blocking collectives  14.8 us (12%)
  between operations  2.31 us (2%)
  other arithmetic  1.56 us (1%)
    pallas_call x3, Pallas kernels, attend(): pl.pallas_call(functools.partial(attend_kernel, scale, picks, shared, hal...  28.7 us
    unnamed x40, local copies, waits for them, and re-layouts  18.5 us
    all_to_all x1, blocking collectives, local(): lax.all_to_all(message, 'decode', split_axis=0, concat_axis=0, tiled=True)  14.8 us
    ppermute x10, waiting for transfers between devices, turn(): return lax.ppermute(array, 'pool', pairs)  11.3 us
    ppermute x10, starting transfers between devices, turn(): return lax.ppermute(array, 'pool', pairs)  9.61 us
    all_to_all x1, starting transfers between devices, local(): lax.all_to_all(packed, ('decode', 'pool'), split_axis=0, concat_axis=0, t...  8.6 us
    all_to_all x1, waiting for transfers between devices, local(): lax.all_to_all(packed, ('decode', 'pool'), split_axis=0, concat_axis=0, t...  8.4 us
    pallas_call x1, Pallas kernels, prepare(): pl.pallas_call(prepare_kernel, grid=(heads,), in_specs=[pl.BlockSpec((row...  7.76 us
  transfers between devices with their start and end apart: 11, of which 7 were waited for; matrix products, arithmetic and copies ran while one was open for 7% of the time, Pallas kernels for 24%

profile of v8, /device:TPU:1, one launch (start us, length us, event | category | flops | bytes accessed | tf_op | source)
XLA Modules:
  0.0 121.2 jit_solution(2011713954790394420)
XLA Ops:
  0.0 1.8 %copy.53.pool_ref = bf16[32,64,576]{2,1,0:T(8,128)(2,1)S(1)} copy(bf16[32,64,576]{2,1,0:T(8,128)(2,1)} %param.14) | data formatting | bytes 4718592
  2.4 14.8 %all_to_all.10 = bf16[16,64,128]{2,1,0:T(8,128)(2,1)S(1)} all-to-all(bf16[16,64,128]{2,1,0:T(8,128)(2,1)S(1)} %get-tuple-element.28), channel_id=1, replica_groups=mesh['decode'=16,'pool'=8] {'decode'}, dimensions={0} | all-to-all | bytes 524288 | tf_op jit(solution)/shard_map/all_to_all | solution.py:442
  17.2 2.3 %pack.1 = bf16[1024,1152]{1,0:T(8,128)(2,1)} custom-call(s32[16,2]{1,0:T(8,128)S(1)} %bitcast.19, bf16[32,64,576]{2,1,0:T(8,128)(2,1)S(1)} %get-tuple-element.29.pool_ref), custom_call_target="tpu_custom_call" | custom-call | bytes 5000000 | tf_op jit(solution)/shard_map/pack/pallas_call | solution.py:125
  19.5 8.6 %all-to-all-start.1 = ((bf16[128,8,1152]{2,1,0:T(8,128)(2,1)}), bf16[128,8,1152]{2,1,0:T(8,128)(2,1)S(1)}, u32[]{:S(2)}, u32[]{:S(2)}) async-start(bf16[128,8,1152]{2,1,0:T(8,128)(2,1)} %bitcast.20), calls=%async_computation.1 | async-start | bytes 4718592 | tf_op jit(solution)/shard_map/all_to_all | solution.py:451
  28.2 2.2 %copy.46 = bf16[512,576]{1,0:T(8,128)(2,1)} copy(bf16[512,576]{0,1:T(8,128)(2,1)} %param.18) | data formatting | bytes 1179648 | tf_op args[8]
  33.8 1.2 %copy-done.4 = bf16[8,128,512]{2,1,0:T(8,128)(2,1)S(1)} copy-done((bf16[8,128,512]{2,1,0:T(8,128)(2,1)S(1)}, bf16[8,128,512]{2,1,0:T(8,128)(2,1)}, u32[]{:S(2)}) %copy-start.4) | copy-done | bytes 1048600
  37.0 7.8 %prepare.1 = (bf16[8,512,768]{2,1,0:T(8,128)(2,1)S(1)}, f32[8,64,128]{2,1,0:T(8,128)S(1)}) custom-call(bf16[512,1024]{1,0:T(8,128)(2,1)S(1)} %copy-done.3, bf16[512,512]{1,0:T(8,128)(2,1)S(1)} %copy-done.8, bf16[8,128,512]{2,1,0:T(8,128)(2,1)S(1)} %copy-done.4, s32[8,64,1]{2,1,0:T(8,128)S(1)} %copy-done.5), custom_call_target="tpu_custom_call" | custom-call | flops 536870912 | bytes 10000000 | tf_op jit(solution)/shard_map/prepare/pallas_call | solution.py:52
  44.8 2.6 %copy-done = bf16[8,512,768]{2,1,0:T(8,128)(2,1)} copy-done((bf16[8,512,768]{2,1,0:T(8,128)(2,1)}, bf16[8,512,768]{2,1,0:T(8,128)(2,1)S(1)}, u32[]{:S(2)}) %copy-start) | copy-done | bytes 6291480
  49.9 1.2 %slice.40 = bf16[1,1]{1,0:T(2,128)(2,1)} slice(bf16[192,576]{1,0:T(8,128)(2,1)} %reshape.108), slice={[0:1], [0:1]} | slice | bytes 4 | tf_op jit(solution)/shard_map/slice | solution.py:454
  53.0 8.4 %all-to-all-done.1.got_ref = bf16[128,8,1152]{2,1,0:T(8,128)(2,1)S(1)} async-done(((bf16[128,8,1152]{2,1,0:T(8,128)(2,1)}), bf16[128,8,1152]{2,1,0:T(8,128)(2,1)S(1)}, u32[]{:S(2)}, u32[]{:S(2)}) %all-to-all-start.1) | async-done | bytes 2359328 | tf_op jit(solution)/shard_map/all_to_all | solution.py:451
  61.5 1.4 %compact.1 = bf16[64,8,1152]{2,1,0:T(8,128)(2,1)S(1)} custom-call(s32[128]{0:T(128)S(1)} %get-tuple-element.52.source_ref, s32[128]{0:T(128)S(1)} %convert_element_type.22.slot_ref, bf16[128,8,1152]{2,1,0:T(8,128)(2,1)S(1)} %all-to-all-done.1.got_ref, f32[1,1]{1,0:T(1,128)S(6)} %add.122.after_ref), custom_call_target="tpu_custom_call" | custom-call | bytes 4000000 | tf_op jit(solution)/shard_map/compact/pallas_call | solution.py:169
  62.9 1.2 %collective-permute-start.2 = (bf16[512,1152]{1,0:T(8,128)(2,1)S(1)}, bf16[512,1152]{1,0:T(8,128)(2,1)S(1)}, u32[]{:S(2)}, u32[]{:S(2)}) collective-permute-start(bf16[512,1152]{1,0:T(8,128)(2,1)S(1)} %bitcast.15), channel_id=1, source_target_pairs={{0,1},{1,0},{2,3},{3,2},{4,5},{5,4},{6,7},{7,6},{8,9},{9,8},{10,11... | collective-permute-start | bytes 3538952 | tf_op jit(solution)/shard_map/ppermute | solution.py:465
  64.2 2.7 %collective-permute-start.1 = (bf16[512,1152]{1,0:T(8,128)(2,1)S(1)}, bf16[512,1152]{1,0:T(8,128)(2,1)S(1)}, u32[]{:S(2)}, u32[]{:S(2)}) collective-permute-start(bf16[512,1152]{1,0:T(8,128)(2,1)S(1)} %bitcast.17), channel_id=1, source_target_pairs={{0,6},{1,7},{2,0},{3,1},{4,2},{5,3},{6,4},{7,5},{8,14},{9,15},{10,... | collective-permute-start | bytes 3538952 | tf_op jit(solution)/shard_map/ppermute | solution.py:465
  68.6 1.4 %collective-permute-done.3 = bf16[192,576]{1,0:T(8,128)(2,1)} collective-permute-done((bf16[192,576]{1,0:T(8,128)(2,1)}, bf16[192,576]{1,0:T(8,128)(2,1)}, u32[]{:S(2)}, u32[]{:S(2)}) %collective-permute-start.3) | collective-permute-done | bytes 221216 | tf_op jit(solution)/shard_map/ppermute | solution.py:465
  71.1 2.8 %copy-done.1 = bf16[8,512,768]{2,1,0:T(8,128)(2,1)S(1)} copy-done((bf16[8,512,768]{2,1,0:T(8,128)(2,1)S(1)}, bf16[8,512,768]{2,1,0:T(8,128)(2,1)}, u32[]{:S(2)}) %copy-start.1) | copy-done | bytes 6291480
  75.0 1.3 %copy-done.11 = bf16[512,1152]{1,0:T(8,128)(2,1)S(1)} copy-done((bf16[512,1152]{1,0:T(8,128)(2,1)S(1)}, bf16[512,1152]{1,0:T(8,128)(2,1)}, u32[]{:S(2)}) %copy-start.11) | copy-done | bytes 1179672
  77.2 12.6 %first.1 = (f32[8,512,128]{2,1,0:T(8,128)S(1)}, f32[8,512,128]{2,1,0:T(8,128)S(1)}, bf16[8,512,512]{2,1,0:T(8,128)(2,1)S(1)}) custom-call(s32[8]{0:T(128)S(1)} %copy-done.9, s32[8]{0:T(128)S(1)} %stack.44.shares_ref, bf16[8,512,768]{2,1,0:T(8,128)(2,1)S(1)} %copy-done.1, bf16[384,640]{1,0:T(8,128)(2,1)S(1)} %fusion.2.refs_0_, ...), custom_call_target="tpu_custom_call" | custom-call | flops 6845104128 | bytes 16777216 | tf_op jit(solution)/shard_map/first/pallas_call | solution.py:385
  89.7 3.1 %collective-permute-done.refs_3_ = bf16[512,1152]{1,0:T(8,128)(2,1)S(1)} collective-permute-done((bf16[512,1152]{1,0:T(8,128)(2,1)S(1)}, bf16[512,1152]{1,0:T(8,128)(2,1)S(1)}, u32[]{:S(2)}, u32[]{:S(2)}) %collective-permute-start) | collective-permute-done | bytes 1179680 | tf_op jit(solution)/shard_map/ppermute | solution.py:465
  94.0 2.7 %collective-permute-start.5 = (bf16[256,1152]{1,0:T(8,128)(2,1)S(1)}, bf16[256,1152]{1,0:T(8,128)(2,1)S(1)}, u32[]{:S(2)}, u32[]{:S(2)}) collective-permute-start(bf16[256,1152]{1,0:T(8,128)(2,1)S(1)} %slice.37), channel_id=1, source_target_pairs={{0,6},{1,7},{2,0},{3,1},{4,2},{5,3},{6,4},{7,5},{8,14},{9,15},{10,... | collective-permute-start | bytes 1769480 | tf_op jit(solution)/shard_map/ppermute | solution.py:465
  97.9 8.5 %second.1 = (f32[8,512,128]{2,1,0:T(8,128)S(1)}, f32[8,512,128]{2,1,0:T(8,128)S(1)}, bf16[8,512,512]{2,1,0:T(8,128)(2,1)S(1)}) custom-call(s32[8]{0:T(128)S(1)} %copy-done.9, s32[8]{0:T(128)S(1)} %stack.44.shares_ref, bf16[8,512,768]{2,1,0:T(8,128)(2,1)S(1)} %copy-done.1, ...), custom_call_target="tpu_custom_call", output_to_operand_aliasing={{0}: (3, {}), {1}: (4, {}), {2}: (5, {})} | custom-call | flops 4563402752 | bytes 16777216 | tf_op jit(solution)/shard_map/second/pallas_call | solution.py:385
  106.4 3.1 %collective-permute-done.4.refs_3_ = bf16[256,1152]{1,0:T(8,128)(2,1)S(1)} collective-permute-done((bf16[256,1152]{1,0:T(8,128)(2,1)S(1)}, bf16[256,1152]{1,0:T(8,128)(2,1)S(1)}, u32[]{:S(2)}, u32[]{:S(2)}) %collective-permute-start.4) | collective-permute-done | bytes 589856 | tf_op jit(solution)/shard_map/ppermute | solution.py:465
  109.5 1.4 %collective-permute-start.8 = (bf16[256,1152]{1,0:T(8,128)(2,1)S(1)}, bf16[256,1152]{1,0:T(8,128)(2,1)S(1)}, u32[]{:S(2)}, u32[]{:S(2)}) collective-permute-start(bf16[256,1152]{1,0:T(8,128)(2,1)S(1)} %collective-permute-done.4.refs_3_), channel_id=1, source_target_pairs={{0,1},{1,0},{2,3},{3,2},{4,5},{5,4},{6,7},{7,6},{8,9},{9,8},{10,11... | collective-permute-start | bytes 1769480 | tf_op jit(solution)/shard_map/ppermute | solution.py:465
  110.9 1.6 %collective-permute-done.8.refs_5_ = bf16[256,1152]{1,0:T(8,128)(2,1)S(1)} collective-permute-done((bf16[256,1152]{1,0:T(8,128)(2,1)S(1)}, bf16[256,1152]{1,0:T(8,128)(2,1)S(1)}, u32[]{:S(2)}, u32[]{:S(2)}) %collective-permute-start.8) | collective-permute-done | bytes 589856 | tf_op jit(solution)/shard_map/ppermute | solution.py:465
  113.4 7.7 %third.1 = bf16[512,1024]{1,0:T(8,128)(2,1)} custom-call(s32[8]{0:T(128)S(1)} %copy-done.9, s32[8]{0:T(128)S(1)} %stack.44.shares_ref, bf16[8,512,768]{2,1,0:T(8,128)(2,1)S(1)} %copy-done.1, f32[8,512,128]{2,1,0:T(8,128)S(1)} %get-tuple-element.44.refs_0_, f32[8,512,128]{2,1,0:T(8,128)S(1)} %get-tuple-element.45.refs_1_, ...), custom_call_target="tpu_custom_call" | custom-call | flops 2281701376 | bytes 16777216 | tf_op jit(solution)/shard_map/third/pallas_call | solution.py:385
  (71 shorter events, 16.4 us)
Async XLA Ops:
  0.0 1.9 %copy-start.18 = (s32[8,16]{1,0:T(8,128)S(1)}, s32[8,16]{1,0:T(8,128)}, u32[]{:S(2)}) copy-start(s32[8,16]{1,0:T(8,128)} %param.15) | copy-start | bytes 1540
  0.0 1.8 %copy-start.16 = (bf16[24,576]{1,0:T(8,128)(2,1)S(1)}, bf16[24,576]{1,0:T(8,128)(2,1)}, u32[]{:S(2)}) copy-start(bf16[24,576]{1,0:T(8,128)(2,1)} %param.17) | copy-start | bytes 82948
  17.2 2.3 %copy-start.14 = (bf16[16,64,128]{2,1,0:T(8,128)(2,1)}, bf16[16,64,128]{2,1,0:T(8,128)(2,1)S(1)}, u32[]{:S(2)}) copy-start(bf16[16,64,128]{2,1,0:T(8,128)(2,1)S(1)} %all_to_all.10) | copy-start | bytes 786436
  19.5 41.9 %all-to-all-start.1 = ((bf16[128,8,1152]{2,1,0:T(8,128)(2,1)}), bf16[128,8,1152]{2,1,0:T(8,128)(2,1)S(1)}, u32[]{:S(2)}, u32[]{:S(2)}) async-start(bf16[128,8,1152]{2,1,0:T(8,128)(2,1)} %bitcast.20), calls=%async_computation.1 | async-start | bytes 4718592 | tf_op jit(solution)/shard_map/all_to_all | solution.py:451
  28.1 4.8 %copy-start.17 = (s32[8,64]{1,0:T(8,128)S(1)}, s32[8,64]{1,0:T(8,128)}, u32[]{:S(2)}) copy-start(s32[8,64]{1,0:T(8,128)} %param.19) | copy-start | bytes 6148
  28.1 5.6 %copy-start.3 = (bf16[512,1024]{1,0:T(8,128)(2,1)S(1)}, bf16[512,1024]{1,0:T(8,128)(2,1)}, u32[]{:S(2)}) copy-start(bf16[512,1024]{1,0:T(8,128)(2,1)} %rows_ref.1) | copy-start | bytes 3145732
  33.8 1.2 %copy-start.4 = (bf16[8,128,512]{2,1,0:T(8,128)(2,1)S(1)}, bf16[8,128,512]{2,1,0:T(8,128)(2,1)}, u32[]{:S(2)}) copy-start(bf16[8,128,512]{2,1,0:T(8,128)(2,1)} %keys_ref.1) | copy-start | bytes 3145732
  37.0 11.9 %copy-start.15 = (bf16[16,64,128]{2,1,0:T(8,128)(2,1)S(1)}, bf16[16,64,128]{2,1,0:T(8,128)(2,1)}, u32[]{:S(2)}) copy-start(bf16[16,64,128]{2,1,0:T(8,128)(2,1)} %copy-done.14) | copy-start | bytes 786436
  44.8 2.6 %copy-start = (bf16[8,512,768]{2,1,0:T(8,128)(2,1)}, bf16[8,512,768]{2,1,0:T(8,128)(2,1)S(1)}, u32[]{:S(2)}) copy-start(bf16[8,512,768]{2,1,0:T(8,128)(2,1)S(1)} %get-tuple-element.27.q_ref) | copy-start | bytes 18874372
  53.0 18.0 %copy-start.9 = (s32[8]{0:T(128)S(1)}, s32[8]{0:T(128)}, u32[]{:S(2)}) copy-start(s32[8]{0:T(128)} %lengths_ref.5) | copy-start | bytes 100
  62.9 3.9 %collective-permute-start.2 = (bf16[512,1152]{1,0:T(8,128)(2,1)S(1)}, bf16[512,1152]{1,0:T(8,128)(2,1)S(1)}, u32[]{:S(2)}, u32[]{:S(2)}) collective-permute-start(bf16[512,1152]{1,0:T(8,128)(2,1)S(1)} %bitcast.15), channel_id=1, source_target_pairs={{0,1},{1,0},{2,3},{3,2},{4,5},{5,4},{6,7},{7,6},{8,9},{9,8},{10,11... | collective-permute-start | bytes 3538952 | tf_op jit(solution)/shard_map/ppermute | solution.py:465
  64.1 28.7 %collective-permute-start = (bf16[512,1152]{1,0:T(8,128)(2,1)S(1)}, bf16[512,1152]{1,0:T(8,128)(2,1)S(1)}, u32[]{:S(2)}, u32[]{:S(2)}) collective-permute-start(bf16[512,1152]{1,0:T(8,128)(2,1)S(1)} %bitcast.16), channel_id=1, source_target_pairs={{0,2},{1,3},{2,4},{3,5},{4,6},{5,7},{6,0},{7,1},{8,10},{9,11},{10,... | collective-permute-start | bytes 3538952 | tf_op jit(solution)/shard_map/ppermute | solution.py:465
  64.2 28.7 %collective-permute-start.1 = (bf16[512,1152]{1,0:T(8,128)(2,1)S(1)}, bf16[512,1152]{1,0:T(8,128)(2,1)S(1)}, u32[]{:S(2)}, u32[]{:S(2)}) collective-permute-start(bf16[512,1152]{1,0:T(8,128)(2,1)S(1)} %bitcast.17), channel_id=1, source_target_pairs={{0,6},{1,7},{2,0},{3,1},{4,2},{5,3},{6,4},{7,5},{8,14},{9,15},{10,... | collective-permute-start | bytes 3538952 | tf_op jit(solution)/shard_map/ppermute | solution.py:465
  67.8 2.1 %collective-permute-start.3 = (bf16[192,576]{1,0:T(8,128)(2,1)}, bf16[192,576]{1,0:T(8,128)(2,1)}, u32[]{:S(2)}, u32[]{:S(2)}) collective-permute-start(bf16[192,576]{1,0:T(8,128)(2,1)} %reshape.108), channel_id=1, source_target_pairs={{0,1},{1,0},{2,3},{3,2},{4,5},{5,4},{6,7},{7,6},{8,9},{9,8},{10,11... | collective-permute-start | bytes 663560 | tf_op jit(solution)/shard_map/ppermute | solution.py:465
  71.1 2.8 %copy-start.1 = (bf16[8,512,768]{2,1,0:T(8,128)(2,1)S(1)}, bf16[8,512,768]{2,1,0:T(8,128)(2,1)}, u32[]{:S(2)}) copy-start(bf16[8,512,768]{2,1,0:T(8,128)(2,1)} %copy-done) | copy-start | bytes 18874372
  73.9 1.1 copy-start.7
  75.0 1.3 %copy-start.11 = (bf16[512,1152]{1,0:T(8,128)(2,1)S(1)}, bf16[512,1152]{1,0:T(8,128)(2,1)}, u32[]{:S(2)}) copy-start(bf16[512,1152]{1,0:T(8,128)(2,1)} %copy-done.10) | copy-start | bytes 3538948
  92.9 3.8 %collective-permute-start.6 = (bf16[512,1152]{1,0:T(8,128)(2,1)S(1)}, bf16[512,1152]{1,0:T(8,128)(2,1)S(1)}, u32[]{:S(2)}, u32[]{:S(2)}) collective-permute-start(bf16[512,1152]{1,0:T(8,128)(2,1)S(1)} %collective-permute-done.refs_3_), channel_id=1, source_target_pairs={{0,1},{1,0},{2,3},{3,2},{4,5},{5,4},{6,7},{7,6},{8,9},{9,8},{10,11... | collective-permute-start | bytes 3538952 | tf_op jit(solution)/shard_map/ppermute | solution.py:465
  93.8 4.2 %collective-permute-start.7 = (bf16[512,1152]{1,0:T(8,128)(2,1)S(1)}, bf16[512,1152]{1,0:T(8,128)(2,1)S(1)}, u32[]{:S(2)}, u32[]{:S(2)}) collective-permute-start(bf16[512,1152]{1,0:T(8,128)(2,1)S(1)} %collective-permute-done.1.refs_4_), channel_id=1, source_target_pairs={{0,1},{1,0},{2,3},{3,2},{4,5},{5,4},{6,7},{7,6},{8,9},{9,8},{10,11... | collective-permute-start | bytes 3538952 | tf_op jit(solution)/shard_map/ppermute | solution.py:465
  93.9 19.5 %copy-start.2 = (bf16[8,512,128]{2,1,0:T(8,128)(2,1)S(1)}, bf16[8,512,128]{2,1,0:T(8,128)(2,1)}, u32[]{:S(2)}) copy-start(bf16[8,512,128]{2,1,0:T(8,128)(2,1)} %refs_7_.1) | copy-start | bytes 3145732
  93.9 15.7 %collective-permute-start.4 = (bf16[256,1152]{1,0:T(8,128)(2,1)S(1)}, bf16[256,1152]{1,0:T(8,128)(2,1)S(1)}, u32[]{:S(2)}, u32[]{:S(2)}) collective-permute-start(bf16[256,1152]{1,0:T(8,128)(2,1)S(1)} %slice.36), channel_id=1, source_target_pairs={{0,2},{1,3},{2,4},{3,5},{4,6},{5,7},{6,0},{7,1},{8,10},{9,11},{10,... | collective-permute-start | bytes 1769480 | tf_op jit(solution)/shard_map/ppermute | solution.py:465
  94.0 15.6 %collective-permute-start.5 = (bf16[256,1152]{1,0:T(8,128)(2,1)S(1)}, bf16[256,1152]{1,0:T(8,128)(2,1)S(1)}, u32[]{:S(2)}, u32[]{:S(2)}) collective-permute-start(bf16[256,1152]{1,0:T(8,128)(2,1)S(1)} %slice.37), channel_id=1, source_target_pairs={{0,6},{1,7},{2,0},{3,1},{4,2},{5,3},{6,4},{7,5},{8,14},{9,15},{10,... | collective-permute-start | bytes 1769480 | tf_op jit(solution)/shard_map/ppermute | solution.py:465
  109.5 3.0 %collective-permute-start.8 = (bf16[256,1152]{1,0:T(8,128)(2,1)S(1)}, bf16[256,1152]{1,0:T(8,128)(2,1)S(1)}, u32[]{:S(2)}, u32[]{:S(2)}) collective-permute-start(bf16[256,1152]{1,0:T(8,128)(2,1)S(1)} %collective-permute-done.4.refs_3_), channel_id=1, source_target_pairs={{0,1},{1,0},{2,3},{3,2},{4,5},{5,4},{6,7},{7,6},{8,9},{9,8},{10,11... | collective-permute-start | bytes 1769480 | tf_op jit(solution)/shard_map/ppermute | solution.py:465
  110.9 2.5 %collective-permute-start.9 = (bf16[256,1152]{1,0:T(8,128)(2,1)S(1)}, bf16[256,1152]{1,0:T(8,128)(2,1)S(1)}, u32[]{:S(2)}, u32[]{:S(2)}) collective-permute-start(bf16[256,1152]{1,0:T(8,128)(2,1)S(1)} %collective-permute-done.5.refs_4_), channel_id=1, source_target_pairs={{0,1},{1,0},{2,3},{3,2},{4,5},{5,4},{6,7},{7,6},{8,9},{9,8},{10,11... | collective-permute-start | bytes 1769480 | tf_op jit(solution)/shard_map/ppermute | solution.py:465
  (6 other events, 5.5 us)
